TPU v7x, 128 devices: a whole 4x4x4 slice. The times are simulated.
128 devices in a mesh: pair: 2 (over core), side: 2 (over y_lo), tp: 32 (over z, y_hi, x).
Axes of the slice: x: 4, y: 4 (y_hi: 2, y_lo: 2; y = y_hi * 2 + y_lo), z: 4, core: 2. Of those that a mesh axis runs over, the one named last changes fastest.
Arguments:
- tokens: bfloat16 [16, 256, 8192], P(('pair', 'side')), may hold values from -6 to 6
- norm_gain: float32 [8192], replicated, may hold values from 0.5 to 1.5
- w_qkv: bfloat16 [8192, 10240], P(('pair', 'side', 'tp')), may hold values from -0.25 to 0.25
- qkv_bias: bfloat16 [10240], replicated, may hold values from -8 to 8
- w_out: bfloat16 [8192, 8192], P(('pair', 'side'), 'tp'), may hold values from -0.125 to 0.125
Outputs:
- block_out: bfloat16 [16, 256, 8192], P(('pair', 'side'), None, 'tp')
All inputs are finite; a program needn't handle non-finite values.
Results may differ from a plain program's by a relative error of at most 0.023.
Values may be sent and summed in bfloat16 or wider, within the bound.
No kernel may reach another device: no remote copies, remote signals or barrier semaphores. Data moves between devices by JAX's collectives and lax.ppermute only.
A program may use at most 192 MiB of HBM per device.

v0:
```python
import jax
import jax.numpy as jnp
from jax import lax
from jax.sharding import PartitionSpec as P

HEADS = 64
KV_HEADS = 8
HD = 128


def rotate_pairs(values, positions):
    half_size = values.shape[-1] // 2
    inverse = 1000000.0 ** (-jnp.arange(half_size, dtype=jnp.float32) * 2.0 / values.shape[-1])
    angles = positions.astype(jnp.float32)[:, None] * inverse[None, :]
    cosine = jnp.cos(angles)[None, :, None, :]
    sine = jnp.sin(angles)[None, :, None, :]
    first_half = values[..., :half_size]
    second_half = values[..., half_size:]
    return jnp.concatenate(
        [first_half * cosine - second_half * sine, second_half * cosine + first_half * sine], -1
    )


def shards(tokens, norm_gain, w_qkv, qkv_bias, w_out):
    seq_count, span_len, width = tokens.shape
    tp_count = lax.axis_size("tp")
    tp_index = lax.axis_index("tp")
    heads_dev = HEADS // tp_count
    group_size = HEADS // KV_HEADS
    q_width = HEADS * HD
    kv_width = KV_HEADS * HD
    row_count = w_qkv.shape[0]
    tok_rows = seq_count * span_len
    inputs = tokens.astype(jnp.float32)
    mean_square = jnp.mean(inputs * inputs, axis=-1, keepdims=True)
    normed = (inputs * lax.rsqrt(mean_square + 1e-06) * norm_gain).astype(jnp.bfloat16)
    flat_rows = normed.reshape(tok_rows, width)
    query_part = w_qkv[:, :q_width].reshape(row_count, tp_count, heads_dev * HD)
    repeat_count = group_size // heads_dev
    key_part = jnp.repeat(
        w_qkv[:, q_width : q_width + kv_width].reshape(row_count, KV_HEADS, HD),
        repeat_count,
        axis=1,
    )
    value_part = jnp.repeat(
        w_qkv[:, q_width + kv_width :].reshape(row_count, KV_HEADS, HD), repeat_count, axis=1
    )
    bundle = jnp.concatenate([query_part, key_part, value_part], axis=2)
    col_count = bundle.shape[2]
    own_cols = lax.all_to_all(bundle, "tp", split_axis=1, concat_axis=0, tiled=True).reshape(
        row_count * tp_count, col_count
    )
    projected = jnp.dot(
        flat_rows,
        lax.all_gather(own_cols, ("pair", "side"), axis=0, tiled=True),
        preferred_element_type=jnp.float32,
    )
    kv_head = tp_index * heads_dev // group_size
    bias_query = lax.dynamic_slice_in_dim(qkv_bias, tp_index * heads_dev * HD, heads_dev * HD, 0)
    bias_key = lax.dynamic_slice_in_dim(qkv_bias, q_width + kv_head * HD, HD, 0)
    bias_value = lax.dynamic_slice_in_dim(qkv_bias, q_width + kv_width + kv_head * HD, HD, 0)
    projected = projected + jnp.concatenate([bias_query, bias_key, bias_value]).astype(jnp.float32)
    positions = jnp.arange(span_len)
    query = rotate_pairs(
        projected[:, : heads_dev * HD].reshape(seq_count, span_len, heads_dev, HD), positions
    ).astype(jnp.bfloat16)
    keys = rotate_pairs(
        projected[:, heads_dev * HD : heads_dev * HD + HD].reshape(seq_count, span_len, 1, HD),
        positions,
    ).astype(jnp.bfloat16)
    values_bf = (
        projected[:, heads_dev * HD + HD :].reshape(seq_count, span_len, HD).astype(jnp.bfloat16)
    )
    scores = jnp.einsum(
        "sqhd,skd->shqk", query, keys[:, :, 0, :], preferred_element_type=jnp.float32
    ) * HD ** (-0.5)
    causal = jnp.arange(span_len)[:, None] >= jnp.arange(span_len)[None, :]
    scores = jnp.where(causal[None, None], scores, -1e30)
    scores = scores - jnp.max(scores, axis=-1, keepdims=True)
    expo = jnp.exp(scores)
    weights = (expo / jnp.sum(expo, axis=-1, keepdims=True)).astype(jnp.bfloat16)
    attended = jnp.einsum(
        "shqk,skd->sqhd", weights, values_bf, preferred_element_type=jnp.float32
    ).astype(jnp.bfloat16)
    attended = attended.reshape(tok_rows, heads_dev * HD)
    share_width = width // tp_count
    w_cols = lax.all_gather(w_out, ("pair", "side"), axis=0, tiled=True)
    own_rows = lax.all_to_all(w_cols, "tp", split_axis=0, concat_axis=1, tiled=True)
    partial_sums = jnp.dot(attended, own_rows, preferred_element_type=jnp.float32)
    summed = lax.psum_scatter(
        partial_sums.astype(jnp.bfloat16), "tp", scatter_dimension=1, tiled=True
    ).astype(jnp.float32)
    residual_part = lax.dynamic_slice_in_dim(inputs, tp_index * share_width, share_width, 2)
    return (residual_part + summed.reshape(seq_count, span_len, share_width)).astype(jnp.bfloat16)


def solution(mesh):
    placed = (
        P(("pair", "side"), None, None),
        P(),
        P(("pair", "side", "tp"), None),
        P(),
        P(("pair", "side"), "tp"),
    )
    return jax.shard_map(
        shards,
        mesh=mesh,
        in_specs=placed,
        out_specs=P(("pair", "side"), None, "tp"),
        check_vma=False,
    )
```

profile of v0, /device:TPU:0, one launch (start us, length us, event | category | flops | bytes accessed | tf_op | source)
XLA Modules:
  0.0 576.3 jit_solution(13650091623182202493)
XLA Ops:
  6.5 0.0 slice-start
  6.5 0.0 all-gather.5.cloned.1.call-start
  6.5 0.7 all-gather.5.cloned.1.call-update
  7.3 0.0 all-gather.3.cloned.1.call-start
  7.3 1.0 slice_bitcast_fusion.1
  8.4 0.0 slice-done
  8.4 0.3 copy.38
  8.6 0.2 broadcast_in_dim.13
  8.8 0.2 broadcast_in_dim.12
  8.9 0.3 pad_maximum_fusion
  9.2 1.2 copy.24
  10.4 42.6 %all_to_all.34 = bf16[64,32,512]{2,0,1:T(8,128)(2,1)} all-to-all(bf16[64,32,512]{2,0,1:T(8,128)(2,1)S(1)} %copy.24), channel_id=1, replica_groups=mesh['pair'=2,'side'=2,'tp'=32] {'tp'}, dimensions={1} | all-to-all | bytes 4194304 | tf_op jit(solution)/shard_map/all_to_all | solution.py:50
  53.0 0.0 all-gather.3.cloned.1.call-update
  53.0 0.8 dynamic_slice.13
  53.8 0.8 fusion.29
  54.6 57.8 %all-gather.5.cloned.1.call-done = bf16[8192,256]{1,0:T(8,128)(2,1)} async-done(((bf16[2048,256]{1,0:T(8,128)(2,1)}), bf16[8192,256]{1,0:T(8,128)(2,1)}) %all-gather.5.cloned.1.call-update) | async-done | bytes 4194320 | tf_op jit(solution)/shard_map/all_gather | solution.py:87
  112.5 10.2 %all-to-all-start.1 = ((bf16[32,256,256]{2,1,0:T(8,128)(2,1)}), bf16[32,256,256]{2,1,0:T(8,128)(2,1)}, u32[]{:S(2)}, u32[]{:S(2)}) async-start(bf16[32,256,256]{2,1,0:T(8,128)(2,1)} %bitcast.66), calls=%async_computation.1 | async-start | bytes 8388608 | tf_op jit(solution)/shard_map/all_to_all | solution.py:88
  122.7 0.0 copy-start
  122.7 0.2 reduce-scatter.2.cloned.1.call-start
  123.0 8.4 %multiply_reduce_fusion = f32[4,256]{1,0:T(4,128)S(1)} fusion(bf16[4,256,8192]{2,1,0:T(8,128)(2,1)} %param.5), kind=kLoop, calls=%fused_computation.2 | loop fusion | flops 25164800 | bytes 16781312 | tf_op jit(solution)/shard_map/reduce_sum | solution.py:35
  131.4 0.5 multiply_cosine_fusion
  131.9 0.0 copy-done
  131.9 15.2 %multiply_convert_fusion = bf16[4,256,8192]{2,1,0:T(8,128)(2,1)} fusion(f32[8192]{0:T(1024)S(1)} %copy-done, f32[4,256]{1,0:T(4,128)S(1)} %add_rsqrt_fusion, bf16[4,256,8192]{2,1,0:T(8,128)(2,1)} %param.5), kind=kLoop, calls=%fused_computation.1 | loop fusion | flops 33554432 | bytes 33591296 | tf_op jit(solution)/shard_map/convert_element_type | solution.py:36
  147.1 35.9 %all-to-all-done.1 = bf16[32,256,256]{2,1,0:T(8,128)(2,1)} async-done(((bf16[32,256,256]{2,1,0:T(8,128)(2,1)}), bf16[32,256,256]{2,1,0:T(8,128)(2,1)}, u32[]{:S(2)}, u32[]{:S(2)}) %all-to-all-start.1) | async-done | bytes 4194336 | tf_op jit(solution)/shard_map/all_to_all | solution.py:88
  183.0 6.4 %copy.30 = bf16[256,32,256]{0,2,1:T(8,128)(2,1)} copy(bf16[256,32,256]{2,0,1:T(8,128)(2,1)} %bitcast.16) | data formatting | bytes 8388608 | tf_op jit(solution)/shard_map/all_to_all | solution.py:88
  189.4 114.8 %all-gather.3.cloned.1.call-done = bf16[8192,512]{1,0:T(8,128)(2,1)} async-done(((bf16[2048,512]{1,0:T(8,128)(2,1)}), bf16[8192,512]{1,0:T(8,128)(2,1)}) %all-gather.3.cloned.1.call-update) | async-done | bytes 8388624 | tf_op jit(solution)/shard_map/all_gather | solution.py:55
  304.2 14.3 %convolution_add_fusion = f32[1024,512]{1,0:T(8,128)S(1)} fusion(bf16[1024,8192]{1,0:T(8,128)(2,1)} %bitcast.62, bf16[8192,512]{1,0:T(8,128)(2,1)} %all-gather.3.cloned.1.call-done, f32[512]{0:T(512)S(1)} %maximum_convert_fusion), kind=kOutput, calls=%fused_computation.9 | convolution fusion | flops 8590458880 | bytes 27265024 | tf_op jit(solution)/shard_map/dot_general | solution.py:53
  318.5 0.1 slice.63
  318.6 0.1 slice.42
  318.7 0.1 slice.45
  318.8 0.5 reshape.152
  319.3 1.1 fusion.28
  320.5 0.3 fusion.13
  320.7 0.3 subtract_convert_fusion
  321.0 2.4 fusion.30
  323.5 1.9 fusion.2
  325.4 0.4 copy.29
  325.8 10.3 %convolution_convert_fusion = bf16[1024,8192]{1,0:T(8,128)(2,1)} fusion(bf16[256,8192]{0,1:T(8,128)(2,1)} %bitcast.63, bf16[128,8,2,128]{3,2,1,0:T(2,128)(2,1)S(1)} %bitcast.71), kind=kOutput, calls=%fused_computation.3 | convolution fusion | flops 4303355904 | bytes 21495808 | tf_op jit(solution)/shard_map/dot_general | solution.py:89
  336.1 0.0 reduce-scatter.2.cloned.1.call-update
  336.2 18.6 %convert_element_type.60 = f32[4,256,8192]{2,1,0:T(8,128)} convert(bf16[4,256,8192]{2,1,0:T(8,128)(2,1)} %param.5) | non-fusion elementwise | flops 8388608 | bytes 50331648 | tf_op jit(solution)/shard_map/convert_element_type | solution.py:34
  354.7 212.7 %reduce-scatter.2.cloned.1.call-done = bf16[1024,256]{1,0:T(8,128)(2,1)} async-done(((bf16[1024,8192]{1,0:T(8,128)(2,1)}), bf16[1024,256]{1,0:T(8,128)(2,1)}) %reduce-scatter.2.cloned.1.call-update) | async-done | bytes 524304 | tf_op jit(solution)/shard_map/reduce_scatter | solution.py:90
  567.5 2.3 fusion.3
  (7 shorter events, 0.1 us)
Async XLA Ops:
  6.5 1.8 slice-start
  6.5 105.9 %all-gather.5.cloned.1.call-start = ((), (), s32[]{:S(2)}) async-start(), calls=%async_computation.4 | async-start | bytes 5242880 | tf_op jit(solution)/shard_map/all_gather | solution.py:87
  7.3 296.9 %all-gather.3.cloned.1.call-start = ((), (), s32[]{:S(2)}) async-start(), calls=%async_computation.3 | async-start | bytes 10485760 | tf_op jit(solution)/shard_map/all_gather | solution.py:55
  112.5 70.5 %all-to-all-start.1 = ((bf16[32,256,256]{2,1,0:T(8,128)(2,1)}), bf16[32,256,256]{2,1,0:T(8,128)(2,1)}, u32[]{:S(2)}, u32[]{:S(2)}) async-start(bf16[32,256,256]{2,1,0:T(8,128)(2,1)} %bitcast.66), calls=%async_computation.1 | async-start | bytes 8388608 | tf_op jit(solution)/shard_map/all_to_all | solution.py:88
  122.7 9.2 %copy-start = (f32[8192]{0:T(1024)S(1)}, f32[8192]{0:T(1024)}, u32[]{:S(2)}) copy-start(f32[8192]{0:T(1024)} %param.6) | copy-start | bytes 98308
  122.7 444.7 %reduce-scatter.2.cloned.1.call-start = ((), (), s32[]{:S(2)}) async-start(), calls=%async_computation.5 | async-start | bytes 17301504 | tf_op jit(solution)/shard_map/reduce_scatter | solution.py:90
Sparse Core Ops, SparseCore 0:
  9.0 103.4 all-gather.4
  114.1 189.9 all-gather.2
  336.3 231.1 reduce-scatter.1
where the time goes:
time: 577 us; the launch traced here: 576 us
  waiting for transfers between devices  422 us (73%)
  other arithmetic  45.9 us (8%)
  blocking collectives  42.6 us (7%)
  matrix products  29 us (5%)
  between operations  13.3 us (2%)
  local copies, waits for them, and re-layouts  13.1 us (2%)
  starting transfers between devices  10.5 us (2%)
    reduce_scatter x1, waiting for transfers between devices, shards(): lax.psum_scatter(partial_sums.astype(jnp.bfloat16), 'tp', scatter_dimensi...  213 us
    all_gather x1, waiting for transfers between devices, shards(): lax.all_gather(own_cols, ('pair', 'side'), axis=0, tiled=True)  115 us
    all_gather x1, waiting for transfers between devices, shards(): w_cols = lax.all_gather(w_out, ('pair', 'side'), axis=0, tiled=True)  57.8 us
    all_to_all x1, blocking collectives, shards(): lax.all_to_all(bundle, 'tp', split_axis=1, concat_axis=0, tiled=True)  42.6 us
    all_to_all x1, waiting for transfers between devices, shards(): lax.all_to_all(w_cols, 'tp', split_axis=0, concat_axis=1, tiled=True)  35.9 us
    convert_element_type x1, other arithmetic, shards(): inputs = tokens.astype(jnp.float32)  18.6 us
    convert_element_type x1, other arithmetic, shards(): (inputs * lax.rsqrt(mean_square + 1e-06) * norm_gain).astype(jnp.bfloat16)  15.2 us
    dot_general x1, matrix products, shards(): jnp.dot(flat_rows, lax.all_gather(own_cols, ('pair', 'side'), axis=0, til...  14.3 us
  transfers between devices with their start and end apart: 4, of which 4 were waited for; matrix products, arithmetic and copies ran while one was open for 9% of the time, Pallas kernels for 0%

commit v1 on v0

v1 whole, which is shorter than its diff:
```python
import functools

import jax
import jax.numpy as jnp
import numpy as np
from jax import lax
from jax.experimental import pallas as pl
from jax.experimental.pallas import tpu as pltpu
from jax.sharding import PartitionSpec as P

HD = 128
SPAN = 256
D = 8192
BF = jnp.bfloat16
F32 = jnp.float32
VMEM_LIMIT = 56 * 1024 * 1024


def rope_tables():
    half = HD // 2
    inverse = 1000000.0 ** (-np.arange(half, dtype=np.float64) * 2.0 / HD)
    angles = (
        np.arange(SPAN, dtype=np.float32)[:, None] * inverse.astype(np.float32)[None, :]
    )
    angles = angles.astype(np.float64)
    return np.cos(angles).astype(np.float32), np.sin(angles).astype(np.float32)


def kv_lanes(part):
    low = list(range(16 * part, 16 * part + 16))
    return low + [64 + i for i in low] + list(range(128 + 32 * part, 160 + 32 * part))


def tables():
    cosine, sine = rope_tables()
    pack = np.zeros((2, 256, 512), np.float32)
    gather = np.zeros((4, 2, 128, 256), np.float32)
    bias_sel = np.zeros((4, 256, 128), np.float32)
    k_cos = np.ones((4, SPAN, 128), np.float32)
    k_sin = np.zeros((4, SPAN, 128), np.float32)
    turn = np.zeros((64, 64), np.float32)
    for lane in range(16):
        turn[lane + 16, lane] = 1.0
        turn[lane, lane + 16] = 1.0
    for part in range(4):
        lanes = kv_lanes(part)
        for lane, column in enumerate(lanes):
            pack[0, column, part * 128 + lane] = 1.0
            pack[1, column, part * 128 + 64 + lane] = 1.0
            gather[part, 0, lane, column] = 1.0
            gather[part, 1, 64 + lane, column] = 1.0
            bias_sel[part, column, lane] = 1.0
        bias_sel[part, :, 64:] = bias_sel[part, :, :64] @ turn
        dims = slice(16 * part, 16 * part + 16)
        for base in (0, 64):
            k_cos[part, :, base : base + 16] = cosine[:, dims]
            k_cos[part, :, base + 16 : base + 32] = cosine[:, dims]
            k_sin[part, :, base : base + 16] = -sine[:, dims]
            k_sin[part, :, base + 16 : base + 32] = sine[:, dims]
    unpack = np.zeros((128, 256), np.float32)
    unpack[:64, :64] = np.eye(64)
    unpack[:64, 64:128] = turn
    unpack[64:, 128:192] = np.eye(64)
    unpack[64:, 192:] = turn
    q_cos = np.concatenate([cosine, cosine], 1)
    q_sin = np.concatenate([-sine, sine], 1)
    return {
        "pack": jnp.asarray(pack, BF),
        "gather": jnp.asarray(gather, BF),
        "bias_sel": jnp.asarray(bias_sel, BF),
        "unpack": jnp.asarray(unpack, BF),
        "k_cos": jnp.asarray(k_cos),
        "k_sin": jnp.asarray(k_sin),
        "q_cos": jnp.asarray(q_cos),
        "q_sin": jnp.asarray(q_sin),
    }


def dot(a, b):
    return jnp.dot(a, b, preferred_element_type=F32)


def params(**kw):
    return pltpu.CompilerParams(vmem_limit_bytes=VMEM_LIMIT, **kw)


def full(shape):
    return pl.BlockSpec(shape, lambda *_: (0,) * len(shape))


def pack_body(wq, wk, wv, gain, sel, kv, q0, q1):
    scale = gain[...]
    for i in range(4):
        for h, out in enumerate((q0, q1)):
            lanes = slice((2 * i + h) * 128, (2 * i + h + 1) * 128)
            out[i] = (wq[:, lanes].astype(F32) * scale).astype(BF)
    both = jnp.concatenate([wk[...], wv[...]], 1).astype(F32) * scale
    both = both.astype(BF)
    packed = dot(both[:32], sel[0]) + dot(both[32:], sel[1])
    for i in range(4):
        kv[i] = packed[:, i * 128 : (i + 1) * 128].astype(BF)


def pack(w_qkv, gain, sel):
    return pl.pallas_call(
        pack_body,
        grid=(8,),
        in_specs=[
            pl.BlockSpec((64, 1024), lambda g: (0, g)),
            pl.BlockSpec((64, 128), lambda g: (0, 64 + g)),
            pl.BlockSpec((64, 128), lambda g: (0, 72 + g)),
            full((64, 1)),
            full((2, 256, 512)),
        ],
        out_specs=[
            pl.BlockSpec((4, 32, 128), lambda g: (g, 0, 0)),
            pl.BlockSpec((4, 64, 128), lambda g: (g, 0, 0)),
            pl.BlockSpec((4, 64, 128), lambda g: (g, 0, 0)),
        ],
        out_shape=[
            jax.ShapeDtypeStruct((32, 32, 128), BF),
            jax.ShapeDtypeStruct((32, 64, 128), BF),
            jax.ShapeDtypeStruct((32, 64, 128), BF),
        ],
        compiler_params=params(),
        name="pack_weights",
        cost_estimate=pl.CostEstimate(flops=1 << 26, bytes_accessed=3 << 20, transcendentals=0),
    )(w_qkv, w_qkv, w_qkv, gain, sel)


def kv_body(idx, xa, xb, w0, w1, w2, w3, unpack, bk, bv, bsel, cos, sin, kv, norm_a, norm_b, ws):
    @pl.when(pl.program_id(0) == 0)
    def _():
        for j, w in enumerate((w0, w1, w2, w3)):
            both = dot(w[...], unpack[...]).astype(BF)
            ws[j, :, :32, :] = both[:, :128].reshape(32, 32, 128)
            ws[j, :, 32:, :] = both[:, 128:].reshape(32, 32, 128)

    bias = jnp.concatenate([bk[0], bv[0]], 1)
    bias = dot(jnp.broadcast_to(bias, (16, 256)), bsel[0])[0:1]
    lane = lax.broadcasted_iota(jnp.int32, (128, 128), 1)
    cosine = cos[0]
    sine = sin[0]
    parts = []
    for x, norm in ((xa, norm_a), (xb, norm_b)):
        square = jnp.zeros((128, 128), F32)
        for c in range(64):
            piece = x[:, c * 128 : (c + 1) * 128].astype(F32)
            square += piece * piece
        mean = jnp.sum(square, axis=1, keepdims=True) * (1.0 / D)
        inv = lax.rsqrt(mean + 1e-6)
        norm[...] = jnp.broadcast_to(inv, (128, 128))
        acc = jnp.zeros((128, 128), F32)
        for j in range(4):
            start = pl.multiple_of(idx[j] * 2048, 2048)
            acc += dot(x[:, pl.ds(start, 2048)], ws[j].reshape(2048, 128))
        parts.append(acc * inv + bias)
    a, b = parts
    left = a * cosine + pltpu.roll(a, 64, 1) * sine
    right = pltpu.roll(b, 64, 1) * cosine + b * sine
    kv[...] = jnp.where(lane < 64, left, right).astype(BF)


def keys_values(idx, x, ws, tab, bias):
    return pl.pallas_call(
        kv_body,
        grid_spec=pltpu.PrefetchScalarGridSpec(
            num_scalar_prefetch=1,
            grid=(4,),
            in_specs=[
                pl.BlockSpec((128, D), lambda i, idx: (i, 0)),
                pl.BlockSpec((128, D), lambda i, idx: (i + 4, 0)),
                *[full((1024, 128))] * 4,
                full((128, 256)),
                pl.BlockSpec((1, 1, 128), lambda i, idx: (64 + idx[5], 0, 0)),
                pl.BlockSpec((1, 1, 128), lambda i, idx: (72 + idx[5], 0, 0)),
                pl.BlockSpec((1, 256, 128), lambda i, idx: (idx[6], 0, 0)),
                pl.BlockSpec((1, 128, 128), lambda i, idx: (idx[6], i % 2, 0)),
                pl.BlockSpec((1, 128, 128), lambda i, idx: (idx[6], i % 2, 0)),
            ],
            out_specs=[
                pl.BlockSpec((128, 128), lambda i, idx: (i, 0)),
                pl.BlockSpec((128, 128), lambda i, idx: (i, 0)),
                pl.BlockSpec((128, 128), lambda i, idx: (i, 0)),
            ],
            scratch_shapes=[pltpu.VMEM((4, 32, 64, 128), BF)],
        ),
        out_shape=[
            jax.ShapeDtypeStruct((512, 128), BF),
            jax.ShapeDtypeStruct((512, 128), F32),
            jax.ShapeDtypeStruct((512, 128), F32),
        ],
        compiler_params=params(),
        name="keys_values",
        cost_estimate=pl.CostEstimate(
            flops=2 * 1024 * 8192 * 256, bytes_accessed=18 << 20, transcendentals=0
        ),
    )(idx, x, x, *ws, tab["unpack"], bias, bias, tab["bias_sel"], tab["k_cos"], tab["k_sin"])


def head_body(
    idx, x, w0, w1, w2, w3, na, nb, bq, cos, sin, p0, p1, p2, p3, g0, g1, g2, g3, att
):
    seq = pl.program_id(0)
    acc = jnp.zeros((SPAN, HD), F32)
    for j, w in enumerate((w0, w1, w2, w3)):
        start = pl.multiple_of(idx[j] * 2048, 2048)
        acc += dot(x[:, pl.ds(start, 2048)], w[...])
    norm = jnp.where(seq < 2, na[...], nb[...])
    query = acc * norm + bq[0].astype(F32)
    query = (query * cos[...] + pltpu.roll(query, 64, 1) * sin[...]).astype(BF)
    kv = jnp.zeros((SPAN, 256), F32)
    for piece, place in ((p0, g0), (p1, g1), (p2, g2), (p3, g3)):
        kv += dot(piece[...], place[0, 0])
    keys = kv[:, :128].astype(BF)
    values = kv[:, 128:].astype(BF)
    scores = lax.dot_general(
        query, keys, (((1,), (1,)), ((), ())), preferred_element_type=F32
    ) * (HD**-0.5)
    row = lax.broadcasted_iota(jnp.int32, (SPAN, SPAN), 0)
    col = lax.broadcasted_iota(jnp.int32, (SPAN, SPAN), 1)
    scores = jnp.where(row >= col, scores, -1e30)
    scores = jnp.exp(scores - jnp.max(scores, axis=1, keepdims=True))
    weights = (scores / jnp.sum(scores, axis=1, keepdims=True)).astype(BF)
    att[...] = dot(weights, values).astype(BF)


def head(h, idx, x, ws, norms, tab, bias, pieces):
    def place(r):
        return pl.BlockSpec((1, 1, 128, 256), lambda i, idx: ((idx[6] + 4 - r) % 4, i // 2, 0, 0))

    return pl.pallas_call(
        head_body,
        grid_spec=pltpu.PrefetchScalarGridSpec(
            num_scalar_prefetch=1,
            grid=(4,),
            in_specs=[
                pl.BlockSpec((SPAN, D), lambda i, idx: (i, 0)),
                *[full((2048, 128))] * 4,
                pl.BlockSpec((SPAN, 128), lambda i, idx: (i % 2, 0)),
                pl.BlockSpec((SPAN, 128), lambda i, idx: (i % 2, 0)),
                pl.BlockSpec((1, 1, 128), lambda i, idx: (2 * idx[4] + h, 0, 0)),
                full((SPAN, 128)),
                full((SPAN, 128)),
                *[pl.BlockSpec((SPAN, 128), lambda i, idx: (i % 2, 0))] * 4,
                *[place(r) for r in range(4)],
            ],
            out_specs=pl.BlockSpec((SPAN, 128), lambda i, idx: (i, 0)),
        ),
        out_shape=jax.ShapeDtypeStruct((1024, 128), BF),
        compiler_params=params(),
        name=f"query_head_{h}",
        cost_estimate=pl.CostEstimate(
            flops=2 * 1024 * 8192 * 256, bytes_accessed=20 << 20, transcendentals=1 << 18
        ),
    )(
        idx,
        x,
        *ws,
        *norms,
        bias,
        tab["q_cos"],
        tab["q_sin"],
        *pieces,
        *[tab["gather"]] * 4,
    )


def route_body(pos, k0, r0, k1, r1, o0, o1, o2, o3, sem):
    for r, out in enumerate((o0, o1, o2, o3)):
        goal = (pos[2] + r) % 4
        same_p = goal // 2 == pos[0]
        same_s = goal % 2 == pos[1]
        for src, cond in (
            (k0, same_p & same_s),
            (r0, jnp.logical_not(same_p) & same_s),
            (k1, same_p & jnp.logical_not(same_s)),
            (r1, jnp.logical_not(same_p) & jnp.logical_not(same_s)),
        ):

            @pl.when(cond)
            def _():
                pltpu.make_async_copy(src, out, sem.at[r]).start()

    for r, out in enumerate((o0, o1, o2, o3)):
        pltpu.make_async_copy(k0, out, sem.at[r]).wait()


def route(pos, blocks):
    any_spec = pl.BlockSpec(memory_space=pl.ANY)
    return pl.pallas_call(
        route_body,
        grid_spec=pltpu.PrefetchScalarGridSpec(
            num_scalar_prefetch=1,
            grid=(),
            in_specs=[any_spec] * 4,
            out_specs=[any_spec] * 4,
            scratch_shapes=[pltpu.SemaphoreType.DMA((4,))],
        ),
        out_shape=[jax.ShapeDtypeStruct((1024, 256), BF)] * 4,
        compiler_params=params(),
        name="route_rows",
        cost_estimate=pl.CostEstimate(flops=0, bytes_accessed=4 << 20, transcendentals=0),
    )(pos, *blocks)


def out_body(idx, *refs):
    atts = refs[:8]
    own = refs[8:12]
    other = refs[12:16]
    out = refs[16]
    wv, sem = refs[17:]
    p = idx[7]

    @pl.when(pl.program_id(0) == 0)
    def _():
        copies = []
        for r in range(4):
            copies.append(
                pltpu.make_async_copy(own[r], wv.at[r, :, :, p], sem.at[r])
            )
            copies.append(
                pltpu.make_async_copy(other[r], wv.at[r, :, :, 1 - p], sem.at[4 + r])
            )
        for copy in copies:
            copy.start()
        for copy in copies:
            copy.wait()

    for r in range(4):
        acc = jnp.zeros((256, 256), F32)
        for xr in range(4):
            part = (idx[6] + 4 - xr) % 4
            for h in range(2):
                acc += dot(atts[h * 4 + xr][...], wv[r, part, h].reshape(256, 256))
        out[r] = acc.astype(BF)


def project_out(idx, atts, own, other):
    any_spec = pl.BlockSpec(memory_space=pl.ANY)
    return pl.pallas_call(
        out_body,
        grid_spec=pltpu.PrefetchScalarGridSpec(
            num_scalar_prefetch=1,
            grid=(4,),
            in_specs=[
                *[pl.BlockSpec((256, 256), lambda i, idx: (i, 0))] * 8,
                *[any_spec] * 8,
            ],
            out_specs=pl.BlockSpec((4, 256, 256), lambda i, idx: (0, i, 0)),
            scratch_shapes=[
                pltpu.VMEM((4, 4, 2, 2, 128, 256), BF),
                pltpu.SemaphoreType.DMA((8,)),
            ],
        ),
        out_shape=jax.ShapeDtypeStruct((4, 1024, 256), BF),
        compiler_params=params(),
        name="project_out",
        cost_estimate=pl.CostEstimate(
            flops=2 * 1024 * 2048 * 1024, bytes_accessed=10 << 20, transcendentals=0
        ),
    )(
        idx,
        *atts,
        *[w.reshape(4, 2, 128, 256) for w in own],
        *[w.reshape(4, 2, 128, 256) for w in other],
    )


SWAP = [(0, 1), (1, 0)]


def shift(dz, dy, dx):
    return [
        (
            z * 8 + y * 4 + x,
            (z + dz) % 4 * 8 + (y + dy) % 2 * 4 + (x + dx) % 4,
        )
        for z in range(4)
        for y in range(2)
        for x in range(4)
    ]


def shards(tokens, norm_gain, w_qkv, qkv_bias, w_out):
    tab = tables()
    seqs, span, width = tokens.shape
    p = lax.axis_index("pair")
    s = lax.axis_index("side")
    t = lax.axis_index("tp")
    z, yh, xi = t // 8, t // 4 % 2, t % 4
    idx = jnp.stack(
        [2 * p + s, 2 * (1 - p) + s, 2 * p + 1 - s, 2 * (1 - p) + 1 - s, t, t // 4, xi, p]
    ).astype(jnp.int32)
    pos = jnp.stack([p, s, z]).astype(jnp.int32)
    x = tokens.reshape(seqs * span, width)
    bias = qkv_bias.reshape(80, 1, 128)

    gain = lax.dynamic_slice_in_dim(norm_gain, (2 * p + s) * 2048 + t * 64, 64, 0)
    kv_w, q0_w, q1_w = pack(w_qkv, gain.reshape(64, 1), tab["pack"])

    def spread(w):
        rows = w.shape[0] * w.shape[1]
        own = lax.all_to_all(w, "tp", split_axis=0, concat_axis=0, tiled=True)
        own = own.reshape(rows, 128)
        side = lax.ppermute(own, "side", SWAP)
        mate = lax.ppermute(own, "pair", SWAP)
        far = lax.ppermute(side, "pair", SWAP)
        return own, mate, side, far

    kv_ws = spread(kv_w)
    q_ws = [spread(q0_w), spread(q1_w)]

    halves = w_out.reshape(2, 1024, 256)
    keep = lax.dynamic_index_in_dim(halves, p, 0, keepdims=False)
    send = lax.dynamic_index_in_dim(halves, 1 - p, 0, keepdims=False)
    recv = lax.ppermute(send, "pair", SWAP)
    keep_s = lax.ppermute(keep, "side", SWAP)
    recv_s = lax.ppermute(recv, "side", SWAP)
    routed = route(pos, (keep, recv, keep_s, recv_s))
    w_own = [routed[0]] + [
        lax.ppermute(routed[r], "tp", shift(r, 0, 0)) for r in range(1, 4)
    ]
    w_other = [lax.ppermute(w, "pair", SWAP) for w in w_own]

    kv_piece, norm_a, norm_b = keys_values(idx, x, kv_ws, tab, bias)
    pieces = [kv_piece] + [
        lax.ppermute(kv_piece, "tp", shift(0, 0, r)) for r in range(1, 4)
    ]

    atts = []
    for h in range(2):
        att = head(h, idx, x, q_ws[h], (norm_a, norm_b), tab, bias, pieces)
        across = lax.ppermute(att, "tp", shift(0, 1, 0))
        first = jnp.where(yh == 0, att, across)
        second = jnp.where(yh == 0, across, att)
        both = jnp.concatenate([first, second], 1)
        atts += [both] + [
            lax.ppermute(both, "tp", shift(0, 0, r)) for r in range(1, 4)
        ]

    partial = project_out(idx, atts, w_own, w_other)
    total = partial[0].astype(F32)
    for r in range(1, 4):
        total += lax.ppermute(partial[r], "tp", shift(-r, 0, 0)).astype(F32)
    residual = lax.dynamic_slice_in_dim(tokens, t * 256, 256, 2).astype(F32)
    return (residual + total.reshape(seqs, span, 256)).astype(BF)


def solution(mesh):
    placed = (
        P(("pair", "side"), None, None),
        P(),
        P(("pair", "side", "tp"), None),
        P(),
        P(("pair", "side"), "tp"),
    )
    return jax.shard_map(
        shards,
        mesh=mesh,
        in_specs=placed,
        out_specs=P(("pair", "side"), None, "tp"),
        check_vma=False,
    )
```

time: 577 us -> 302 us (0.52)
  waiting for transfers between devices: 422 us -> 105 us
  Pallas kernels: 0 us -> 122 us
  other arithmetic: 45.9 us -> 4.11 us
  starting transfers between devices: 10.5 us -> 41.6 us
  matrix products: 29 us -> 0 us
  blocking collectives: 42.6 us -> 21.6 us
  between operations: 13.3 us -> 0.44 us
  local copies, waits for them, and re-layouts: 13.1 us -> 6.84 us
    reduce_scatter x1 -> x0, waiting for transfers between devices: 213 us -> none  [shards(): lax.psum_scatter(partial_sums.astype(jnp.bfloat16), 'tp', scatter_dimensi...]
    all_gather x2 -> x0, waiting for transfers between devices: 173 us -> none  [the longest x1 115 us: shards(): lax.all_gather(own_cols, ('pair', 'side'), axis=0, tiled=True)]
    pallas_call x0 -> x6, Pallas kernels: none -> 122 us  [the longest x1 65.3 us: route(): pl.pallas_call(route_body, grid_spec=pltpu.PrefetchScalarGridSpec(num_sca...]
    ppermute x0 -> x33, waiting for transfers between devices: none -> 81.2 us  [the longest x6 40.5 us: shards(): lax.ppermute(both, 'tp', shift(0, 0, r))]
    convert_element_type x5 -> x1, other arithmetic: 36.1 us -> 1.96 us  [shards(): return (residual + total.reshape(seqs, span, 256)).astype(BF)]
    ppermute x0 -> x33, starting transfers between devices: none -> 32.6 us  [the longest x6 9.35 us: shards(): lax.ppermute(both, 'tp', shift(0, 0, r))]
    dot_general x3 -> x0, matrix products: 26.6 us -> none  [the longest x1 14.3 us: shards(): jnp.dot(flat_rows, lax.all_gather(own_cols, ('pair', 'side'), axis=0, til...]
    all_to_all x1, blocking collectives: 42.6 us -> 21.6 us  [spread(): own = lax.all_to_all(w, 'tp', split_axis=0, concat_axis=0, tiled=True)]
  transfers between devices with their start and end apart: 4 -> 35, of which waited for: 4 -> 12; matrix products, arithmetic and copies ran while one was open for 9% -> 1% of each run, Pallas kernels for 0% -> 35%
where the time goes in v1:
time: 302 us
  Pallas kernels  122 us (40%)
  waiting for transfers between devices  105 us (35%)
  starting transfers between devices  41.6 us (14%)
  blocking collectives  21.6 us (7%)
  local copies, waits for them, and re-layouts  6.84 us (2%)
  other arithmetic  4.11 us (1%)
    pallas_call x1, Pallas kernels, route(): pl.pallas_call(route_body, grid_spec=pltpu.PrefetchScalarGridSpec(num_sca...  65.3 us
    ppermute x6, waiting for transfers between devices, shards(): lax.ppermute(both, 'tp', shift(0, 0, r))  40.5 us
    pallas_call x2, Pallas kernels, head(): pl.pallas_call(head_body, grid_spec=pltpu.PrefetchScalarGridSpec(num_scal...  26.2 us
    all_to_all x2, waiting for transfers between devices, spread(): own = lax.all_to_all(w, 'tp', split_axis=0, concat_axis=0, tiled=True)  23.8 us
    ppermute x3, waiting for transfers between devices, shards(): total += lax.ppermute(partial[r], 'tp', shift(-r, 0, 0)).astype(F32)  23.6 us
    all_to_all x1, blocking collectives, spread(): own = lax.all_to_all(w, 'tp', split_axis=0, concat_axis=0, tiled=True)  21.6 us
    pallas_call x1, Pallas kernels, keys_values(): pl.pallas_call(kv_body, grid_spec=pltpu.PrefetchScalarGridSpec(num_scalar...  13.7 us
    pallas_call x1, Pallas kernels, project_out(): pl.pallas_call(out_body, grid_spec=pltpu.PrefetchScalarGridSpec(num_scala...  10.4 us
  transfers between devices with their start and end apart: 35, of which 12 were waited for; matrix products, arithmetic and copies ran while one was open for 1% of the time, Pallas kernels for 35%

profile of v1, /device:TPU:0, one launch (start us, length us, event | category | flops | bytes accessed | tf_op | source)
XLA Modules:
  0.0 301.5 jit_solution(6734110815698526973)
XLA Ops:
  0.0 0.8 copy-done
  0.8 0.1 dynamic-slice_bitcast_fusion.2
  0.8 0.7 copy.15.gain
  1.6 6.4 %pack_weights.1 = (bf16[32,32,128]{2,1,0:T(8,128)(2,1)}, bf16[32,64,128]{2,1,0:T(8,128)(2,1)}, bf16[32,64,128]{2,1,0:T(8,128)(2,1)}) custom-call(bf16[64,10240]{1,0:T(8,128)(2,1)} %wv.1, bf16[64,10240]{1,0:T(8,128)(2,1)} %wv.1, bf16[64,10240]{1,0:T(8,128)(2,1)} %wv.1, f32[64,1]{1,0:T(8,128)} %copy.15.gain, bf16[2,256,512]{2,1,0:T(8,128)(2,1)} %constant.92.clone.sel), custom_call_target="tpu_custom_call" | custom-call | flops 67108864 | bytes 3145728 | tf_op jit(solution)/shard_map/pack_weights/pallas_call | solution.py:105
  7.9 21.6 %all_to_all.15 = bf16[32,32,128]{2,1,0:T(8,128)(2,1)S(1)} all-to-all(bf16[32,32,128]{2,1,0:T(8,128)(2,1)} %get-tuple-element.16), channel_id=1, replica_groups=mesh['pair'=2,'side'=2,'tp'=32] {'tp'}, dimensions={0} | all-to-all | bytes 524288 | tf_op jit(solution)/shard_map/all_to_all | solution.py:404
  29.5 4.0 %all-to-all-start.2 = ((bf16[32,64,128]{2,1,0:T(8,128)(2,1)}), bf16[32,64,128]{2,1,0:T(8,128)(2,1)S(1)}, u32[]{:S(2)}, u32[]{:S(2)}) async-start(bf16[32,64,128]{2,1,0:T(8,128)(2,1)} %get-tuple-element.20), calls=%async_computation.2 | async-start | bytes 1048576 | tf_op jit(solution)/shard_map/all_to_all | solution.py:404
  33.6 0.9 dynamic-slice_bitcast_fusion
  34.5 0.7 collective-permute-start.4
  35.2 10.4 %all-to-all-done.2 = bf16[32,64,128]{2,1,0:T(8,128)(2,1)S(1)} async-done(((bf16[32,64,128]{2,1,0:T(8,128)(2,1)}), bf16[32,64,128]{2,1,0:T(8,128)(2,1)S(1)}, u32[]{:S(2)}, u32[]{:S(2)}) %all-to-all-start.2) | async-done | bytes 524320 | tf_op jit(solution)/shard_map/all_to_all | solution.py:404
  45.6 0.7 collective-permute-start.14
  46.2 5.0 %all-to-all-start = ((bf16[32,64,128]{2,1,0:T(8,128)(2,1)}), bf16[32,64,128]{2,1,0:T(8,128)(2,1)S(1)}, u32[]{:S(2)}, u32[]{:S(2)}) async-start(bf16[32,64,128]{2,1,0:T(8,128)(2,1)} %get-tuple-element.15), calls=%async_computation | async-start | bytes 1048576 | tf_op jit(solution)/shard_map/all_to_all | solution.py:404
  51.2 0.1 collective-permute-start.3
  51.3 0.5 collective-permute-start.5
  51.8 0.3 collective-permute-start.21
  52.1 0.6 copy.16.bk.bv.bq
  52.7 0.6 stack.45.idx
  53.4 13.4 %all-to-all-done = bf16[32,64,128]{2,1,0:T(8,128)(2,1)S(1)} async-done(((bf16[32,64,128]{2,1,0:T(8,128)(2,1)}), bf16[32,64,128]{2,1,0:T(8,128)(2,1)S(1)}, u32[]{:S(2)}, u32[]{:S(2)}) %all-to-all-start) | async-done | bytes 524320 | tf_op jit(solution)/shard_map/all_to_all | solution.py:404
  66.8 0.9 collective-permute-start.1
  67.7 1.2 collective-permute-start.22
  68.9 13.7 %keys_values.1 = (bf16[512,128]{1,0:T(8,128)(2,1)}, f32[512,128]{1,0:T(8,128)}, f32[512,128]{1,0:T(8,128)}) custom-call(s32[8]{0:T(128)} %stack.45.idx, bf16[1024,8192]{1,0:T(8,128)(2,1)} %bitcast.42, bf16[1024,8192]{1,0:T(8,128)(2,1)} %bitcast.43, bf16[1024,128]{1,0:T(8,128)(2,1)} %bitcast.55, bf16[1024,128]{1,0:T(8,128)(2,1)} %collective-permute-done.3.w1, ...), custom_call_target="tpu_custom_call" | custom-call | flops 4294967296 | bytes 18874368 | tf_op jit(solution)/shard_map/keys_values/pallas_call | solution.py:165
  82.7 1.9 collective-permute-start.8
  84.6 4.3 %collective-permute-done.8.p3 = bf16[512,128]{1,0:T(8,128)(2,1)S(1)} collective-permute-done((bf16[512,128]{1,0:T(8,128)(2,1)}, bf16[512,128]{1,0:T(8,128)(2,1)S(1)}, u32[]{:S(2)}, u32[]{:S(2)}) %collective-permute-start.8) | collective-permute-done | bytes 131104 | tf_op jit(solution)/shard_map/ppermute | solution.py:428
  88.8 2.5 collective-permute-start.7
  91.4 4.4 %collective-permute-done.7.p2 = bf16[512,128]{1,0:T(8,128)(2,1)S(1)} collective-permute-done((bf16[512,128]{1,0:T(8,128)(2,1)}, bf16[512,128]{1,0:T(8,128)(2,1)S(1)}, u32[]{:S(2)}, u32[]{:S(2)}) %collective-permute-start.7) | collective-permute-done | bytes 131104 | tf_op jit(solution)/shard_map/ppermute | solution.py:428
  95.7 1.7 collective-permute-start.6
  97.4 0.8 copy-done.15
  98.3 0.5 collective-permute-start.2
  98.8 0.7 pad_add_fusion.pos
  99.4 65.3 %route_rows.1 = (bf16[1024,256]{1,0:T(8,128)(2,1)}, bf16[1024,256]{1,0:T(8,128)(2,1)}, bf16[1024,256]{1,0:T(8,128)(2,1)}, bf16[1024,256]{1,0:T(8,128)(2,1)}) custom-call(s32[3]{0:T(128)} %pad_add_fusion.pos, bf16[1024,256]{1,0:T(8,128)(2,1)} %copy-done.3, bf16[1024,256]{1,0:T(8,128)(2,1)} %copy-done.12, bf16[1024,256]{1,0:T(8,128)(2,1)} %copy-done.13, ...), custom_call_target="tpu_custom_call" | custom-call | bytes 4194304 | tf_op jit(solution)/shard_map/route_rows/pallas_call | solution.py:291
  164.8 0.7 collective-permute-start.23
  165.5 2.2 collective-permute-start.24
  167.7 1.4 collective-permute-start.25
  169.1 13.2 %query_head_1.1 = bf16[1024,128]{1,0:T(8,128)(2,1)} custom-call(s32[8]{0:T(128)} %stack.45.idx, bf16[1024,8192]{1,0:T(8,128)(2,1)} %bitcast.44, bf16[2048,128]{1,0:T(8,128)(2,1)} %bitcast.49, bf16[2048,128]{1,0:T(8,128)(2,1)} %collective-permute-done.13.w1, bf16[2048,128]{1,0:T(8,128)(2,1)} %copy-done.11, bf16[2048,128]{1,0:T(8,128)(2,1)} %collective-permute-done.15.w3, ...), custom_call_target="tpu_custom_call" | custom-call | flops 4294967296 | bytes 20971520 | tf_op jit(solution)/shard_map/query_head_1/pallas_call | solution.py:232
  182.3 0.1 collective-permute-start.26
  182.4 3.7 %collective-permute-start.16 = (bf16[1024,128]{1,0:T(8,128)(2,1)}, bf16[1024,128]{1,0:T(8,128)(2,1)S(1)}, u32[]{:S(2)}, u32[]{:S(2)}) collective-permute-start(bf16[1024,128]{1,0:T(8,128)(2,1)} %query_head_1.1), channel_id=1, source_target_pairs={{0,4},{1,5},{2,6},{3,7},{4,0},{5,1},{6,2},{7,3},{8,12},{9,13},{10,... | collective-permute-start | bytes 786440 | tf_op jit(solution)/shard_map/ppermute | solution.py:434
  186.1 13.0 %query_head_0.1 = bf16[1024,128]{1,0:T(8,128)(2,1)} custom-call(s32[8]{0:T(128)} %stack.45.idx, bf16[1024,8192]{1,0:T(8,128)(2,1)} %bitcast.45, bf16[2048,128]{1,0:T(8,128)(2,1)} %bitcast.52, bf16[2048,128]{1,0:T(8,128)(2,1)} %collective-permute-done.w1, bf16[2048,128]{1,0:T(8,128)(2,1)} %collective-permute-done.1.w2, bf16[2048,128]{1,0:T(8,128)(2,1)} %copy-done.14, ...), custom_call_target="tpu_custom_call" | custom-call | flops 4294967296 | bytes 20971520 | tf_op jit(solution)/shard_map/query_head_0/pallas_call | solution.py:232
  199.1 0.8 collective-permute-start.9
  199.9 0.2 collective-permute-start.27
  200.1 0.3 collective-permute-start.28
  200.4 0.2 collective-permute-start.29
  200.7 0.1 pad_maximum_fusion.1.refs_4_
  200.8 8.5 %collective-permute-done.9 = bf16[1024,128]{1,0:T(8,128)(2,1)S(1)} collective-permute-done((bf16[1024,128]{1,0:T(8,128)(2,1)}, bf16[1024,128]{1,0:T(8,128)(2,1)S(1)}, u32[]{:S(2)}, u32[]{:S(2)}) %collective-permute-start.9) | collective-permute-done | bytes 262176 | tf_op jit(solution)/shard_map/ppermute | solution.py:434
  209.3 1.7 collective-permute-start.19
  211.0 0.1 pad_maximum_fusion.refs_0_
  211.2 1.6 collective-permute-start.18
  212.8 0.2 collective-permute-start.17
  213.0 3.1 %collective-permute-start.12 = (bf16[1024,256]{1,0:T(8,128)(2,1)S(1)}, bf16[1024,256]{1,0:T(8,128)(2,1)S(1)}, u32[]{:S(2)}, u32[]{:S(2)}) collective-permute-start(bf16[1024,256]{1,0:T(8,128)(2,1)S(1)} %pad_maximum_fusion.refs_0_), channel_id=1, source_target_pairs={{0,3},{1,0},{2,1},{3,2},{4,7},{5,4},{6,5},{7,6},{8,11},{9,8},{10,9... | collective-permute-start | bytes 1572872 | tf_op jit(solution)/shard_map/ppermute | solution.py:439
  216.1 0.8 collective-permute-start.11
  216.8 17.5 %collective-permute-done.19.refs_7_ = bf16[1024,256]{1,0:T(8,128)(2,1)S(1)} collective-permute-done((bf16[1024,256]{1,0:T(8,128)(2,1)S(1)}, bf16[1024,256]{1,0:T(8,128)(2,1)S(1)}, u32[]{:S(2)}, u32[]{:S(2)}) %collective-permute-start.19) | collective-permute-done | bytes 524320 | tf_op jit(solution)/shard_map/ppermute | solution.py:439
  234.3 2.0 collective-permute-start.10
  236.3 2.6 collective-permute-done.17.refs_5_
  238.9 7.7 %collective-permute-done.12.refs_3_ = bf16[1024,256]{1,0:T(8,128)(2,1)S(1)} collective-permute-done((bf16[1024,256]{1,0:T(8,128)(2,1)S(1)}, bf16[1024,256]{1,0:T(8,128)(2,1)S(1)}, u32[]{:S(2)}, u32[]{:S(2)}) %collective-permute-start.12) | collective-permute-done | bytes 524320 | tf_op jit(solution)/shard_map/ppermute | solution.py:439
  246.6 3.5 %collective-permute-done.11.refs_2_ = bf16[1024,256]{1,0:T(8,128)(2,1)S(1)} collective-permute-done((bf16[1024,256]{1,0:T(8,128)(2,1)S(1)}, bf16[1024,256]{1,0:T(8,128)(2,1)S(1)}, u32[]{:S(2)}, u32[]{:S(2)}) %collective-permute-start.11) | collective-permute-done | bytes 524320 | tf_op jit(solution)/shard_map/ppermute | solution.py:439
  250.2 9.2 %collective-permute-done.10.refs_1_ = bf16[1024,256]{1,0:T(8,128)(2,1)S(1)} collective-permute-done((bf16[1024,256]{1,0:T(8,128)(2,1)S(1)}, bf16[1024,256]{1,0:T(8,128)(2,1)S(1)}, u32[]{:S(2)}, u32[]{:S(2)}) %collective-permute-start.10) | collective-permute-done | bytes 524320 | tf_op jit(solution)/shard_map/ppermute | solution.py:439
  259.4 0.7 copy-done.32
  260.1 10.4 %project_out.1 = bf16[4,1024,256]{2,1,0:T(8,128)(2,1)} custom-call(s32[8]{0:T(128)} %stack.45.idx, bf16[1024,256]{1,0:T(8,128)(2,1)} %copy-done.17, bf16[1024,256]{1,0:T(8,128)(2,1)} %copy-done.32, bf16[1024,256]{1,0:T(8,128)(2,1)} %copy-done.31, bf16[1024,256]{1,0:T(8,128)(2,1)} %copy-done.30, bf16[1024,256]{1,0:T(8,128)(2,1)} %copy-done.16, ...), custom_call_target="tpu_custom_call" | custom-call | flops 4294967296 | bytes 10485760 | tf_op jit(solution)/shard_map/project_out/pallas_call | solution.py:341
  270.5 1.5 slice_bitcast_fusion.2
  272.0 0.1 collective-permute-start.30
  272.1 2.0 collective-permute-start.32
  274.1 0.7 collective-permute-start.31
  274.7 12.1 %collective-permute-done.30 = bf16[1024,256]{1,0:T(8,128)(2,1)S(1)} collective-permute-done((bf16[1024,256]{1,0:T(8,128)(2,1)S(1)}, bf16[1024,256]{1,0:T(8,128)(2,1)S(1)}, u32[]{:S(2)}, u32[]{:S(2)}) %collective-permute-start.30) | collective-permute-done | bytes 524320 | tf_op jit(solution)/shard_map/ppermute | solution.py:445
  286.8 11.5 %collective-permute-done.32 = bf16[1024,256]{1,0:T(8,128)(2,1)S(1)} collective-permute-done((bf16[1024,256]{1,0:T(8,128)(2,1)S(1)}, bf16[1024,256]{1,0:T(8,128)(2,1)S(1)}, u32[]{:S(2)}, u32[]{:S(2)}) %collective-permute-start.32) | collective-permute-done | bytes 524320 | tf_op jit(solution)/shard_map/ppermute | solution.py:445
  298.3 1.3 fusion.1
  299.6 2.0 add_convert_fusion
  (92 shorter events, 0.3 us)
Async XLA Ops:
  1.6 32.0 %copy-start.7 = (bf16[2048,256]{1,0:T(8,128)(2,1)S(1)}, bf16[2048,256]{1,0:T(8,128)(2,1)}, u32[]{:S(2)}) copy-start(bf16[2048,256]{1,0:T(8,128)(2,1)} %param.17) | copy-start | bytes 3145732
  29.5 21.7 %copy-start.4 = (bf16[32,32,128]{2,1,0:T(8,128)(2,1)}, bf16[32,32,128]{2,1,0:T(8,128)(2,1)S(1)}, u32[]{:S(2)}) copy-start(bf16[32,32,128]{2,1,0:T(8,128)(2,1)S(1)} %all_to_all.15) | copy-start | bytes 786436
  29.5 22.5 %copy-start.18 = (bf16[10240]{0:T(1024)(128)(2,1)S(1)}, bf16[10240]{0:T(1024)(128)(2,1)}, u32[]{:S(2)}) copy-start(bf16[10240]{0:T(1024)(128)(2,1)} %param.16) | copy-start | bytes 61444
  29.5 16.0 %all-to-all-start.2 = ((bf16[32,64,128]{2,1,0:T(8,128)(2,1)}), bf16[32,64,128]{2,1,0:T(8,128)(2,1)S(1)}, u32[]{:S(2)}, u32[]{:S(2)}) async-start(bf16[32,64,128]{2,1,0:T(8,128)(2,1)} %get-tuple-element.20), calls=%async_computation.2 | async-start | bytes 1048576 | tf_op jit(solution)/shard_map/all_to_all | solution.py:404
  34.5 48.1 %copy-start.3 = (bf16[1024,256]{1,0:T(8,128)(2,1)}, bf16[1024,256]{1,0:T(8,128)(2,1)S(1)}, u32[]{:S(2)}) copy-start(bf16[1024,256]{1,0:T(8,128)(2,1)S(1)} %get-tuple-element.29.k0) | copy-start | bytes 1572868
  34.5 32.3 %collective-permute-start.20 = (bf16[1024,256]{1,0:T(8,128)(2,1)}, bf16[1024,256]{1,0:T(8,128)(2,1)S(1)}, u32[]{:S(2)}, u32[]{:S(2)}) collective-permute-start(bf16[1024,256]{1,0:T(8,128)(2,1)} %get-tuple-element.28), channel_id=1, source_target_pairs={{0,64},{64,0},{1,65},{65,1},{2,66},{66,2},{3,67},{67,3},{4,68},{68... | collective-permute-start | bytes 1572872 | tf_op jit(solution)/shard_map/ppermute | solution.py:417
  34.5 16.9 %collective-permute-start.4 = (bf16[1024,128]{1,0:T(8,128)(2,1)S(1)}, bf16[1024,128]{1,0:T(8,128)(2,1)}, u32[]{:S(2)}, u32[]{:S(2)}) collective-permute-start(bf16[1024,128]{1,0:T(8,128)(2,1)S(1)} %bitcast.53), channel_id=1, source_target_pairs={{0,32},{32,0},{1,33},{33,1},{2,34},{34,2},{3,35},{35,3},{4,36},{36... | collective-permute-start | bytes 786440 | tf_op jit(solution)/shard_map/ppermute | solution.py:406
  45.5 37.1 %copy-start.1 = (bf16[32,64,128]{2,1,0:T(8,128)(2,1)}, bf16[32,64,128]{2,1,0:T(8,128)(2,1)S(1)}, u32[]{:S(2)}) copy-start(bf16[32,64,128]{2,1,0:T(8,128)(2,1)S(1)} %all-to-all-done.2) | copy-start | bytes 1572868
  45.6 23.4 %collective-permute-start.14 = (bf16[2048,128]{1,0:T(8,128)(2,1)S(1)}, bf16[2048,128]{1,0:T(8,128)(2,1)S(1)}, u32[]{:S(2)}, u32[]{:S(2)}) collective-permute-start(bf16[2048,128]{1,0:T(8,128)(2,1)S(1)} %bitcast.47), channel_id=1, source_target_pairs={{0,32},{32,0},{1,33},{33,1},{2,34},{34,2},{3,35},{35,3},{4,36},{36... | collective-permute-start | bytes 1572872 | tf_op jit(solution)/shard_map/ppermute | solution.py:406
  46.2 20.6 %all-to-all-start = ((bf16[32,64,128]{2,1,0:T(8,128)(2,1)}), bf16[32,64,128]{2,1,0:T(8,128)(2,1)S(1)}, u32[]{:S(2)}, u32[]{:S(2)}) async-start(bf16[32,64,128]{2,1,0:T(8,128)(2,1)} %get-tuple-element.15), calls=%async_computation | async-start | bytes 1048576 | tf_op jit(solution)/shard_map/all_to_all | solution.py:404
  51.2 2.1 collective-permute-start.3
  51.3 16.4 %collective-permute-start.5 = (bf16[1024,128]{1,0:T(8,128)(2,1)}, bf16[1024,128]{1,0:T(8,128)(2,1)}, u32[]{:S(2)}, u32[]{:S(2)}) collective-permute-start(bf16[1024,128]{1,0:T(8,128)(2,1)} %collective-permute-done.4.w2), channel_id=1, source_target_pairs={{0,64},{64,0},{1,65},{65,1},{2,66},{66,2},{3,67},{67,3},{4,68},{68... | collective-permute-start | bytes 786440 | tf_op jit(solution)/shard_map/ppermute | solution.py:408
  51.8 30.8 %collective-permute-start.21 = (bf16[1024,256]{1,0:T(8,128)(2,1)S(1)}, bf16[1024,256]{1,0:T(8,128)(2,1)S(1)}, u32[]{:S(2)}, u32[]{:S(2)}) collective-permute-start(bf16[1024,256]{1,0:T(8,128)(2,1)S(1)} %get-tuple-element.29.k0), channel_id=1, source_target_pairs={{0,32},{32,0},{1,33},{33,1},{2,34},{34,2},{3,35},{35,3},{4,36},{36... | collective-permute-start | bytes 1572872 | tf_op jit(solution)/shard_map/ppermute | solution.py:418
  53.4 112.1 %collective-permute-start.13 = (bf16[2048,128]{1,0:T(8,128)(2,1)S(1)}, bf16[2048,128]{1,0:T(8,128)(2,1)}, u32[]{:S(2)}, u32[]{:S(2)}) collective-permute-start(bf16[2048,128]{1,0:T(8,128)(2,1)S(1)} %bitcast.48), channel_id=1, source_target_pairs={{0,64},{64,0},{1,65},{65,1},{2,66},{66,2},{3,67},{67,3},{4,68},{68... | collective-permute-start | bytes 1572872 | tf_op jit(solution)/shard_map/ppermute | solution.py:407
  66.8 30.6 %copy-start.2 = (bf16[32,64,128]{2,1,0:T(8,128)(2,1)}, bf16[32,64,128]{2,1,0:T(8,128)(2,1)S(1)}, u32[]{:S(2)}) copy-start(bf16[32,64,128]{2,1,0:T(8,128)(2,1)S(1)} %all-to-all-done) | copy-start | bytes 1572868
  66.8 15.8 %copy-start.12 = (bf16[1024,256]{1,0:T(8,128)(2,1)}, bf16[1024,256]{1,0:T(8,128)(2,1)S(1)}, u32[]{:S(2)}) copy-start(bf16[1024,256]{1,0:T(8,128)(2,1)S(1)} %collective-permute-done.20.r0) | copy-start | bytes 1572868
  66.8 30.6 %collective-permute-start.1 = (bf16[2048,128]{1,0:T(8,128)(2,1)S(1)}, bf16[2048,128]{1,0:T(8,128)(2,1)}, u32[]{:S(2)}, u32[]{:S(2)}) collective-permute-start(bf16[2048,128]{1,0:T(8,128)(2,1)S(1)} %bitcast.50), channel_id=1, source_target_pairs={{0,32},{32,0},{1,33},{33,1},{2,34},{34,2},{3,35},{35,3},{4,36},{36... | collective-permute-start | bytes 1572872 | tf_op jit(solution)/shard_map/ppermute | solution.py:406
  67.7 29.7 %collective-permute-start.22 = (bf16[1024,256]{1,0:T(8,128)(2,1)S(1)}, bf16[1024,256]{1,0:T(8,128)(2,1)S(1)}, u32[]{:S(2)}, u32[]{:S(2)}) collective-permute-start(bf16[1024,256]{1,0:T(8,128)(2,1)S(1)} %collective-permute-done.20.r0), channel_id=1, source_target_pairs={{0,32},{32,0},{1,33},{33,1},{2,34},{34,2},{3,35},{35,3},{4,36},{36... | collective-permute-start | bytes 1572872 | tf_op jit(solution)/shard_map/ppermute | solution.py:419
  68.9 13.7 %copy-start.11 = (bf16[2048,128]{1,0:T(8,128)(2,1)}, bf16[2048,128]{1,0:T(8,128)(2,1)S(1)}, u32[]{:S(2)}) copy-start(bf16[2048,128]{1,0:T(8,128)(2,1)S(1)} %collective-permute-done.14.w2) | copy-start | bytes 1572868
  68.9 98.7 %collective-permute-start.15 = (bf16[2048,128]{1,0:T(8,128)(2,1)S(1)}, bf16[2048,128]{1,0:T(8,128)(2,1)}, u32[]{:S(2)}, u32[]{:S(2)}) collective-permute-start(bf16[2048,128]{1,0:T(8,128)(2,1)S(1)} %collective-permute-done.14.w2), channel_id=1, source_target_pairs={{0,64},{64,0},{1,65},{65,1},{2,66},{66,2},{3,67},{67,3},{4,68},{68... | collective-permute-start | bytes 1572872 | tf_op jit(solution)/shard_map/ppermute | solution.py:408
  82.7 16.8 %copy-start.13 = (bf16[1024,256]{1,0:T(8,128)(2,1)}, bf16[1024,256]{1,0:T(8,128)(2,1)S(1)}, u32[]{:S(2)}) copy-start(bf16[1024,256]{1,0:T(8,128)(2,1)S(1)} %collective-permute-done.21.k1) | copy-start | bytes 1572868
  82.7 6.2 %collective-permute-start.8 = (bf16[512,128]{1,0:T(8,128)(2,1)}, bf16[512,128]{1,0:T(8,128)(2,1)S(1)}, u32[]{:S(2)}, u32[]{:S(2)}) collective-permute-start(bf16[512,128]{1,0:T(8,128)(2,1)} %get-tuple-element.19.p0), channel_id=1, source_target_pairs={{0,3},{1,0},{2,1},{3,2},{4,7},{5,4},{6,5},{7,6},{8,11},{9,8},{10,9... | collective-permute-start | bytes 393224 | tf_op jit(solution)/shard_map/ppermute | solution.py:428
  88.8 80.3 %copy-start.8 = (bf16[512,128]{1,0:T(8,128)(2,1)}, bf16[512,128]{1,0:T(8,128)(2,1)S(1)}, u32[]{:S(2)}) copy-start(bf16[512,128]{1,0:T(8,128)(2,1)S(1)} %collective-permute-done.8.p3) | copy-start | bytes 393220
  88.8 6.9 %collective-permute-start.7 = (bf16[512,128]{1,0:T(8,128)(2,1)}, bf16[512,128]{1,0:T(8,128)(2,1)S(1)}, u32[]{:S(2)}, u32[]{:S(2)}) collective-permute-start(bf16[512,128]{1,0:T(8,128)(2,1)} %get-tuple-element.19.p0), channel_id=1, source_target_pairs={{0,2},{1,3},{2,0},{3,1},{4,6},{5,7},{6,4},{7,5},{8,10},{9,11},{10,... | collective-permute-start | bytes 393224 | tf_op jit(solution)/shard_map/ppermute | solution.py:428
  95.7 73.4 %copy-start.9 = (bf16[512,128]{1,0:T(8,128)(2,1)}, bf16[512,128]{1,0:T(8,128)(2,1)S(1)}, u32[]{:S(2)}) copy-start(bf16[512,128]{1,0:T(8,128)(2,1)S(1)} %collective-permute-done.7.p2) | copy-start | bytes 393220
  95.7 69.0 %collective-permute-start.6 = (bf16[512,128]{1,0:T(8,128)(2,1)}, bf16[512,128]{1,0:T(8,128)(2,1)S(1)}, u32[]{:S(2)}, u32[]{:S(2)}) collective-permute-start(bf16[512,128]{1,0:T(8,128)(2,1)} %get-tuple-element.19.p0), channel_id=1, source_target_pairs={{0,1},{1,2},{2,3},{3,0},{4,5},{5,6},{6,7},{7,4},{8,9},{9,10},{10,1... | collective-permute-start | bytes 393224 | tf_op jit(solution)/shard_map/ppermute | solution.py:428
  97.4 84.9 %collective-permute-start = (bf16[2048,128]{1,0:T(8,128)(2,1)S(1)}, bf16[2048,128]{1,0:T(8,128)(2,1)}, u32[]{:S(2)}, u32[]{:S(2)}) collective-permute-start(bf16[2048,128]{1,0:T(8,128)(2,1)S(1)} %bitcast.51), channel_id=1, source_target_pairs={{0,64},{64,0},{1,65},{65,1},{2,66},{66,2},{3,67},{67,3},{4,68},{68... | collective-permute-start | bytes 1572872 | tf_op jit(solution)/shard_map/ppermute | solution.py:407
  98.3 84.1 %collective-permute-start.2 = (bf16[2048,128]{1,0:T(8,128)(2,1)}, bf16[2048,128]{1,0:T(8,128)(2,1)S(1)}, u32[]{:S(2)}, u32[]{:S(2)}) collective-permute-start(bf16[2048,128]{1,0:T(8,128)(2,1)} %collective-permute-done.1.w2), channel_id=1, source_target_pairs={{0,64},{64,0},{1,65},{65,1},{2,66},{66,2},{3,67},{67,3},{4,68},{68... | collective-permute-start | bytes 1572872 | tf_op jit(solution)/shard_map/ppermute | solution.py:408
  164.8 4.3 %copy-start.10 = (bf16[512,128]{1,0:T(8,128)(2,1)}, bf16[512,128]{1,0:T(8,128)(2,1)S(1)}, u32[]{:S(2)}) copy-start(bf16[512,128]{1,0:T(8,128)(2,1)S(1)} %collective-permute-done.6.p1) | copy-start | bytes 393220
  164.8 34.3 %collective-permute-start.23 = (bf16[1024,256]{1,0:T(8,128)(2,1)}, bf16[1024,256]{1,0:T(8,128)(2,1)S(1)}, u32[]{:S(2)}, u32[]{:S(2)}) collective-permute-start(bf16[1024,256]{1,0:T(8,128)(2,1)} %get-tuple-element.22), channel_id=1, source_target_pairs={{0,8},{1,9},{2,10},{3,11},{4,12},{5,13},{6,14},{7,15},{8,16},{9,17... | collective-permute-start | bytes 1572872 | tf_op jit(solution)/shard_map/ppermute | solution.py:422
  165.5 34.4 %collective-permute-start.24 = (bf16[1024,256]{1,0:T(8,128)(2,1)}, bf16[1024,256]{1,0:T(8,128)(2,1)S(1)}, u32[]{:S(2)}, u32[]{:S(2)}) collective-permute-start(bf16[1024,256]{1,0:T(8,128)(2,1)} %get-tuple-element.23), channel_id=1, source_target_pairs={{0,16},{1,17},{2,18},{3,19},{4,20},{5,21},{6,22},{7,23},{8,24},{9,... | collective-permute-start | bytes 1572872 | tf_op jit(solution)/shard_map/ppermute | solution.py:422
  167.7 32.5 %collective-permute-start.25 = (bf16[1024,256]{1,0:T(8,128)(2,1)}, bf16[1024,256]{1,0:T(8,128)(2,1)S(1)}, u32[]{:S(2)}, u32[]{:S(2)}) collective-permute-start(bf16[1024,256]{1,0:T(8,128)(2,1)} %get-tuple-element.24), channel_id=1, source_target_pairs={{0,24},{1,25},{2,26},{3,27},{4,28},{5,29},{6,30},{7,31},{8,0},{9,1... | collective-permute-start | bytes 1572872 | tf_op jit(solution)/shard_map/ppermute | solution.py:422
  169.1 13.2 %copy-start.19 = (bf16[1024,256]{1,0:T(8,128)(2,1)S(1)}, bf16[1024,256]{1,0:T(8,128)(2,1)}, u32[]{:S(2)}) copy-start(bf16[1024,256]{1,0:T(8,128)(2,1)} %get-tuple-element.21) | copy-start | bytes 1572868
  182.3 18.4 %copy-start.5 = (bf16[1024,128]{1,0:T(8,128)(2,1)S(1)}, bf16[1024,128]{1,0:T(8,128)(2,1)}, u32[]{:S(2)}) copy-start(bf16[1024,128]{1,0:T(8,128)(2,1)} %query_head_1.1) | copy-start | bytes 786436
  182.3 28.9 %collective-permute-start.26 = (bf16[1024,256]{1,0:T(8,128)(2,1)S(1)}, bf16[1024,256]{1,0:T(8,128)(2,1)S(1)}, u32[]{:S(2)}, u32[]{:S(2)}) collective-permute-start(bf16[1024,256]{1,0:T(8,128)(2,1)S(1)} %copy-done.19), channel_id=1, source_target_pairs={{0,64},{64,0},{1,65},{65,1},{2,66},{66,2},{3,67},{67,3},{4,68},{68... | collective-permute-start | bytes 1572872 | tf_op jit(solution)/shard_map/ppermute | solution.py:424
  182.4 18.0 %collective-permute-start.16 = (bf16[1024,128]{1,0:T(8,128)(2,1)}, bf16[1024,128]{1,0:T(8,128)(2,1)S(1)}, u32[]{:S(2)}, u32[]{:S(2)}) collective-permute-start(bf16[1024,128]{1,0:T(8,128)(2,1)} %query_head_1.1), channel_id=1, source_target_pairs={{0,4},{1,5},{2,6},{3,7},{4,0},{5,1},{6,2},{7,3},{8,12},{9,13},{10,... | collective-permute-start | bytes 786440 | tf_op jit(solution)/shard_map/ppermute | solution.py:434
  199.1 11.9 %copy-start.6 = (bf16[1024,128]{1,0:T(8,128)(2,1)S(1)}, bf16[1024,128]{1,0:T(8,128)(2,1)}, u32[]{:S(2)}) copy-start(bf16[1024,128]{1,0:T(8,128)(2,1)} %query_head_0.1) | copy-start | bytes 786436
  199.1 12.0 %copy-start.20 = (bf16[1024,256]{1,0:T(8,128)(2,1)}, bf16[1024,256]{1,0:T(8,128)(2,1)S(1)}, u32[]{:S(2)}) copy-start(bf16[1024,256]{1,0:T(8,128)(2,1)S(1)} %collective-permute-done.23) | copy-start | bytes 1572868
  199.1 10.2 %collective-permute-start.9 = (bf16[1024,128]{1,0:T(8,128)(2,1)}, bf16[1024,128]{1,0:T(8,128)(2,1)S(1)}, u32[]{:S(2)}, u32[]{:S(2)}) collective-permute-start(bf16[1024,128]{1,0:T(8,128)(2,1)} %query_head_0.1), channel_id=1, source_target_pairs={{0,4},{1,5},{2,6},{3,7},{4,0},{5,1},{6,2},{7,3},{8,12},{9,13},{10,... | collective-permute-start | bytes 786440 | tf_op jit(solution)/shard_map/ppermute | solution.py:434
  199.9 11.2 %copy-start.21 = (bf16[1024,256]{1,0:T(8,128)(2,1)}, bf16[1024,256]{1,0:T(8,128)(2,1)S(1)}, u32[]{:S(2)}) copy-start(bf16[1024,256]{1,0:T(8,128)(2,1)S(1)} %collective-permute-done.24) | copy-start | bytes 1572868
  199.9 12.9 %collective-permute-start.27 = (bf16[1024,256]{1,0:T(8,128)(2,1)S(1)}, bf16[1024,256]{1,0:T(8,128)(2,1)S(1)}, u32[]{:S(2)}, u32[]{:S(2)}) collective-permute-start(bf16[1024,256]{1,0:T(8,128)(2,1)S(1)} %collective-permute-done.23), channel_id=1, source_target_pairs={{0,64},{64,0},{1,65},{65,1},{2,66},{66,2},{3,67},{67,3},{4,68},{68... | collective-permute-start | bytes 1572872 | tf_op jit(solution)/shard_map/ppermute | solution.py:424
  200.1 11.0 %copy-start.22 = (bf16[1024,256]{1,0:T(8,128)(2,1)}, bf16[1024,256]{1,0:T(8,128)(2,1)S(1)}, u32[]{:S(2)}) copy-start(bf16[1024,256]{1,0:T(8,128)(2,1)S(1)} %collective-permute-done.25) | copy-start | bytes 1572868
  200.1 12.8 %collective-permute-start.28 = (bf16[1024,256]{1,0:T(8,128)(2,1)S(1)}, bf16[1024,256]{1,0:T(8,128)(2,1)S(1)}, u32[]{:S(2)}, u32[]{:S(2)}) collective-permute-start(bf16[1024,256]{1,0:T(8,128)(2,1)S(1)} %collective-permute-done.24), channel_id=1, source_target_pairs={{0,64},{64,0},{1,65},{65,1},{2,66},{66,2},{3,67},{67,3},{4,68},{68... | collective-permute-start | bytes 1572872 | tf_op jit(solution)/shard_map/ppermute | solution.py:424
  200.4 15.6 %collective-permute-start.29 = (bf16[1024,256]{1,0:T(8,128)(2,1)S(1)}, bf16[1024,256]{1,0:T(8,128)(2,1)S(1)}, u32[]{:S(2)}, u32[]{:S(2)}) collective-permute-start(bf16[1024,256]{1,0:T(8,128)(2,1)S(1)} %collective-permute-done.25), channel_id=1, source_target_pairs={{0,64},{64,0},{1,65},{65,1},{2,66},{66,2},{3,67},{67,3},{4,68},{68... | collective-permute-start | bytes 1572872 | tf_op jit(solution)/shard_map/ppermute | solution.py:424
  200.8 58.6 %copy-start.16 = (bf16[1024,256]{1,0:T(8,128)(2,1)}, bf16[1024,256]{1,0:T(8,128)(2,1)S(1)}, u32[]{:S(2)}) copy-start(bf16[1024,256]{1,0:T(8,128)(2,1)S(1)} %pad_maximum_fusion.1.refs_4_) | copy-start | bytes 1572868
  209.3 25.1 %collective-permute-start.19 = (bf16[1024,256]{1,0:T(8,128)(2,1)S(1)}, bf16[1024,256]{1,0:T(8,128)(2,1)S(1)}, u32[]{:S(2)}, u32[]{:S(2)}) collective-permute-start(bf16[1024,256]{1,0:T(8,128)(2,1)S(1)} %pad_maximum_fusion.1.refs_4_), channel_id=1, source_target_pairs={{0,3},{1,0},{2,1},{3,2},{4,7},{5,4},{6,5},{7,6},{8,11},{9,8},{10,9... | collective-permute-start | bytes 1572872 | tf_op jit(solution)/shard_map/ppermute | solution.py:439
  211.1 48.2 %copy-start.17 = (bf16[1024,256]{1,0:T(8,128)(2,1)}, bf16[1024,256]{1,0:T(8,128)(2,1)S(1)}, u32[]{:S(2)}) copy-start(bf16[1024,256]{1,0:T(8,128)(2,1)S(1)} %pad_maximum_fusion.refs_0_) | copy-start | bytes 1572868
  211.2 48.2 %copy-start.23 = (bf16[1024,256]{1,0:T(8,128)(2,1)}, bf16[1024,256]{1,0:T(8,128)(2,1)S(1)}, u32[]{:S(2)}) copy-start(bf16[1024,256]{1,0:T(8,128)(2,1)S(1)} %collective-permute-done.26) | copy-start | bytes 1572868
  211.2 25.1 %collective-permute-start.18 = (bf16[1024,256]{1,0:T(8,128)(2,1)S(1)}, bf16[1024,256]{1,0:T(8,128)(2,1)S(1)}, u32[]{:S(2)}, u32[]{:S(2)}) collective-permute-start(bf16[1024,256]{1,0:T(8,128)(2,1)S(1)} %pad_maximum_fusion.1.refs_4_), channel_id=1, source_target_pairs={{0,2},{1,3},{2,0},{3,1},{4,6},{5,7},{6,4},{7,5},{8,10},{9,11},{10,... | collective-permute-start | bytes 1572872 | tf_op jit(solution)/shard_map/ppermute | solution.py:439
  212.8 46.5 %copy-start.24 = (bf16[1024,256]{1,0:T(8,128)(2,1)}, bf16[1024,256]{1,0:T(8,128)(2,1)S(1)}, u32[]{:S(2)}) copy-start(bf16[1024,256]{1,0:T(8,128)(2,1)S(1)} %collective-permute-done.27) | copy-start | bytes 1572868
  212.8 26.1 %collective-permute-start.17 = (bf16[1024,256]{1,0:T(8,128)(2,1)S(1)}, bf16[1024,256]{1,0:T(8,128)(2,1)S(1)}, u32[]{:S(2)}, u32[]{:S(2)}) collective-permute-start(bf16[1024,256]{1,0:T(8,128)(2,1)S(1)} %pad_maximum_fusion.1.refs_4_), channel_id=1, source_target_pairs={{0,1},{1,2},{2,3},{3,0},{4,5},{5,6},{6,7},{7,4},{8,9},{9,10},{10,1... | collective-permute-start | bytes 1572872 | tf_op jit(solution)/shard_map/ppermute | solution.py:439
  213.0 46.4 %copy-start.25 = (bf16[1024,256]{1,0:T(8,128)(2,1)}, bf16[1024,256]{1,0:T(8,128)(2,1)S(1)}, u32[]{:S(2)}) copy-start(bf16[1024,256]{1,0:T(8,128)(2,1)S(1)} %collective-permute-done.28) | copy-start | bytes 1572868
  213.0 33.7 %collective-permute-start.12 = (bf16[1024,256]{1,0:T(8,128)(2,1)S(1)}, bf16[1024,256]{1,0:T(8,128)(2,1)S(1)}, u32[]{:S(2)}, u32[]{:S(2)}) collective-permute-start(bf16[1024,256]{1,0:T(8,128)(2,1)S(1)} %pad_maximum_fusion.refs_0_), channel_id=1, source_target_pairs={{0,3},{1,0},{2,1},{3,2},{4,7},{5,4},{6,5},{7,6},{8,11},{9,8},{10,9... | collective-permute-start | bytes 1572872 | tf_op jit(solution)/shard_map/ppermute | solution.py:439
  216.0 43.3 %copy-start.26 = (bf16[1024,256]{1,0:T(8,128)(2,1)}, bf16[1024,256]{1,0:T(8,128)(2,1)S(1)}, u32[]{:S(2)}) copy-start(bf16[1024,256]{1,0:T(8,128)(2,1)S(1)} %collective-permute-done.29) | copy-start | bytes 1572868
  216.1 34.1 %collective-permute-start.11 = (bf16[1024,256]{1,0:T(8,128)(2,1)S(1)}, bf16[1024,256]{1,0:T(8,128)(2,1)S(1)}, u32[]{:S(2)}, u32[]{:S(2)}) collective-permute-start(bf16[1024,256]{1,0:T(8,128)(2,1)S(1)} %pad_maximum_fusion.refs_0_), channel_id=1, source_target_pairs={{0,2},{1,3},{2,0},{3,1},{4,6},{5,7},{6,4},{7,5},{8,10},{9,11},{10,... | collective-permute-start | bytes 1572872 | tf_op jit(solution)/shard_map/ppermute | solution.py:439
  234.3 25.1 %copy-start.27 = (bf16[1024,256]{1,0:T(8,128)(2,1)}, bf16[1024,256]{1,0:T(8,128)(2,1)S(1)}, u32[]{:S(2)}) copy-start(bf16[1024,256]{1,0:T(8,128)(2,1)S(1)} %collective-permute-done.19.refs_7_) | copy-start | bytes 1572868
  234.3 25.0 %collective-permute-start.10 = (bf16[1024,256]{1,0:T(8,128)(2,1)S(1)}, bf16[1024,256]{1,0:T(8,128)(2,1)S(1)}, u32[]{:S(2)}, u32[]{:S(2)}) collective-permute-start(bf16[1024,256]{1,0:T(8,128)(2,1)S(1)} %pad_maximum_fusion.refs_0_), channel_id=1, source_target_pairs={{0,1},{1,2},{2,3},{3,0},{4,5},{5,6},{6,7},{7,4},{8,9},{9,10},{10,1... | collective-permute-start | bytes 1572872 | tf_op jit(solution)/shard_map/ppermute | solution.py:439
  236.3 23.1 %copy-start.28 = (bf16[1024,256]{1,0:T(8,128)(2,1)}, bf16[1024,256]{1,0:T(8,128)(2,1)S(1)}, u32[]{:S(2)}) copy-start(bf16[1024,256]{1,0:T(8,128)(2,1)S(1)} %collective-permute-done.18.refs_6_) | copy-start | bytes 1572868
  238.9 20.4 %copy-start.29 = (bf16[1024,256]{1,0:T(8,128)(2,1)}, bf16[1024,256]{1,0:T(8,128)(2,1)S(1)}, u32[]{:S(2)}) copy-start(bf16[1024,256]{1,0:T(8,128)(2,1)S(1)} %collective-permute-done.17.refs_5_) | copy-start | bytes 1572868
  246.6 12.8 %copy-start.30 = (bf16[1024,256]{1,0:T(8,128)(2,1)}, bf16[1024,256]{1,0:T(8,128)(2,1)S(1)}, u32[]{:S(2)}) copy-start(bf16[1024,256]{1,0:T(8,128)(2,1)S(1)} %collective-permute-done.12.refs_3_) | copy-start | bytes 1572868
  250.2 9.2 %copy-start.31 = (bf16[1024,256]{1,0:T(8,128)(2,1)}, bf16[1024,256]{1,0:T(8,128)(2,1)S(1)}, u32[]{:S(2)}) copy-start(bf16[1024,256]{1,0:T(8,128)(2,1)S(1)} %collective-permute-done.11.refs_2_) | copy-start | bytes 1572868
  272.0 14.9 %collective-permute-start.30 = (bf16[1024,256]{1,0:T(8,128)(2,1)S(1)}, bf16[1024,256]{1,0:T(8,128)(2,1)S(1)}, u32[]{:S(2)}, u32[]{:S(2)}) collective-permute-start(bf16[1024,256]{1,0:T(8,128)(2,1)S(1)} %get-tuple-element.25), channel_id=1, source_target_pairs={{0,24},{1,25},{2,26},{3,27},{4,28},{5,29},{6,30},{7,31},{8,0},{9,1... | collective-permute-start | bytes 1572872 | tf_op jit(solution)/shard_map/ppermute | solution.py:445
  272.1 26.2 %collective-permute-start.32 = (bf16[1024,256]{1,0:T(8,128)(2,1)S(1)}, bf16[1024,256]{1,0:T(8,128)(2,1)S(1)}, u32[]{:S(2)}, u32[]{:S(2)}) collective-permute-start(bf16[1024,256]{1,0:T(8,128)(2,1)S(1)} %get-tuple-element.26), channel_id=1, source_target_pairs={{0,8},{1,9},{2,10},{3,11},{4,12},{5,13},{6,14},{7,15},{8,16},{9,17... | collective-permute-start | bytes 1572872 | tf_op jit(solution)/shard_map/ppermute | solution.py:445
  274.1 24.2 %collective-permute-start.31 = (bf16[1024,256]{1,0:T(8,128)(2,1)S(1)}, bf16[1024,256]{1,0:T(8,128)(2,1)S(1)}, u32[]{:S(2)}, u32[]{:S(2)}) collective-permute-start(bf16[1024,256]{1,0:T(8,128)(2,1)S(1)} %get-tuple-element.27), channel_id=1, source_target_pairs={{0,16},{1,17},{2,18},{3,19},{4,20},{5,21},{6,22},{7,23},{8,24},{9,... | collective-permute-start | bytes 1572872 | tf_op jit(solution)/shard_map/ppermute | solution.py:445
  (4 other events, 6.1 us)

commit v2 on v0

v2 whole, which is shorter than its diff:
```python
import functools

import jax
import jax.numpy as jnp
import numpy as np
from jax import lax
from jax.experimental import pallas as pl
from jax.experimental.pallas import tpu as pltpu
from jax.sharding import PartitionSpec as P

HD = 128
SPAN = 256
D = 8192
BF = jnp.bfloat16
F32 = jnp.float32
VMEM_LIMIT = 22 * 1024 * 1024


def rope_tables():
    half = HD // 2
    inverse = 1000000.0 ** (-np.arange(half, dtype=np.float64) * 2.0 / HD)
    angles = (
        np.arange(SPAN, dtype=np.float32)[:, None] * inverse.astype(np.float32)[None, :]
    )
    angles = angles.astype(np.float64)
    return np.cos(angles).astype(np.float32), np.sin(angles).astype(np.float32)


def kv_lanes(part):
    low = list(range(16 * part, 16 * part + 16))
    return low + [64 + i for i in low] + list(range(128 + 32 * part, 160 + 32 * part))


def tables():
    cosine, sine = rope_tables()
    pack = np.zeros((2, 256, 512), np.float32)
    gather = np.zeros((4, 2, 128, 256), np.float32)
    bias_sel = np.zeros((4, 256, 128), np.float32)
    k_cos = np.ones((4, SPAN, 128), np.float32)
    k_sin = np.zeros((4, SPAN, 128), np.float32)
    turn = np.zeros((64, 64), np.float32)
    for lane in range(16):
        turn[lane + 16, lane] = 1.0
        turn[lane, lane + 16] = 1.0
    for part in range(4):
        lanes = kv_lanes(part)
        for lane, column in enumerate(lanes):
            pack[0, column, part * 128 + lane] = 1.0
            pack[1, column, part * 128 + 64 + lane] = 1.0
            gather[part, 0, lane, column] = 1.0
            gather[part, 1, 64 + lane, column] = 1.0
            bias_sel[part, column, lane] = 1.0
        bias_sel[part, :, 64:] = bias_sel[part, :, :64] @ turn
        dims = slice(16 * part, 16 * part + 16)
        for base in (0, 64):
            k_cos[part, :, base : base + 16] = cosine[:, dims]
            k_cos[part, :, base + 16 : base + 32] = cosine[:, dims]
            k_sin[part, :, base : base + 16] = -sine[:, dims]
            k_sin[part, :, base + 16 : base + 32] = sine[:, dims]
    unpack = np.zeros((128, 256), np.float32)
    unpack[:64, :64] = np.eye(64)
    unpack[:64, 64:128] = turn
    unpack[64:, 128:192] = np.eye(64)
    unpack[64:, 192:] = turn
    q_cos = np.concatenate([cosine, cosine], 1)
    q_sin = np.concatenate([-sine, sine], 1)
    return {
        "pack": jnp.asarray(pack, BF),
        "gather": jnp.asarray(gather, BF),
        "bias_sel": jnp.asarray(bias_sel, BF),
        "unpack": jnp.asarray(unpack, BF),
        "k_cos": jnp.asarray(k_cos),
        "k_sin": jnp.asarray(k_sin),
        "q_cos": jnp.asarray(q_cos),
        "q_sin": jnp.asarray(q_sin),
    }


def dot(a, b):
    return jnp.dot(a, b, preferred_element_type=F32)


def params(**kw):
    return pltpu.CompilerParams(vmem_limit_bytes=VMEM_LIMIT, **kw)


VM = pl.BlockSpec(memory_space=pltpu.VMEM)
SM = pl.BlockSpec(memory_space=pltpu.SMEM)
AN = pl.BlockSpec(memory_space=pl.ANY)


def shape(dims, dtype=BF):
    return jax.ShapeDtypeStruct(dims, dtype)


def cost(flops, mib, trans=0):
    return pl.CostEstimate(flops=flops, bytes_accessed=mib << 20, transcendentals=trans)


def call(body, name, in_specs, out_shape, out_specs, estimate, scratch=()):
    return pl.pallas_call(
        body,
        in_specs=in_specs,
        out_specs=out_specs,
        out_shape=out_shape,
        scratch_shapes=list(scratch),
        compiler_params=params(),
        name=name,
        cost_estimate=estimate,
    )


def pack_body(idx, w, gain, sel, after, out):
    row = gain[pl.ds(idx[0] * 16 + idx[4] // 2, 1), :]
    lane = lax.broadcasted_iota(jnp.int32, (64, 128), 1)
    sub = lax.broadcasted_iota(jnp.int32, (64, 128), 0)
    hit = lane == sub + idx[4] % 2 * 64
    scale = jnp.sum(jnp.where(hit, jnp.broadcast_to(row, (64, 128)), 0.0), axis=1, keepdims=True)
    for t in range(32):
        for h in range(2):
            lanes = slice((2 * t + h) * 128, (2 * t + h + 1) * 128)
            out[t, 32 + 64 * h : 96 + 64 * h, :] = (w[:, lanes].astype(F32) * scale).astype(BF)
    for g in range(8):
        keys = w[:, 8192 + g * 128 : 8320 + g * 128]
        values = w[:, 9216 + g * 128 : 9344 + g * 128]
        both = (jnp.concatenate([keys, values], 1).astype(F32) * scale).astype(BF)
        packed = dot(both[:32], sel[0]) + dot(both[32:], sel[1])
        for i in range(4):
            out[4 * g + i, :32, :] = packed[:, i * 128 : (i + 1) * 128].astype(BF)


def pack(idx, w_qkv, gain, sel, after):
    return call(
        pack_body,
        "pack_weights",
        [SM, VM, VM, VM, AN],
        shape((32, 160, 128)),
        VM,
        cost(1 << 26, 3),
    )(idx, w_qkv, gain, sel, after)


def cut_body(lo, hi, src, *refs):
    refs[-1][...] = src[:, lo:hi, :]


def cut(lo, hi, src, after, name):
    return call(
        functools.partial(cut_body, lo, hi),
        name,
        [VM] + [AN] * len(after),
        shape((32, hi - lo, 128)),
        VM,
        cost(0, 1),
    )(src, *after)


def norm_body(x, out):
    def step(i, _):
        rows = pl.ds(pl.multiple_of(i * 128, 128), 128)
        square = jnp.zeros((128, 128), F32)
        for c in range(64):
            piece = x[rows, c * 128 : (c + 1) * 128].astype(F32)
            square += piece * piece
        mean = jnp.sum(square, axis=1, keepdims=True) * (1.0 / D)
        out[rows, :] = jnp.broadcast_to(lax.rsqrt(mean + 1e-6), (128, 128))
        return 0

    lax.fori_loop(0, 8, step, 0)


def norms(x):
    return call(
        norm_body, "token_norms", [VM], shape((1024, 128), F32), VM, cost(1 << 25, 16)
    )(x)


def kv_body(idx, x, own, mate, side, far, norm, unpack, bias, bsel, cos, sin, kv, ws):
    acc = None
    pieces = (own[:, :32, :], mate[:, :32, :], side[...], far[...])
    for j, w in enumerate(pieces):
        both = dot(w.reshape(1024, 128), unpack[...]).astype(BF)
        ws[:, :32, :] = both[:, :128].reshape(32, 32, 128)
        ws[:, 32:, :] = both[:, 128:].reshape(32, 32, 128)
        start = pl.multiple_of(idx[j] * 2048, 2048)
        part = dot(x[:, pl.ds(start, 2048)], ws[...].reshape(2048, 128))
        acc = part if acc is None else acc + part
    g = idx[5]
    base = jnp.concatenate([bias[pl.ds(64 + g, 1), :], bias[pl.ds(72 + g, 1), :]], 1)
    base = dot(jnp.broadcast_to(base, (8, 256)).astype(BF), bsel[idx[6]])[0:1]
    cosine = cos[idx[6]]
    sine = sin[idx[6]]
    acc = acc * norm[...] + base
    lane = lax.broadcasted_iota(jnp.int32, (SPAN, 128), 1)
    for i in range(2):
        a = acc[i * 256 : (i + 1) * 256]
        b = acc[512 + i * 256 : 512 + (i + 1) * 256]
        left = a * cosine + pltpu.roll(a, 64, 1) * sine
        right = pltpu.roll(b, 64, 1) * cosine + b * sine
        kv[i * 256 : (i + 1) * 256] = jnp.where(lane < 64, left, right).astype(BF)


def keys_values(idx, x, ws, norm, tab, bias):
    return call(
        kv_body,
        "keys_values",
        [SM] + [VM] * 11,
        shape((512, 128)),
        VM,
        cost(2 * 1024 * 8192 * 256, 2),
        [pltpu.VMEM((32, 64, 128), BF)],
    )(
        idx, x, *ws, norm, tab["unpack"], bias, tab["bias_sel"], tab["k_cos"], tab["k_sin"]
    )


def join_body(idx, p0, p1, p2, p3, gather, keys, values):
    for half in range(2):
        kv = jnp.zeros((512, 256), F32)
        for r, piece in enumerate((p0, p1, p2, p3)):
            kv += dot(piece[...], gather[(idx[6] + 4 - r) % 4, half])
        keys[half * 512 : (half + 1) * 512] = kv[:, :128].astype(BF)
        values[half * 512 : (half + 1) * 512] = kv[:, 128:].astype(BF)


def join_kv(idx, pieces, tab):
    return call(
        join_body,
        "join_keys_values",
        [SM] + [VM] * 5,
        [shape((1024, 128))] * 2,
        [VM] * 2,
        cost(1 << 28, 1),
    )(idx, *pieces, tab["gather"])


def head_body(h, idx, x, own, mate, side, far, norm, bias, cos, sin, keys, values, att):
    lanes = slice(32 + 64 * h, 96 + 64 * h)
    acc = None
    for j, w in enumerate((own[:, lanes, :], mate[:, lanes, :], side[...], far[...])):
        start = pl.multiple_of(idx[j] * 2048, 2048)
        part = dot(x[:, pl.ds(start, 2048)], w.reshape(2048, 128))
        acc = part if acc is None else acc + part
    acc = acc * norm[...] + bias[pl.ds(2 * idx[4] + h, 1), :]
    row = lax.broadcasted_iota(jnp.int32, (SPAN, SPAN), 0)
    col = lax.broadcasted_iota(jnp.int32, (SPAN, SPAN), 1)
    ones = jnp.ones((SPAN, HD), BF)
    for seq in range(4):
        rows = slice(seq * SPAN, (seq + 1) * SPAN)
        query = acc[rows]
        query = (query * cos[...] + pltpu.roll(query, 64, 1) * sin[...]).astype(BF)
        scores = lax.dot_general(
            query, keys[rows], (((1,), (1,)), ((), ())), preferred_element_type=F32
        ) * (HD**-0.5)
        scores = jnp.where(row >= col, scores, -1e30)
        expo = jnp.exp(scores - jnp.max(scores, axis=1, keepdims=True)).astype(BF)
        mixed = dot(expo, jnp.concatenate([values[rows], ones], 1))
        att[rows] = (mixed[:, :HD] / mixed[:, HD:]).astype(BF)


def head(h, idx, x, ws, norm, tab, bias, keys, values):
    return call(
        functools.partial(head_body, h),
        f"query_head_{h}",
        [SM] + [VM] * 11,
        shape((1024, 128)),
        VM,
        cost(2 * 1024 * 8192 * 256, 2, 1 << 18),
    )(idx, x, *ws, norm, bias, tab["q_cos"], tab["q_sin"], keys, values)


def beside_body(idx, att, across, out):
    same = idx[8] == idx[7]
    out[:, :128] = jnp.where(same, att[...], across[...])
    out[:, 128:] = jnp.where(same, across[...], att[...])


def beside(idx, att, across, name):
    return call(
        beside_body, name, [SM, VM, VM], shape((1024, 256)), VM, cost(0, 1)
    )(idx, att, across)


def route_body(idx, keep, recv, keep_s, recv_s, *outs):
    for r, out in enumerate(outs):
        goal = (idx[9] + r) % 4
        same_pair = goal // 2 == idx[7]
        same_side = goal % 2 == idx[10]
        for ref, hit in (
            (keep, same_pair & same_side),
            (recv, jnp.logical_not(same_pair) & same_side),
            (keep_s, same_pair & jnp.logical_not(same_side)),
            (recv_s, jnp.logical_not(same_pair) & jnp.logical_not(same_side)),
        ):

            @pl.when(hit)
            def _():
                out[...] = ref[...]


def route(idx, blocks):
    return call(
        route_body,
        "route_rows",
        [SM] + [VM] * 4,
        [shape((1024, 256))] * 4,
        [VM] * 4,
        cost(0, 4),
    )(idx, *blocks)


def pick_body(idx, w, keep, send):
    p = idx[7]
    keep[...] = w[pl.ds(pl.multiple_of(p * 1024, 1024), 1024), :]
    send[...] = w[pl.ds(pl.multiple_of((1 - p) * 1024, 1024), 1024), :]


def pick(idx, w):
    return call(
        pick_body, "pick_rows", [SM, VM], [shape((1024, 256))] * 2, [VM] * 2, cost(0, 2)
    )(idx, w)


def out_body(idx, *refs):
    atts = refs[:8]
    own = refs[8:12]
    other = refs[12:16]
    outs = refs[16:]
    for r in range(4):
        acc = None
        for xr in range(4):
            part = (idx[6] + 4 - xr) % 4
            for h in range(2):
                rows = pl.ds(pl.multiple_of(part * 256 + h * 128, 128), 128)
                w = jnp.concatenate([own[r][rows, :], other[r][rows, :]], 0)
                term = dot(atts[h * 4 + xr][...], w)
                acc = term if acc is None else acc + term
        outs[r][...] = acc.astype(BF)


def project_out(idx, atts, own, other):
    return call(
        out_body,
        "project_out",
        [SM] + [VM] * 16,
        [shape((1024, 256))] * 4,
        [VM] * 4,
        cost(2 * 1024 * 2048 * 1024, 4),
    )(idx, *atts, *own, *other)


def finish_body(idx, x, p0, p1, p2, p3, out):
    total = x[:, pl.ds(pl.multiple_of(idx[4] * 256, 256), 256)].astype(F32)
    for part in (p0, p1, p2, p3):
        total += part[...].astype(F32)
    out[...] = total.astype(BF)


def finish(idx, x, parts):
    return call(
        finish_body, "add_residual", [SM] + [VM] * 5, shape((1024, 256)), VM, cost(1 << 20, 3)
    )(idx, x, *parts)


SWAP = [(0, 1), (1, 0)]


def shift(dz, dy, dx):
    return [
        (
            z * 8 + y * 4 + x,
            (z + dz) % 4 * 8 + (y + dy) % 2 * 4 + (x + dx) % 4,
        )
        for z in range(4)
        for y in range(2)
        for x in range(4)
    ]


def shards(tokens, norm_gain, w_qkv, qkv_bias, w_out):
    tab = tables()
    seqs, span, width = tokens.shape
    p = lax.axis_index("pair")
    s = lax.axis_index("side")
    t = lax.axis_index("tp")
    z, yh, xi = t // 8, t // 4 % 2, t % 4
    idx = jnp.stack(
        [
            2 * p + s,
            2 * (1 - p) + s,
            2 * p + 1 - s,
            2 * (1 - p) + 1 - s,
            t,
            t // 4,
            xi,
            p,
            yh,
            z,
            s,
        ]
    ).astype(jnp.int32)
    x = tokens.reshape(seqs * span, width)
    bias = qkv_bias.reshape(80, 128).astype(F32)

    keep, send = pick(idx, w_out)
    recv = lax.ppermute(send, "pair", SWAP)
    keep_s = lax.ppermute(keep, "side", SWAP)
    recv_s = lax.ppermute(recv, "side", SWAP)

    packed = pack(idx, w_qkv, norm_gain.reshape(64, 128), tab["pack"], recv)
    own = lax.all_to_all(packed, "tp", split_axis=0, concat_axis=0, tiled=True)
    mate = lax.ppermute(own, "pair", SWAP)
    sides, fars = [], []

    def across(lo, hi, after, name):
        side = lax.ppermute(cut(lo, hi, own, after, name), "side", SWAP)
        fars.append(lax.ppermute(side, "pair", SWAP))
        sides.append(side)

    across(0, 32, [keep_s, recv_s], "cut_kv")
    routed = route(idx, (keep, recv, keep_s, recv_s))
    across(32, 96, [sides[0]], "cut_0")
    across(96, 160, [sides[1]], "cut_1")
    w_own = [routed[0]] + [
        lax.ppermute(routed[r], "tp", shift(r, 0, 0)) for r in range(1, 4)
    ]
    w_other = [lax.ppermute(w, "pair", SWAP) for w in w_own]

    norm = norms(x)
    kv_piece = keys_values(idx, x, (own, mate, sides[0], fars[0]), norm, tab, bias)
    pieces = [kv_piece] + [
        lax.ppermute(kv_piece, "tp", shift(0, 0, r)) for r in range(1, 4)
    ]
    keys, values = join_kv(idx, pieces, tab)

    atts = []
    for h in range(2):
        ws = (own, mate, sides[1 + h], fars[1 + h])
        att = head(h, idx, x, ws, norm, tab, bias, keys, values)
        both = beside(idx, att, lax.ppermute(att, "tp", shift(0, 1, 0)), f"beside_{h}")
        atts += [both] + [
            lax.ppermute(both, "tp", shift(0, 0, r)) for r in range(1, 4)
        ]

    partial = project_out(idx, atts, w_own, w_other)
    parts = [partial[0]] + [
        lax.ppermute(partial[r], "tp", shift(-r, 0, 0)) for r in range(1, 4)
    ]
    return finish(idx, x, parts).reshape(seqs, span, 256)


def solution(mesh):
    placed = (
        P(("pair", "side"), None, None),
        P(),
        P(("pair", "side", "tp"), None),
        P(),
        P(("pair", "side"), "tp"),
    )
    return jax.shard_map(
        shards,
        mesh=mesh,
        in_specs=placed,
        out_specs=P(("pair", "side"), None, "tp"),
        check_vma=False,
    )
```

time: 577 us -> 223 us (0.39)
  waiting for transfers between devices: 422 us -> 126 us
  other arithmetic: 45.9 us -> 0.01 us
  blocking collectives: 42.6 us -> 0 us
  Pallas kernels: 0 us -> 40.3 us
  starting transfers between devices: 10.5 us -> 44.2 us
  matrix products: 29 us -> 0 us
  between operations: 13.3 us -> 0.26 us
    reduce_scatter x1 -> x0, waiting for transfers between devices: 213 us -> none  [shards(): lax.psum_scatter(partial_sums.astype(jnp.bfloat16), 'tp', scatter_dimensi...]
    all_gather x2 -> x0, waiting for transfers between devices: 173 us -> none  [the longest x1 115 us: shards(): lax.all_gather(own_cols, ('pair', 'side'), axis=0, tiled=True)]
    ppermute x0 -> x31, waiting for transfers between devices: none -> 107 us  [the longest x6 40.6 us: shards(): lax.ppermute(both, 'tp', shift(0, 0, r))]
    all_to_all x1 -> x0, blocking collectives: 42.6 us -> none  [shards(): lax.all_to_all(bundle, 'tp', split_axis=1, concat_axis=0, tiled=True)]
    pallas_call x0 -> x15, Pallas kernels: none -> 40.3 us  [the longest x2 12.8 us: head(): call(functools.partial(head_body, h), f'query_head_{h}', [SM] + [VM] * 11...]
    convert_element_type x5 -> x1, other arithmetic: 36.1 us -> 0.01 us  [shards(): bias = qkv_bias.reshape(80, 128).astype(F32)]
    ppermute x0 -> x31, starting transfers between devices: none -> 33.3 us  [the longest x3 7.17 us: shards(): lax.ppermute(kv_piece, 'tp', shift(0, 0, r))]
    dot_general x3 -> x0, matrix products: 26.6 us -> none  [the longest x1 14.3 us: shards(): jnp.dot(flat_rows, lax.all_gather(own_cols, ('pair', 'side'), axis=0, til...]
  transfers between devices with their start and end apart: 4 -> 32, of which waited for: 4 -> 16; matrix products, arithmetic and copies ran while one was open for 9% -> 0% of each run, Pallas kernels for 0% -> 14%
where the time goes in v2:
time: 223 us; the launch traced here: 221 us
  waiting for transfers between devices  126 us (57%)
  starting transfers between devices  44.2 us (20%)
  Pallas kernels  40.3 us (18%)
  local copies, waits for them, and re-layouts  10.8 us (5%)
    ppermute x6, waiting for transfers between devices, shards(): lax.ppermute(both, 'tp', shift(0, 0, r))  40.6 us
    ppermute x3, waiting for transfers between devices, shards(): lax.ppermute(partial[r], 'tp', shift(-r, 0, 0))  22.9 us
    all_to_all x1, waiting for transfers between devices, shards(): own = lax.all_to_all(packed, 'tp', split_axis=0, concat_axis=0, tiled=True)  19.1 us
    ppermute x3, waiting for transfers between devices, across(): side = lax.ppermute(cut(lo, hi, own, after, name), 'side', SWAP)  17 us
    pallas_call x2, Pallas kernels, head(): call(functools.partial(head_body, h), f'query_head_{h}', [SM] + [VM] * 11...  12.8 us
    all_to_all x1, starting transfers between devices, shards(): own = lax.all_to_all(packed, 'tp', split_axis=0, concat_axis=0, tiled=True)  10.9 us
    unnamed x28, local copies, waits for them, and re-layouts  10.7 us
    ppermute x1, waiting for transfers between devices, shards(): recv_s = lax.ppermute(recv, 'side', SWAP)  10.4 us
  transfers between devices with their start and end apart: 32, of which 16 were waited for; matrix products, arithmetic and copies ran while one was open for 0% of the time, Pallas kernels for 14%

profile of v2, /device:TPU:0, one launch (start us, length us, event | category | flops | bytes accessed | tf_op | source)
XLA Modules:
  0.0 221.5 jit_solution(188347164348553608)
XLA Ops:
  0.0 0.1 stack.47.idx
  0.1 1.2 copy-done.3
  1.3 0.6 pick_rows.1
  1.9 0.1 collective-permute-start
  2.0 1.9 collective-permute-done.after.recv
  3.9 1.3 copy-done.2
  5.3 0.8 copy-done.12
  6.0 2.7 %pack_weights.1 = bf16[32,160,128]{2,1,0:T(8,128)(2,1)} custom-call(s32[11]{0:T(128)S(1)} %stack.47.idx, bf16[64,10240]{1,0:T(8,128)(2,1)S(1)} %copy-done.2, f32[64,128]{1,0:T(8,128)S(1)} %bitcast.22, bf16[2,256,512]{2,1,0:T(8,128)(2,1)S(1)} %copy-done.9, bf16[1024,256]{1,0:T(8,128)(2,1)S(1)} %collective-permute-done.after.recv), custom_call_target="tpu_custom_call" | custom-call | flops 67108864 | bytes 3145728 | tf_op jit(solution)/shard_map/pack_weights/pallas_call | solution.py:133
  8.7 10.9 %all-to-all-start = ((bf16[32,160,128]{2,1,0:T(8,128)(2,1)}), bf16[32,160,128]{2,1,0:T(8,128)(2,1)S(1)}, u32[]{:S(2)}, u32[]{:S(2)}) async-start(bf16[32,160,128]{2,1,0:T(8,128)(2,1)} %pack_weights.1), calls=%async_computation | async-start | bytes 2621440 | tf_op jit(solution)/shard_map/all_to_all | solution.py:411
  19.6 0.8 collective-permute-start.2
  20.3 1.3 collective-permute-start.3
  21.7 19.1 %all-to-all-done.src.own = bf16[32,160,128]{2,1,0:T(8,128)(2,1)S(1)} async-done(((bf16[32,160,128]{2,1,0:T(8,128)(2,1)}), bf16[32,160,128]{2,1,0:T(8,128)(2,1)S(1)}, u32[]{:S(2)}, u32[]{:S(2)}) %all-to-all-start) | async-done | bytes 1310752 | tf_op jit(solution)/shard_map/all_to_all | solution.py:411
  40.7 6.3 %collective-permute-done.2.refs_0_.keep_s = bf16[1024,256]{1,0:T(8,128)(2,1)S(1)} collective-permute-done((bf16[1024,256]{1,0:T(8,128)(2,1)S(1)}, bf16[1024,256]{1,0:T(8,128)(2,1)S(1)}, u32[]{:S(2)}, u32[]{:S(2)}) %collective-permute-start.2) | collective-permute-done | bytes 524320 | tf_op jit(solution)/shard_map/ppermute | solution.py:407
  47.1 10.4 %collective-permute-done.3.refs_1_.recv_s = bf16[1024,256]{1,0:T(8,128)(2,1)S(1)} collective-permute-done((bf16[1024,256]{1,0:T(8,128)(2,1)S(1)}, bf16[1024,256]{1,0:T(8,128)(2,1)S(1)}, u32[]{:S(2)}, u32[]{:S(2)}) %collective-permute-start.3) | collective-permute-done | bytes 524320 | tf_op jit(solution)/shard_map/ppermute | solution.py:408
  57.5 1.4 collective-permute-start.4
  59.0 6.2 %collective-permute-done.4.refs_0_.side = bf16[32,32,128]{2,1,0:T(8,128)(2,1)S(1)} collective-permute-done((bf16[32,32,128]{2,1,0:T(8,128)(2,1)S(1)}, bf16[32,32,128]{2,1,0:T(8,128)(2,1)S(1)}, u32[]{:S(2)}, u32[]{:S(2)}) %collective-permute-start.4) | collective-permute-done | bytes 262176 | tf_op jit(solution)/shard_map/ppermute | solution.py:416
  65.2 0.0 copy-start.13
  65.2 1.4 collective-permute-start.5
  66.6 10.9 %collective-permute-done.5.side.refs_0_ = bf16[32,64,128]{2,1,0:T(8,128)(2,1)S(1)} collective-permute-done((bf16[32,64,128]{2,1,0:T(8,128)(2,1)S(1)}, bf16[32,64,128]{2,1,0:T(8,128)(2,1)S(1)}, u32[]{:S(2)}, u32[]{:S(2)}) %collective-permute-start.5) | collective-permute-done | bytes 524320 | tf_op jit(solution)/shard_map/ppermute | solution.py:416
  77.5 1.4 collective-permute-start.15
  78.9 5.8 %copy-done = bf16[4,256,8192]{2,1,0:T(8,128)(2,1)S(1)} copy-done((bf16[4,256,8192]{2,1,0:T(8,128)(2,1)S(1)}, bf16[4,256,8192]{2,1,0:T(8,128)(2,1)}, u32[]{:S(2)}) %copy-start) | copy-done | bytes 16777240
  84.7 4.1 %token_norms.1.norm = f32[1024,128]{1,0:T(8,128)S(1)} custom-call(bf16[1024,8192]{1,0:T(8,128)(2,1)S(1)} %bitcast.17), custom_call_target="tpu_custom_call" | custom-call | flops 33554432 | bytes 16777216 | tf_op jit(solution)/shard_map/token_norms/pallas_call | solution.py:173
  88.8 0.1 collective-permute-start.6
  89.0 1.5 copy-done.1
  90.5 0.0 copy-done.6
  90.5 9.9 %keys_values.1.p0 = bf16[512,128]{1,0:T(8,128)(2,1)S(1)} custom-call(s32[11]{0:T(128)S(1)} %stack.47.idx, bf16[1024,8192]{1,0:T(8,128)(2,1)S(1)} %bitcast.18, bf16[32,160,128]{2,1,0:T(8,128)(2,1)S(1)} %all-to-all-done.src.own, bf16[32,160,128]{2,1,0:T(8,128)(2,1)S(1)} %collective-permute-done.1.mate, ...), custom_call_target="tpu_custom_call" | custom-call | flops 4294967296 | bytes 2097152 | tf_op jit(solution)/shard_map/keys_values/pallas_call | solution.py:204
  100.4 0.0 copy-start.8
  100.4 0.0 copy-start.4
  100.4 0.0 copy-start.5
  100.5 3.1 %collective-permute-start.10 = (bf16[512,128]{1,0:T(8,128)(2,1)S(1)}, bf16[512,128]{1,0:T(8,128)(2,1)S(1)}, u32[]{:S(2)}, u32[]{:S(2)}) collective-permute-start(bf16[512,128]{1,0:T(8,128)(2,1)S(1)} %keys_values.1.p0), channel_id=1, source_target_pairs={{0,3},{1,0},{2,1},{3,2},{4,7},{5,4},{6,5},{7,6},{8,11},{9,8},{10,9... | collective-permute-start | bytes 393224 | tf_op jit(solution)/shard_map/ppermute | solution.py:432
  103.5 4.1 %collective-permute-start.9 = (bf16[512,128]{1,0:T(8,128)(2,1)S(1)}, bf16[512,128]{1,0:T(8,128)(2,1)S(1)}, u32[]{:S(2)}, u32[]{:S(2)}) collective-permute-start(bf16[512,128]{1,0:T(8,128)(2,1)S(1)} %keys_values.1.p0), channel_id=1, source_target_pairs={{0,2},{1,3},{2,0},{3,1},{4,6},{5,7},{6,4},{7,5},{8,10},{9,11},{10,... | collective-permute-start | bytes 393224 | tf_op jit(solution)/shard_map/ppermute | solution.py:432
  107.6 0.8 route_rows.1
  108.4 1.3 collective-permute-start.21
  109.8 1.3 collective-permute-done.8.p1
  111.1 3.0 %collective-permute-start.22 = (bf16[1024,256]{1,0:T(8,128)(2,1)S(1)}, bf16[1024,256]{1,0:T(8,128)(2,1)S(1)}, u32[]{:S(2)}, u32[]{:S(2)}) collective-permute-start(bf16[1024,256]{1,0:T(8,128)(2,1)S(1)} %get-tuple-element.23), channel_id=1, source_target_pairs={{0,16},{1,17},{2,18},{3,19},{4,20},{5,21},{6,22},{7,23},{8,24},{9,... | collective-permute-start | bytes 1572872 | tf_op jit(solution)/shard_map/ppermute | solution.py:425
  114.0 1.0 collective-permute-start.23
  115.0 1.2 join_keys_values.1
  116.3 6.4 %query_head_0.1.att = bf16[1024,128]{1,0:T(8,128)(2,1)S(1)} custom-call(s32[11]{0:T(128)S(1)} %stack.47.idx, bf16[1024,8192]{1,0:T(8,128)(2,1)S(1)} %bitcast.19, bf16[32,160,128]{2,1,0:T(8,128)(2,1)S(1)} %all-to-all-done.src.own, bf16[32,160,128]{2,1,0:T(8,128)(2,1)S(1)} %collective-permute-done.1.mate, ...), custom_call_target="tpu_custom_call" | custom-call | flops 4294967296 | bytes 2097152 | tf_op jit(solution)/shard_map/query_head_0/pallas_call | solution.py:262
  122.7 2.7 %collective-permute-start.11 = (bf16[1024,128]{1,0:T(8,128)(2,1)S(1)}, bf16[1024,128]{1,0:T(8,128)(2,1)S(1)}, u32[]{:S(2)}, u32[]{:S(2)}) collective-permute-start(bf16[1024,128]{1,0:T(8,128)(2,1)S(1)} %query_head_0.1.att), channel_id=1, source_target_pairs={{0,4},{1,5},{2,6},{3,7},{4,0},{5,1},{6,2},{7,3},{8,12},{9,13},{10,... | collective-permute-start | bytes 786440 | tf_op jit(solution)/shard_map/ppermute | solution.py:440
  125.4 6.4 %query_head_1.1.att = bf16[1024,128]{1,0:T(8,128)(2,1)S(1)} custom-call(s32[11]{0:T(128)S(1)} %stack.47.idx, bf16[1024,8192]{1,0:T(8,128)(2,1)S(1)} %bitcast.20, bf16[32,160,128]{2,1,0:T(8,128)(2,1)S(1)} %all-to-all-done.src.own, bf16[32,160,128]{2,1,0:T(8,128)(2,1)S(1)} %collective-permute-done.1.mate, ...), custom_call_target="tpu_custom_call" | custom-call | flops 4294967296 | bytes 2097152 | tf_op jit(solution)/shard_map/query_head_1/pallas_call | solution.py:262
  131.8 1.0 collective-permute-start.17
  132.8 3.2 %collective-permute-done.22.refs_10_ = bf16[1024,256]{1,0:T(8,128)(2,1)S(1)} collective-permute-done((bf16[1024,256]{1,0:T(8,128)(2,1)S(1)}, bf16[1024,256]{1,0:T(8,128)(2,1)S(1)}, u32[]{:S(2)}, u32[]{:S(2)}) %collective-permute-start.22) | collective-permute-done | bytes 524320 | tf_op jit(solution)/shard_map/ppermute | solution.py:425
  136.0 0.5 collective-permute-start.26
  136.5 0.1 collective-permute-start.27
  136.6 0.7 beside_0.1.refs_0_
  137.3 3.2 %collective-permute-done.17.across = bf16[1024,128]{1,0:T(8,128)(2,1)S(1)} collective-permute-done((bf16[1024,128]{1,0:T(8,128)(2,1)S(1)}, bf16[1024,128]{1,0:T(8,128)(2,1)S(1)}, u32[]{:S(2)}, u32[]{:S(2)}) %collective-permute-start.17) | collective-permute-done | bytes 262176 | tf_op jit(solution)/shard_map/ppermute | solution.py:440
  140.5 0.2 collective-permute-start.12
  140.7 0.7 beside_1.1.refs_4_
  141.4 2.9 %collective-permute-start.13 = (bf16[1024,256]{1,0:T(8,128)(2,1)S(1)}, bf16[1024,256]{1,0:T(8,128)(2,1)S(1)}, u32[]{:S(2)}, u32[]{:S(2)}) collective-permute-start(bf16[1024,256]{1,0:T(8,128)(2,1)S(1)} %beside_0.1.refs_0_), channel_id=1, source_target_pairs={{0,2},{1,3},{2,0},{3,1},{4,6},{5,7},{6,4},{7,5},{8,10},{9,11},{10,... | collective-permute-start | bytes 1572872 | tf_op jit(solution)/shard_map/ppermute | solution.py:442
  144.3 2.1 collective-permute-start.14
  146.4 1.5 collective-permute-start.19
  148.0 19.8 %collective-permute-done.12.refs_1_ = bf16[1024,256]{1,0:T(8,128)(2,1)S(1)} collective-permute-done((bf16[1024,256]{1,0:T(8,128)(2,1)S(1)}, bf16[1024,256]{1,0:T(8,128)(2,1)S(1)}, u32[]{:S(2)}, u32[]{:S(2)}) %collective-permute-start.12) | collective-permute-done | bytes 524320 | tf_op jit(solution)/shard_map/ppermute | solution.py:442
  167.8 0.0 collective-permute-start.20
  167.8 1.6 collective-permute-done.14.refs_3_
  169.4 17.7 %collective-permute-done.18.refs_5_ = bf16[1024,256]{1,0:T(8,128)(2,1)S(1)} collective-permute-done((bf16[1024,256]{1,0:T(8,128)(2,1)S(1)}, bf16[1024,256]{1,0:T(8,128)(2,1)S(1)}, u32[]{:S(2)}, u32[]{:S(2)}) %collective-permute-start.18) | collective-permute-done | bytes 524320 | tf_op jit(solution)/shard_map/ppermute | solution.py:442
  187.2 1.4 collective-permute-done.20.refs_7_
  188.6 5.0 %project_out.1 = (bf16[1024,256]{1,0:T(8,128)(2,1)S(1)}, bf16[1024,256]{1,0:T(8,128)(2,1)S(1)}, bf16[1024,256]{1,0:T(8,128)(2,1)S(1)}, bf16[1024,256]{1,0:T(8,128)(2,1)S(1)}) custom-call(s32[11]{0:T(128)S(1)} %stack.47.idx, bf16[1024,256]{1,0:T(8,128)(2,1)S(1)} %beside_0.1.refs_0_, bf16[1024,256]{1,0:T(8,128)(2,1)S(1)} %collective-permute-done.12.refs_1_, ...), custom_call_target="tpu_custom_call" | custom-call | flops 4294967296 | bytes 4194304 | tf_op jit(solution)/shard_map/project_out/pallas_call | solution.py:342
  193.6 1.5 collective-permute-start.28
  195.1 1.1 collective-permute-start.29
  196.3 0.7 collective-permute-start.30
  196.9 11.7 %collective-permute-done.28.p1 = bf16[1024,256]{1,0:T(8,128)(2,1)S(1)} collective-permute-done((bf16[1024,256]{1,0:T(8,128)(2,1)S(1)}, bf16[1024,256]{1,0:T(8,128)(2,1)S(1)}, u32[]{:S(2)}, u32[]{:S(2)}) %collective-permute-start.28) | collective-permute-done | bytes 524320 | tf_op jit(solution)/shard_map/ppermute | solution.py:447
  208.6 2.9 %collective-permute-done.29.p2 = bf16[1024,256]{1,0:T(8,128)(2,1)S(1)} collective-permute-done((bf16[1024,256]{1,0:T(8,128)(2,1)S(1)}, bf16[1024,256]{1,0:T(8,128)(2,1)S(1)}, u32[]{:S(2)}, u32[]{:S(2)}) %collective-permute-start.29) | collective-permute-done | bytes 524320 | tf_op jit(solution)/shard_map/ppermute | solution.py:447
  211.5 8.3 %collective-permute-done.30.p3 = bf16[1024,256]{1,0:T(8,128)(2,1)S(1)} collective-permute-done((bf16[1024,256]{1,0:T(8,128)(2,1)S(1)}, bf16[1024,256]{1,0:T(8,128)(2,1)S(1)}, u32[]{:S(2)}, u32[]{:S(2)}) %collective-permute-start.30) | collective-permute-done | bytes 524320 | tf_op jit(solution)/shard_map/ppermute | solution.py:447
  219.8 1.7 add_residual.1
  (45 shorter events, 0.2 us)
Async XLA Ops:
  0.1 1.2 copy-start.3
  1.3 2.6 %copy-start.9 = (bf16[2,256,512]{2,1,0:T(8,128)(2,1)S(1)}, bf16[2,256,512]{2,1,0:T(8,128)(2,1)}, u32[]{:S(2)}) copy-start(bf16[2,256,512]{2,1,0:T(8,128)(2,1)} %constant.76.clone.sel) | copy-start | bytes 1572868
  1.9 2.0 collective-permute-start
  3.9 1.3 copy-start.2
  5.2 0.8 copy-start.12
  8.7 32.1 %all-to-all-start = ((bf16[32,160,128]{2,1,0:T(8,128)(2,1)}), bf16[32,160,128]{2,1,0:T(8,128)(2,1)S(1)}, u32[]{:S(2)}, u32[]{:S(2)}) async-start(bf16[32,160,128]{2,1,0:T(8,128)(2,1)} %pack_weights.1), calls=%async_computation | async-start | bytes 2621440 | tf_op jit(solution)/shard_map/all_to_all | solution.py:411
  19.6 27.5 %collective-permute-start.2 = (bf16[1024,256]{1,0:T(8,128)(2,1)S(1)}, bf16[1024,256]{1,0:T(8,128)(2,1)S(1)}, u32[]{:S(2)}, u32[]{:S(2)}) collective-permute-start(bf16[1024,256]{1,0:T(8,128)(2,1)S(1)} %get-tuple-element.18.keep), channel_id=1, source_target_pairs={{0,32},{32,0},{1,33},{33,1},{2,34},{34,2},{3,35},{35,3},{4,36},{36... | collective-permute-start | bytes 1572872 | tf_op jit(solution)/shard_map/ppermute | solution.py:407
  20.3 37.2 %collective-permute-start.3 = (bf16[1024,256]{1,0:T(8,128)(2,1)S(1)}, bf16[1024,256]{1,0:T(8,128)(2,1)S(1)}, u32[]{:S(2)}, u32[]{:S(2)}) collective-permute-start(bf16[1024,256]{1,0:T(8,128)(2,1)S(1)} %collective-permute-done.after.recv), channel_id=1, source_target_pairs={{0,32},{32,0},{1,33},{33,1},{2,34},{34,2},{3,35},{35,3},{4,36},{36... | collective-permute-start | bytes 1572872 | tf_op jit(solution)/shard_map/ppermute | solution.py:408
  40.7 48.2 %collective-permute-start.1 = (bf16[32,160,128]{2,1,0:T(8,128)(2,1)S(1)}, bf16[32,160,128]{2,1,0:T(8,128)(2,1)S(1)}, u32[]{:S(2)}, u32[]{:S(2)}) collective-permute-start(bf16[32,160,128]{2,1,0:T(8,128)(2,1)S(1)} %all-to-all-done.src.own), channel_id=1, source_target_pairs={{0,64},{64,0},{1,65},{65,1},{2,66},{66,2},{3,67},{67,3},{4,68},{68... | collective-permute-start | bytes 3932168 | tf_op jit(solution)/shard_map/ppermute | solution.py:412
  57.5 7.6 %collective-permute-start.4 = (bf16[32,32,128]{2,1,0:T(8,128)(2,1)S(1)}, bf16[32,32,128]{2,1,0:T(8,128)(2,1)S(1)}, u32[]{:S(2)}, u32[]{:S(2)}) collective-permute-start(bf16[32,32,128]{2,1,0:T(8,128)(2,1)S(1)} %cut_kv.1), channel_id=1, source_target_pairs={{0,32},{32,0},{1,33},{33,1},{2,34},{34,2},{3,35},{35,3},{4,36},{36... | collective-permute-start | bytes 786440 | tf_op jit(solution)/shard_map/ppermute | solution.py:416
  65.2 13.8 %copy-start.13 = (bf16[10240]{0:T(1024)(128)(2,1)S(1)}, bf16[10240]{0:T(1024)(128)(2,1)}, u32[]{:S(2)}) copy-start(bf16[10240]{0:T(1024)(128)(2,1)} %param.16) | copy-start | bytes 61444
  65.2 12.3 %collective-permute-start.5 = (bf16[32,64,128]{2,1,0:T(8,128)(2,1)S(1)}, bf16[32,64,128]{2,1,0:T(8,128)(2,1)S(1)}, u32[]{:S(2)}, u32[]{:S(2)}) collective-permute-start(bf16[32,64,128]{2,1,0:T(8,128)(2,1)S(1)} %cut_0.1), channel_id=1, source_target_pairs={{0,32},{32,0},{1,33},{33,1},{2,34},{34,2},{3,35},{35,3},{4,36},{36... | collective-permute-start | bytes 1572872 | tf_op jit(solution)/shard_map/ppermute | solution.py:416
  66.6 22.3 %collective-permute-start.7 = (bf16[32,32,128]{2,1,0:T(8,128)(2,1)S(1)}, bf16[32,32,128]{2,1,0:T(8,128)(2,1)S(1)}, u32[]{:S(2)}, u32[]{:S(2)}) collective-permute-start(bf16[32,32,128]{2,1,0:T(8,128)(2,1)S(1)} %collective-permute-done.4.refs_0_.side), channel_id=1, source_target_pairs={{0,64},{64,0},{1,65},{65,1},{2,66},{66,2},{3,67},{67,3},{4,68},{68... | collective-permute-start | bytes 786440 | tf_op jit(solution)/shard_map/ppermute | solution.py:417
  77.5 11.5 %copy-start.7 = (f32[4,256,128]{2,1,0:T(8,128)S(1)}, f32[4,256,128]{2,1,0:T(8,128)}, u32[]{:S(2)}) copy-start(f32[4,256,128]{2,1,0:T(8,128)} %constant.81.clone.sin) | copy-start | bytes 1572868
  77.5 11.5 %copy-start.10 = (bf16[4,256,128]{2,1,0:T(8,128)(2,1)S(1)}, bf16[4,256,128]{2,1,0:T(8,128)(2,1)}, u32[]{:S(2)}) copy-start(bf16[4,256,128]{2,1,0:T(8,128)(2,1)} %constant.78.clone.bsel) | copy-start | bytes 786436
  77.5 11.5 %copy-start.11 = (bf16[128,256]{1,0:T(8,128)(2,1)S(1)}, bf16[128,256]{1,0:T(8,128)(2,1)}, u32[]{:S(2)}) copy-start(bf16[128,256]{1,0:T(8,128)(2,1)} %constant.79.clone.unpack) | copy-start | bytes 196612
  77.5 30.1 %collective-permute-start.15 = (bf16[32,64,128]{2,1,0:T(8,128)(2,1)S(1)}, bf16[32,64,128]{2,1,0:T(8,128)(2,1)S(1)}, u32[]{:S(2)}, u32[]{:S(2)}) collective-permute-start(bf16[32,64,128]{2,1,0:T(8,128)(2,1)S(1)} %cut_1.1), channel_id=1, source_target_pairs={{0,32},{32,0},{1,33},{33,1},{2,34},{34,2},{3,35},{35,3},{4,36},{36... | collective-permute-start | bytes 1572872 | tf_op jit(solution)/shard_map/ppermute | solution.py:416
  78.9 5.8 %copy-start = (bf16[4,256,8192]{2,1,0:T(8,128)(2,1)S(1)}, bf16[4,256,8192]{2,1,0:T(8,128)(2,1)}, u32[]{:S(2)}) copy-start(bf16[4,256,8192]{2,1,0:T(8,128)(2,1)} %param.13) | copy-start | bytes 50331652
  84.7 5.8 %copy-start.1 = (bf16[4,256,8192]{2,1,0:T(8,128)(2,1)S(1)}, bf16[4,256,8192]{2,1,0:T(8,128)(2,1)}, u32[]{:S(2)}) copy-start(bf16[4,256,8192]{2,1,0:T(8,128)(2,1)} %param.13) | copy-start | bytes 50331652
  84.7 5.8 %copy-start.6 = (f32[4,256,128]{2,1,0:T(8,128)S(1)}, f32[4,256,128]{2,1,0:T(8,128)}, u32[]{:S(2)}) copy-start(f32[4,256,128]{2,1,0:T(8,128)} %constant.80.clone.cos) | copy-start | bytes 1572868
  88.8 27.4 %collective-permute-start.6 = (bf16[32,64,128]{2,1,0:T(8,128)(2,1)S(1)}, bf16[32,64,128]{2,1,0:T(8,128)(2,1)S(1)}, u32[]{:S(2)}, u32[]{:S(2)}) collective-permute-start(bf16[32,64,128]{2,1,0:T(8,128)(2,1)S(1)} %collective-permute-done.5.side.refs_0_), channel_id=1, source_target_pairs={{0,64},{64,0},{1,65},{65,1},{2,66},{66,2},{3,67},{67,3},{4,68},{68... | collective-permute-start | bytes 1572872 | tf_op jit(solution)/shard_map/ppermute | solution.py:417
  100.4 14.6 %copy-start.8 = (bf16[4,2,128,256]{3,2,1,0:T(8,128)(2,1)S(1)}, bf16[4,2,128,256]{3,2,1,0:T(8,128)(2,1)}, u32[]{:S(2)}) copy-start(bf16[4,2,128,256]{3,2,1,0:T(8,128)(2,1)} %constant.77.clone.gather) | copy-start | bytes 1572868
  100.4 15.8 %copy-start.4 = (f32[256,128]{1,0:T(8,128)S(1)}, f32[256,128]{1,0:T(8,128)}, u32[]{:S(2)}) copy-start(f32[256,128]{1,0:T(8,128)} %constant.82.clone.cos) | copy-start | bytes 393220
  100.4 15.8 %copy-start.5 = (f32[256,128]{1,0:T(8,128)S(1)}, f32[256,128]{1,0:T(8,128)}, u32[]{:S(2)}) copy-start(f32[256,128]{1,0:T(8,128)} %constant.83.clone.sin) | copy-start | bytes 393220
  100.5 8.0 %collective-permute-start.10 = (bf16[512,128]{1,0:T(8,128)(2,1)S(1)}, bf16[512,128]{1,0:T(8,128)(2,1)S(1)}, u32[]{:S(2)}, u32[]{:S(2)}) collective-permute-start(bf16[512,128]{1,0:T(8,128)(2,1)S(1)} %keys_values.1.p0), channel_id=1, source_target_pairs={{0,3},{1,0},{2,1},{3,2},{4,7},{5,4},{6,5},{7,6},{8,11},{9,8},{10,9... | collective-permute-start | bytes 393224 | tf_op jit(solution)/shard_map/ppermute | solution.py:432
  103.5 7.5 %collective-permute-start.8 = (bf16[512,128]{1,0:T(8,128)(2,1)S(1)}, bf16[512,128]{1,0:T(8,128)(2,1)S(1)}, u32[]{:S(2)}, u32[]{:S(2)}) collective-permute-start(bf16[512,128]{1,0:T(8,128)(2,1)S(1)} %keys_values.1.p0), channel_id=1, source_target_pairs={{0,1},{1,2},{2,3},{3,0},{4,5},{5,6},{6,7},{7,4},{8,9},{9,10},{10,1... | collective-permute-start | bytes 393224 | tf_op jit(solution)/shard_map/ppermute | solution.py:432
  103.5 10.5 %collective-permute-start.9 = (bf16[512,128]{1,0:T(8,128)(2,1)S(1)}, bf16[512,128]{1,0:T(8,128)(2,1)S(1)}, u32[]{:S(2)}, u32[]{:S(2)}) collective-permute-start(bf16[512,128]{1,0:T(8,128)(2,1)S(1)} %keys_values.1.p0), channel_id=1, source_target_pairs={{0,2},{1,3},{2,0},{3,1},{4,6},{5,7},{6,4},{7,5},{8,10},{9,11},{10,... | collective-permute-start | bytes 393224 | tf_op jit(solution)/shard_map/ppermute | solution.py:432
  107.6 17.8 %collective-permute-start.16 = (bf16[32,64,128]{2,1,0:T(8,128)(2,1)S(1)}, bf16[32,64,128]{2,1,0:T(8,128)(2,1)S(1)}, u32[]{:S(2)}, u32[]{:S(2)}) collective-permute-start(bf16[32,64,128]{2,1,0:T(8,128)(2,1)S(1)} %collective-permute-done.15.side), channel_id=1, source_target_pairs={{0,64},{64,0},{1,65},{65,1},{2,66},{66,2},{3,67},{67,3},{4,68},{68... | collective-permute-start | bytes 1572872 | tf_op jit(solution)/shard_map/ppermute | solution.py:417
  108.4 24.4 %collective-permute-start.21 = (bf16[1024,256]{1,0:T(8,128)(2,1)S(1)}, bf16[1024,256]{1,0:T(8,128)(2,1)S(1)}, u32[]{:S(2)}, u32[]{:S(2)}) collective-permute-start(bf16[1024,256]{1,0:T(8,128)(2,1)S(1)} %get-tuple-element.22), channel_id=1, source_target_pairs={{0,8},{1,9},{2,10},{3,11},{4,12},{5,13},{6,14},{7,15},{8,16},{9,17... | collective-permute-start | bytes 1572872 | tf_op jit(solution)/shard_map/ppermute | solution.py:425
  111.1 24.9 %collective-permute-start.22 = (bf16[1024,256]{1,0:T(8,128)(2,1)S(1)}, bf16[1024,256]{1,0:T(8,128)(2,1)S(1)}, u32[]{:S(2)}, u32[]{:S(2)}) collective-permute-start(bf16[1024,256]{1,0:T(8,128)(2,1)S(1)} %get-tuple-element.23), channel_id=1, source_target_pairs={{0,16},{1,17},{2,18},{3,19},{4,20},{5,21},{6,22},{7,23},{8,24},{9,... | collective-permute-start | bytes 1572872 | tf_op jit(solution)/shard_map/ppermute | solution.py:425
  114.0 21.9 %collective-permute-start.23 = (bf16[1024,256]{1,0:T(8,128)(2,1)S(1)}, bf16[1024,256]{1,0:T(8,128)(2,1)S(1)}, u32[]{:S(2)}, u32[]{:S(2)}) collective-permute-start(bf16[1024,256]{1,0:T(8,128)(2,1)S(1)} %get-tuple-element.24), channel_id=1, source_target_pairs={{0,24},{1,25},{2,26},{3,27},{4,28},{5,29},{6,30},{7,31},{8,0},{9,1... | collective-permute-start | bytes 1572872 | tf_op jit(solution)/shard_map/ppermute | solution.py:425
  122.7 13.8 %collective-permute-start.11 = (bf16[1024,128]{1,0:T(8,128)(2,1)S(1)}, bf16[1024,128]{1,0:T(8,128)(2,1)S(1)}, u32[]{:S(2)}, u32[]{:S(2)}) collective-permute-start(bf16[1024,128]{1,0:T(8,128)(2,1)S(1)} %query_head_0.1.att), channel_id=1, source_target_pairs={{0,4},{1,5},{2,6},{3,7},{4,0},{5,1},{6,2},{7,3},{8,12},{9,13},{10,... | collective-permute-start | bytes 786440 | tf_op jit(solution)/shard_map/ppermute | solution.py:440
  131.8 8.6 %collective-permute-start.17 = (bf16[1024,128]{1,0:T(8,128)(2,1)S(1)}, bf16[1024,128]{1,0:T(8,128)(2,1)S(1)}, u32[]{:S(2)}, u32[]{:S(2)}) collective-permute-start(bf16[1024,128]{1,0:T(8,128)(2,1)S(1)} %query_head_1.1.att), channel_id=1, source_target_pairs={{0,4},{1,5},{2,6},{3,7},{4,0},{5,1},{6,2},{7,3},{8,12},{9,13},{10,... | collective-permute-start | bytes 786440 | tf_op jit(solution)/shard_map/ppermute | solution.py:440
  132.8 8.6 %collective-permute-start.24 = (bf16[1024,256]{1,0:T(8,128)(2,1)S(1)}, bf16[1024,256]{1,0:T(8,128)(2,1)S(1)}, u32[]{:S(2)}, u32[]{:S(2)}) collective-permute-start(bf16[1024,256]{1,0:T(8,128)(2,1)S(1)} %get-tuple-element.21.refs_8_), channel_id=1, source_target_pairs={{0,64},{64,0},{1,65},{65,1},{2,66},{66,2},{3,67},{67,3},{4,68},{68... | collective-permute-start | bytes 1572872 | tf_op jit(solution)/shard_map/ppermute | solution.py:427
  136.0 8.3 %collective-permute-start.25 = (bf16[1024,256]{1,0:T(8,128)(2,1)S(1)}, bf16[1024,256]{1,0:T(8,128)(2,1)S(1)}, u32[]{:S(2)}, u32[]{:S(2)}) collective-permute-start(bf16[1024,256]{1,0:T(8,128)(2,1)S(1)} %collective-permute-done.21.refs_9_), channel_id=1, source_target_pairs={{0,64},{64,0},{1,65},{65,1},{2,66},{66,2},{3,67},{67,3},{4,68},{68... | collective-permute-start | bytes 1572872 | tf_op jit(solution)/shard_map/ppermute | solution.py:427
  136.0 10.4 %collective-permute-start.26 = (bf16[1024,256]{1,0:T(8,128)(2,1)S(1)}, bf16[1024,256]{1,0:T(8,128)(2,1)S(1)}, u32[]{:S(2)}, u32[]{:S(2)}) collective-permute-start(bf16[1024,256]{1,0:T(8,128)(2,1)S(1)} %collective-permute-done.22.refs_10_), channel_id=1, source_target_pairs={{0,64},{64,0},{1,65},{65,1},{2,66},{66,2},{3,67},{67,3},{4,68},{68... | collective-permute-start | bytes 1572872 | tf_op jit(solution)/shard_map/ppermute | solution.py:427
  136.5 9.9 %collective-permute-start.27 = (bf16[1024,256]{1,0:T(8,128)(2,1)S(1)}, bf16[1024,256]{1,0:T(8,128)(2,1)S(1)}, u32[]{:S(2)}, u32[]{:S(2)}) collective-permute-start(bf16[1024,256]{1,0:T(8,128)(2,1)S(1)} %collective-permute-done.23.refs_11_), channel_id=1, source_target_pairs={{0,64},{64,0},{1,65},{65,1},{2,66},{66,2},{3,67},{67,3},{4,68},{68... | collective-permute-start | bytes 1572872 | tf_op jit(solution)/shard_map/ppermute | solution.py:427
  140.5 27.3 %collective-permute-start.12 = (bf16[1024,256]{1,0:T(8,128)(2,1)S(1)}, bf16[1024,256]{1,0:T(8,128)(2,1)S(1)}, u32[]{:S(2)}, u32[]{:S(2)}) collective-permute-start(bf16[1024,256]{1,0:T(8,128)(2,1)S(1)} %beside_0.1.refs_0_), channel_id=1, source_target_pairs={{0,1},{1,2},{2,3},{3,0},{4,5},{5,6},{6,7},{7,4},{8,9},{9,10},{10,1... | collective-permute-start | bytes 1572872 | tf_op jit(solution)/shard_map/ppermute | solution.py:442
  141.4 26.4 %collective-permute-start.13 = (bf16[1024,256]{1,0:T(8,128)(2,1)S(1)}, bf16[1024,256]{1,0:T(8,128)(2,1)S(1)}, u32[]{:S(2)}, u32[]{:S(2)}) collective-permute-start(bf16[1024,256]{1,0:T(8,128)(2,1)S(1)} %beside_0.1.refs_0_), channel_id=1, source_target_pairs={{0,2},{1,3},{2,0},{3,1},{4,6},{5,7},{6,4},{7,5},{8,10},{9,11},{10,... | collective-permute-start | bytes 1572872 | tf_op jit(solution)/shard_map/ppermute | solution.py:442
  144.3 25.1 %collective-permute-start.14 = (bf16[1024,256]{1,0:T(8,128)(2,1)S(1)}, bf16[1024,256]{1,0:T(8,128)(2,1)S(1)}, u32[]{:S(2)}, u32[]{:S(2)}) collective-permute-start(bf16[1024,256]{1,0:T(8,128)(2,1)S(1)} %beside_0.1.refs_0_), channel_id=1, source_target_pairs={{0,3},{1,0},{2,1},{3,2},{4,7},{5,4},{6,5},{7,6},{8,11},{9,8},{10,9... | collective-permute-start | bytes 1572872 | tf_op jit(solution)/shard_map/ppermute | solution.py:442
  146.4 40.7 %collective-permute-start.18 = (bf16[1024,256]{1,0:T(8,128)(2,1)S(1)}, bf16[1024,256]{1,0:T(8,128)(2,1)S(1)}, u32[]{:S(2)}, u32[]{:S(2)}) collective-permute-start(bf16[1024,256]{1,0:T(8,128)(2,1)S(1)} %beside_1.1.refs_4_), channel_id=1, source_target_pairs={{0,1},{1,2},{2,3},{3,0},{4,5},{5,6},{6,7},{7,4},{8,9},{9,10},{10,1... | collective-permute-start | bytes 1572872 | tf_op jit(solution)/shard_map/ppermute | solution.py:442
  146.4 40.7 %collective-permute-start.19 = (bf16[1024,256]{1,0:T(8,128)(2,1)S(1)}, bf16[1024,256]{1,0:T(8,128)(2,1)S(1)}, u32[]{:S(2)}, u32[]{:S(2)}) collective-permute-start(bf16[1024,256]{1,0:T(8,128)(2,1)S(1)} %beside_1.1.refs_4_), channel_id=1, source_target_pairs={{0,2},{1,3},{2,0},{3,1},{4,6},{5,7},{6,4},{7,5},{8,10},{9,11},{10,... | collective-permute-start | bytes 1572872 | tf_op jit(solution)/shard_map/ppermute | solution.py:442
  167.8 20.8 %collective-permute-start.20 = (bf16[1024,256]{1,0:T(8,128)(2,1)S(1)}, bf16[1024,256]{1,0:T(8,128)(2,1)S(1)}, u32[]{:S(2)}, u32[]{:S(2)}) collective-permute-start(bf16[1024,256]{1,0:T(8,128)(2,1)S(1)} %beside_1.1.refs_4_), channel_id=1, source_target_pairs={{0,3},{1,0},{2,1},{3,2},{4,7},{5,4},{6,5},{7,6},{8,11},{9,8},{10,9... | collective-permute-start | bytes 1572872 | tf_op jit(solution)/shard_map/ppermute | solution.py:442
  193.6 14.9 %collective-permute-start.28 = (bf16[1024,256]{1,0:T(8,128)(2,1)S(1)}, bf16[1024,256]{1,0:T(8,128)(2,1)S(1)}, u32[]{:S(2)}, u32[]{:S(2)}) collective-permute-start(bf16[1024,256]{1,0:T(8,128)(2,1)S(1)} %get-tuple-element.26), channel_id=1, source_target_pairs={{0,24},{1,25},{2,26},{3,27},{4,28},{5,29},{6,30},{7,31},{8,0},{9,1... | collective-permute-start | bytes 1572872 | tf_op jit(solution)/shard_map/ppermute | solution.py:447
  195.1 16.4 %collective-permute-start.29 = (bf16[1024,256]{1,0:T(8,128)(2,1)S(1)}, bf16[1024,256]{1,0:T(8,128)(2,1)S(1)}, u32[]{:S(2)}, u32[]{:S(2)}) collective-permute-start(bf16[1024,256]{1,0:T(8,128)(2,1)S(1)} %get-tuple-element.27), channel_id=1, source_target_pairs={{0,16},{1,17},{2,18},{3,19},{4,20},{5,21},{6,22},{7,23},{8,24},{9,... | collective-permute-start | bytes 1572872 | tf_op jit(solution)/shard_map/ppermute | solution.py:447
  196.3 23.6 %collective-permute-start.30 = (bf16[1024,256]{1,0:T(8,128)(2,1)S(1)}, bf16[1024,256]{1,0:T(8,128)(2,1)S(1)}, u32[]{:S(2)}, u32[]{:S(2)}) collective-permute-start(bf16[1024,256]{1,0:T(8,128)(2,1)S(1)} %get-tuple-element.28), channel_id=1, source_target_pairs={{0,8},{1,9},{2,10},{3,11},{4,12},{5,13},{6,14},{7,15},{8,16},{9,17... | collective-permute-start | bytes 1572872 | tf_op jit(solution)/shard_map/ppermute | solution.py:447

commit v3 on v2

v3 whole, which is shorter than its diff:
```python
import functools

import jax
import jax.numpy as jnp
import numpy as np
from jax import lax
from jax.experimental import pallas as pl
from jax.experimental.pallas import tpu as pltpu
from jax.sharding import PartitionSpec as P

HD = 128
SPAN = 256
D = 8192
BF = jnp.bfloat16
F32 = jnp.float32
TP, KV_HEAD, X, PAIR, Y_HI, Z, SIDE = range(7)
VMEM_LIMIT = 20 * 1024 * 1024


def rope_tables():
    half = HD // 2
    inverse = 1000000.0 ** (-np.arange(half, dtype=np.float64) * 2.0 / HD)
    angles = (
        np.arange(SPAN, dtype=np.float32)[:, None] * inverse.astype(np.float32)[None, :]
    )
    angles = angles.astype(np.float64)
    return np.cos(angles).astype(np.float32), np.sin(angles).astype(np.float32)


def kv_lanes(part):
    low = list(range(16 * part, 16 * part + 16))
    return low + [64 + i for i in low] + list(range(128 + 32 * part, 160 + 32 * part))


def tables():
    cosine, sine = rope_tables()
    pack = np.zeros((2, 256, 512), np.float32)
    gather = np.zeros((4, 2, 128, 256), np.float32)
    bias_sel = np.zeros((4, 256, 128), np.float32)
    k_cos = np.ones((4, SPAN, 128), np.float32)
    k_sin = np.zeros((4, SPAN, 128), np.float32)
    turn = np.zeros((64, 64), np.float32)
    for lane in range(16):
        turn[lane + 16, lane] = 1.0
        turn[lane, lane + 16] = 1.0
    for part in range(4):
        lanes = kv_lanes(part)
        for lane, column in enumerate(lanes):
            pack[0, column, part * 128 + lane] = 1.0
            pack[1, column, part * 128 + 64 + lane] = 1.0
            gather[part, 0, lane, column] = 1.0
            gather[part, 1, 64 + lane, column] = 1.0
            bias_sel[part, column, lane] = 1.0
        bias_sel[part, :, 64:] = bias_sel[part, :, :64] @ turn
        dims = slice(16 * part, 16 * part + 16)
        for base in (0, 64):
            k_cos[part, :, base : base + 16] = cosine[:, dims]
            k_cos[part, :, base + 16 : base + 32] = cosine[:, dims]
            k_sin[part, :, base : base + 16] = -sine[:, dims]
            k_sin[part, :, base + 16 : base + 32] = sine[:, dims]
    unpack = np.zeros((128, 256), np.float32)
    unpack[:64, :64] = np.eye(64)
    unpack[:64, 64:128] = turn
    unpack[64:, 128:192] = np.eye(64)
    unpack[64:, 192:] = turn
    q_cos = np.concatenate([cosine, cosine], 1)
    q_sin = np.concatenate([-sine, sine], 1)
    return {
        "pack": jnp.asarray(pack, BF),
        "gather": jnp.asarray(gather, BF),
        "bias_sel": jnp.asarray(bias_sel, BF),
        "unpack": jnp.asarray(unpack, BF),
        "k_cos": jnp.asarray(k_cos),
        "k_sin": jnp.asarray(k_sin),
        "q_cos": jnp.asarray(q_cos),
        "q_sin": jnp.asarray(q_sin),
    }


def dot(a, b):
    return jnp.dot(a, b, preferred_element_type=F32)


def params(**kw):
    return pltpu.CompilerParams(vmem_limit_bytes=VMEM_LIMIT, **kw)


VM = pl.BlockSpec(memory_space=pltpu.VMEM)
SM = pl.BlockSpec(memory_space=pltpu.SMEM)
AN = pl.BlockSpec(memory_space=pl.ANY)


def shape(dims, dtype=BF):
    return jax.ShapeDtypeStruct(dims, dtype)


def cost(mib):
    return pl.CostEstimate(flops=0, bytes_accessed=mib << 20, transcendentals=0)


def call(body, name, in_specs, out_shape, out_specs, estimate, scratch=(), after=()):
    count = len(in_specs)

    def run(*refs):
        body(*refs[:count], *refs[count + len(after) :])

    kernel = pl.pallas_call(
        run,
        in_specs=in_specs + [AN] * len(after),
        out_specs=out_specs,
        out_shape=out_shape,
        scratch_shapes=list(scratch),
        compiler_params=params(),
        name=name,
        cost_estimate=estimate,
    )
    return lambda *args: kernel(*args, *after)


def pack_body(idx, w, gain, sel, out):
    row = gain[pl.ds((2 * idx[PAIR] + idx[SIDE]) * 16 + idx[TP] // 2, 1), :]
    lane = lax.broadcasted_iota(jnp.int32, (64, 128), 1)
    sub = lax.broadcasted_iota(jnp.int32, (64, 128), 0)
    hit = lane == sub + idx[TP] % 2 * 64
    scale = jnp.sum(jnp.where(hit, jnp.broadcast_to(row, (64, 128)), 0.0), axis=1, keepdims=True)
    for t in range(32):
        place = t // 8 * 4 + t % 4
        which = pl.ds((t // 4 + idx[Y_HI]) % 2, 1)
        for h in range(2):
            lanes = slice((2 * t + h) * 128, (2 * t + h + 1) * 128)
            block = (w[:, lanes].astype(F32) * scale).astype(BF)
            out[place, which, 32 + 64 * h : 96 + 64 * h, :] = block[None]
    for g in range(8):
        keys = w[:, 8192 + g * 128 : 8320 + g * 128]
        values = w[:, 9216 + g * 128 : 9344 + g * 128]
        both = (jnp.concatenate([keys, values], 1).astype(F32) * scale).astype(BF)
        packed = dot(both[:32], sel[0]) + dot(both[32:], sel[1])
        which = pl.ds((g + idx[Y_HI]) % 2, 1)
        for i in range(4):
            block = packed[:, i * 128 : (i + 1) * 128].astype(BF)
            out[g // 2 * 4 + i, which, :32, :] = block[None]


def pack(idx, w_qkv, gain, sel):
    return call(
        pack_body,
        "pack_weights",
        [SM, VM, VM, VM],
        shape((16, 2, 160, 128)),
        VM,
        cost(0),
    )(idx, w_qkv, gain, sel)


def cut_body(src, kv, q):
    kv[...] = src[:, 1, :32, :]
    q[...] = src[:, 1, 32:, :]


def cut(src, after):
    return call(
        cut_body,
        "cut_other_half",
        [VM],
        [shape((16, 32, 128)), shape((16, 128, 128))],
        [VM] * 2,
        cost(0),
        after=after,
    )(src)


def near_body(lo, hi, src, got, out):
    out[0] = src[:, 0, lo:hi, :]
    out[1] = got[...]


def near_rows(lo, hi, src, got, after, name):
    return call(
        functools.partial(near_body, lo, hi),
        name,
        [VM, VM],
        shape((2, 16, hi - lo, 128)),
        VM,
        cost(0),
        after=after,
    )(src, got)


def row_groups(idx, own, mate, side, far):
    p, s, y = idx[PAIR], idx[SIDE], idx[Y_HI]
    for ref, core, here in ((own, p, s), (mate, 1 - p, s), (side, p, 1 - s), (far, 1 - p, 1 - s)):
        yield ref, 0, 2 * core + here, y
        yield ref, 1, 2 * core + 1 - here, 1 - y


def norm_body(idx, x, out, residual):
    def step(i, _):
        rows = pl.ds(pl.multiple_of(i * 128, 128), 128)
        square = jnp.zeros((128, 128), F32)
        for c in range(64):
            piece = x[rows, c * 128 : (c + 1) * 128].astype(F32)
            square += piece * piece
        mean = jnp.sum(square, axis=1, keepdims=True) * (1.0 / D)
        out[rows, :] = jnp.broadcast_to(lax.rsqrt(mean + 1e-6), (128, 128))
        return 0

    lax.fori_loop(0, 8, step, 0)
    residual[...] = x[:, pl.ds(pl.multiple_of(idx[TP] * 256, 256), 256)]


def norms(idx, x, after):
    return call(
        norm_body,
        "token_norms",
        [SM, VM],
        [shape((1024, 128), F32), shape((1024, 256))],
        [VM] * 2,
        cost(0),
        after=after,
    )(idx, x)


def kv_body(idx, x, own, mate, side, far, norm, unpack, bias, bsel, cos, sin, kv, ws, acc, buf, sem):
    for i in range(4):
        pltpu.make_async_copy(x.at[pl.ds(i * 128, 128)], buf.at[i], sem.at[i]).start()
    for ref, i, block, y in row_groups(idx, own, mate, side, far):
        both = dot(ref[i].reshape(512, 128), unpack[...]).astype(BF).reshape(4, 4, 32, 256)
        for z in range(4):
            ws[block, z, y, :, :32, :] = both[z, :, :, :128]
            ws[block, z, y, :, 32:, :] = both[z, :, :, 128:]
    tiles = [
        pltpu.make_async_copy(x.at[pl.ds(i * 128, 128)], buf.at[i % 4], sem.at[i])
        for i in range(8)
    ]
    for i in range(8):
        tiles[i].wait()
        sums = None
        for j in range(4):
            piece = buf[i % 4, :, j * 2048 : (j + 1) * 2048]
            part = dot(piece, ws[j].reshape(2048, 128))
            sums = part if sums is None else sums + part
        acc[i * 128 : (i + 1) * 128, :] = sums
        if i < 4:
            tiles[i + 4].start()
    g = idx[KV_HEAD]
    part = idx[X]
    base = jnp.concatenate([bias[pl.ds(64 + g, 1), :], bias[pl.ds(72 + g, 1), :]], 1)
    base = dot(jnp.broadcast_to(base, (8, 256)).astype(BF), bsel[part])[0:1]
    cosine = cos[part]
    sine = sin[part]
    acc[...] = acc[...] * norm[...] + base
    lane = lax.broadcasted_iota(jnp.int32, (SPAN, 128), 1)
    for i in range(2):
        a = acc[i * 256 : (i + 1) * 256]
        b = acc[512 + i * 256 : 512 + (i + 1) * 256]
        left = a * cosine + pltpu.roll(a, 64, 1) * sine
        right = pltpu.roll(b, 64, 1) * cosine + b * sine
        kv[i * 256 : (i + 1) * 256] = jnp.where(lane < 64, left, right).astype(BF)


def keys_values(idx, x, ws, norm, tab, bias, after):
    return call(
        kv_body,
        "keys_values",
        [SM, AN] + [VM] * 10,
        shape((512, 128)),
        VM,
        cost(0),
        [
            pltpu.VMEM((4, 4, 2, 4, 64, 128), BF),
            pltpu.VMEM((1024, 128), F32),
            pltpu.VMEM((4, 128, D), BF),
            pltpu.SemaphoreType.DMA((8,)),
        ],
        after,
    )(
        idx, x, *ws, norm, tab["unpack"], bias, tab["bias_sel"], tab["k_cos"], tab["k_sin"]
    )


def join_body(idx, kv, first, second, gather, keys, values):
    for half in range(2):
        both = jnp.zeros((512, 256), F32)
        for k, piece in enumerate((kv, first, second.at[0], second.at[1])):
            both += dot(piece[...], gather[idx[X] ^ k, half])
        keys[half * 512 : (half + 1) * 512] = both[:, :128].astype(BF)
        values[half * 512 : (half + 1) * 512] = both[:, 128:].astype(BF)


def join_kv(idx, pieces, tab, after):
    return call(
        join_body,
        "join_keys_values",
        [SM] + [VM] * 4,
        [shape((1024, 128))] * 2,
        [VM] * 2,
        cost(0),
        after=after,
    )(idx, *pieces, tab["gather"])


def heads_body(idx, x, own, mate, side, far, norm, bias, cos, sin, keys, values, *refs):
    atts, ws = refs[:2], refs[2]
    for ref, i, block, y in row_groups(idx, own, mate, side, far.at[0]):
        for z in range(4):
            for h in range(2):
                rows = ref[i, 4 * z : 4 * z + 4, 64 * h : 64 * h + 64, :]
                ws[block, z, y, :, 128 * h : 128 * h + 128] = rows.reshape(256, 128)
    acc = None
    for j in range(4):
        part = dot(x[:, j * 2048 : (j + 1) * 2048], ws[j].reshape(2048, 256))
        acc = part if acc is None else acc + part
    row = lax.broadcasted_iota(jnp.int32, (SPAN, SPAN), 0)
    col = lax.broadcasted_iota(jnp.int32, (SPAN, SPAN), 1)
    ones = jnp.ones((SPAN, HD), BF)
    for seq in range(4):
        rows = slice(seq * SPAN, (seq + 1) * SPAN)
        with_ones = jnp.concatenate([values[rows], ones], 1)
        for h, att in enumerate(atts):
            query = acc[rows, h * 128 : (h + 1) * 128] * norm[rows, :]
            query += bias[pl.ds(2 * idx[TP] + h, 1), :]
            query = (query * cos[...] + pltpu.roll(query, 64, 1) * sin[...]).astype(BF)
            scores = lax.dot_general(
                query, keys[rows], (((1,), (1,)), ((), ())), preferred_element_type=F32
            ) * (HD**-0.5)
            scores = jnp.where(row >= col, scores, -1e30)
            expo = jnp.exp(scores - jnp.max(scores, axis=1, keepdims=True)).astype(BF)
            mixed = dot(expo, with_ones)
            att[rows] = (mixed[:, :HD] / mixed[:, HD:]).astype(BF)


def heads(idx, x, ws, norm, tab, bias, keys, values, after):
    return call(
        heads_body,
        "query_heads",
        [SM] + [VM] * 11,
        [shape((1024, 128))] * 2,
        [VM] * 2,
        cost(0),
        [pltpu.VMEM((4, 4, 2, 256, 256), BF)],
        after=after,
    )(idx, x, *ws, norm, bias, tab["q_cos"], tab["q_sin"], keys, values)


def beside_body(idx, att, across, *outs):
    same = idx[Y_HI] == idx[PAIR]
    for i, out in enumerate(outs):
        rows = slice(512 * i, 512 * i + 512)
        out[:, :128] = jnp.where(same, att[rows, :], across[rows, :])
        out[:, 128:] = jnp.where(same, across[rows, :], att[rows, :])


def beside(idx, att, across, after):
    return call(
        beside_body,
        "beside",
        [SM, VM, VM],
        [shape((512, 256))] * 2,
        [VM] * 2,
        cost(0),
        after=after,
    )(idx, att, across)


def stack_body(*refs):
    for i, ref in enumerate(refs[:-1]):
        refs[-1][i] = ref[...]


def stack(name, arrays, after):
    dims = (len(arrays),) + arrays[0].shape
    return call(
        stack_body,
        name,
        [VM] * len(arrays),
        shape(dims),
        VM,
        cost(0),
        after=after,
    )(*arrays)


def gather_body(a0, a1, a2, a3, *outs):
    for i, out in enumerate(outs):
        for k, ref in enumerate((a0, a1, a2, a3)):
            out[k] = ref[512 * i : 512 * i + 512, :]


def gather_halves(arrays, after):
    return call(
        gather_body,
        "stack_head0",
        [VM] * 4,
        [shape((4, 512, 128))] * 2,
        [VM] * 2,
        cost(0),
        after=after,
    )(*arrays)


def pick_body(idx, here, across, keep, send):
    p = idx[PAIR]
    for i, w in enumerate((here, across)):
        side = idx[SIDE] if i == 0 else 1 - idx[SIDE]
        keep[side] = w[pl.ds(pl.multiple_of(p * 1024, 1024), 1024), :]
        send[side] = w[pl.ds(pl.multiple_of((1 - p) * 1024, 1024), 1024), :]


def pick(idx, here, across, after):
    return call(
        pick_body,
        "pick_rows",
        [SM, VM, VM],
        [shape((2, 1024, 256))] * 2,
        [VM] * 2,
        cost(0),
        after=after,
    )(idx, here, across)


def route_body(idx, keep, recv, *outs):
    for r, out in enumerate(outs):
        goal = (idx[Z] + r) % 4
        same = goal // 2 == idx[PAIR]

        @pl.when(same)
        def _():
            out[...] = keep[goal % 2]

        @pl.when(jnp.logical_not(same))
        def _():
            out[...] = recv[goal % 2]


def route(idx, keep, recv, after):
    return call(
        route_body,
        "route_rows",
        [SM, VM, VM],
        [shape((1024, 256))] * 4,
        [VM] * 4,
        cost(0),
        after=after,
    )(idx, keep, recv)


def w_rows(idx, own, other, r, part):
    rows = []
    for h in range(2):
        for w in (own, other):
            rows.append(w[r, pl.ds(pl.multiple_of(part * 256 + h * 128, 128), 128), :])
    return jnp.concatenate(rows, 0)


def out_body(i, idx, h0, h1, h2, h3, there, a0, a1, a2, a3, own, other, *outs):
    same = idx[Y_HI] == idx[PAIR]
    half = slice(512 * i, 512 * i + 512)
    lanes = []
    for k, (here, both) in enumerate(zip((h0, h1, h2, h3), (a0, a1, a2, a3))):
        near = here[half, :]
        far = there[k]
        lanes.append(
            jnp.concatenate(
                [jnp.where(same, near, far), jnp.where(same, far, near), both[...]], 1
            )
        )
    for r, out in enumerate(outs):
        acc = None
        for k in range(4):
            term = dot(lanes[k], w_rows(idx, own, other, r, (idx[X] + 4 - k) % 4))
            acc = term if acc is None else acc + term
        out[...] = acc.astype(BF)


def project_out(i, idx, here, there, both, own, other, after):
    return call(
        functools.partial(out_body, i),
        f"project_out_{i}",
        [SM] + [VM] * 11,
        [shape((512, 256))] * 4,
        [VM] * 4,
        cost(0),
        after=after,
    )(idx, *here, there, *both, own, other)


def finish_body(i, residual, p0, p1, p2, p3, *refs):
    total = residual[512 * i : 512 * i + 512, :].astype(F32)
    for part in (p0, p1, p2, p3):
        total += part[...].astype(F32)
    if i:
        refs[1][:512, :] = refs[0][...]
        refs[1][512:, :] = total.astype(BF)
    else:
        refs[0][...] = total.astype(BF)


def finish(i, residual, parts, former):
    return call(
        functools.partial(finish_body, i),
        f"add_residual_{i}",
        [VM] * (5 + len(former)),
        shape((512 + 512 * i, 256)),
        VM,
        cost(0),
    )(residual, *parts, *former)


SWAP = [(0, 1), (1, 0)]


def shift(dz, dy, dx):
    return [
        (
            z * 8 + y * 4 + x,
            (z + dz) % 4 * 8 + (y + dy) % 2 * 4 + (x + dx) % 4,
        )
        for z in range(4)
        for y in range(2)
        for x in range(4)
    ]


def flip(bits):
    return [(t, t ^ bits) for t in range(32)]


PLANES = [[z * 8 + y * 4 + x for z in range(4) for x in range(4)] for y in range(2)]
DIAGONAL = [
    (s * 32 + t, (1 - s) * 32 + (t ^ 4)) for s in range(2) for t in range(32)
]


def shards(tokens, norm_gain, w_qkv, qkv_bias, w_out):
    tab = tables()
    seqs, span, width = tokens.shape
    p = lax.axis_index("pair")
    s = lax.axis_index("side")
    t = lax.axis_index("tp")
    idx = jnp.stack([t, t // 4, t % 4, p, t // 4 % 2, t // 8, s]).astype(jnp.int32)
    bias = qkv_bias.reshape(80, 128).astype(F32)
    x = tokens.reshape(seqs * span, width)

    w_across = lax.ppermute(w_out, "side", SWAP)
    packed = pack(idx, w_qkv, norm_gain.reshape(64, 128), tab["pack"])
    blocks = lax.all_to_all(
        packed, "tp", split_axis=0, concat_axis=0, tiled=True, axis_index_groups=PLANES
    )
    norm, residual = norms(idx, x, [packed])
    keep, send = pick(idx, w_out, w_across, [norm])
    recv = lax.ppermute(send, "pair", SWAP)
    kv_got, q_got = [
        lax.ppermute(part, ("side", "tp"), DIAGONAL) for part in cut(blocks, [keep])
    ]
    routed = route(idx, keep, recv, [])
    kv_own = near_rows(0, 32, blocks, kv_got, [routed[0]], "near_kv")
    kv_side = lax.ppermute(kv_own, "side", SWAP)
    kv_mate = lax.ppermute(kv_own, "pair", SWAP)
    q_own = near_rows(32, 160, blocks, q_got, [kv_side], "near_q")
    q_side = lax.ppermute(q_own, "side", SWAP)
    q_mate = lax.ppermute(q_own, "pair", SWAP)
    kv_far = lax.ppermute(kv_side, "pair", SWAP)
    kv_piece = keys_values(
        idx, x, (kv_own, kv_mate, kv_side, kv_far), norm, tab, bias, [q_own]
    )
    first = lax.ppermute(kv_piece, "tp", flip(1))
    pieces = stack("stack_kv", [kv_piece, first], [])
    second = lax.ppermute(pieces, "tp", flip(2))
    keys, values = join_kv(idx, (kv_piece, first, second), tab, [])
    w_own = stack(
        "stack_rows",
        [routed[0]] + [lax.ppermute(routed[r], "tp", shift(r, 0, 0)) for r in range(1, 4)],
        [keys],
    )
    w_other = lax.ppermute(w_own, "pair", SWAP)
    q_late = stack("late_q", [q_side], [w_own])
    q_far = lax.ppermute(q_late, "pair", SWAP)
    att0, att1 = heads(
        idx, x, (q_own, q_mate, q_side, q_far), norm, tab, bias, keys, values, [q_late]
    )

    here = [att0] + [lax.ppermute(att0, "tp", shift(0, 0, r)) for r in range(1, 4)]
    stacked = gather_halves(here, [])
    there = [lax.ppermute(half, "tp", shift(0, 1, 0)) for half in stacked]
    halves = beside(idx, att1, lax.ppermute(att1, "tp", shift(0, 1, 0)), [stacked[0]])

    former = []
    done = []
    for i in range(2):
        plane = [halves[i]] + [
            lax.ppermute(halves[i], "tp", shift(0, 0, r)) for r in range(1, 4)
        ]
        partial = project_out(i, idx, here, there[i], plane, w_own, w_other, done)
        done = [partial[0]]
        parts = [partial[0]] + [
            lax.ppermute(partial[r], "tp", shift(-r, 0, 0)) for r in range(1, 4)
        ]
        former = [finish(i, residual, parts, former)]
    return former[0].reshape(seqs, span, 256)


def solution(mesh):
    placed = (
        P(("pair", "side"), None, None),
        P(),
        P(("pair", "side", "tp"), None),
        P(),
        P(("pair", "side"), "tp"),
    )
    return jax.shard_map(
        shards,
        mesh=mesh,
        in_specs=placed,
        out_specs=P(("pair", "side"), None, "tp"),
        check_vma=False,
    )
```

time: 223 us -> 183 us (0.82)
  waiting for transfers between devices: 126 us -> 68.8 us
  starting transfers between devices: 44.2 us -> 56.5 us
  local copies, waits for them, and re-layouts: 10.8 us -> 17 us
  Pallas kernels: 40.3 us -> 36.7 us
    ppermute x24, waiting for transfers between devices: 78.9 us -> 51 us  [the longest x2 10.4 us: shards(): lax.ppermute(part, ('side', 'tp'), DIAGONAL)]
    all_to_all x1, waiting for transfers between devices: 19.1 us -> 6.16 us  [shards(): lax.all_to_all(packed, 'tp', split_axis=0, concat_axis=0, tiled=True, axi...]
    ppermute x24, starting transfers between devices: 24.7 us -> 37.1 us  [the longest x6 11.2 us: shards(): lax.ppermute(halves[i], 'tp', shift(0, 0, r))]
    ppermute x3 -> x6, waiting for transfers between devices: 22.9 us -> 11.6 us  [shards(): lax.ppermute(partial[r], 'tp', shift(-r, 0, 0))]
    unnamed x28 -> x40, local copies, waits for them, and re-layouts: 10.7 us -> 16.9 us
    ppermute x3 -> x6, starting transfers between devices: 3.28 us -> 7.92 us  [shards(): lax.ppermute(partial[r], 'tp', shift(-r, 0, 0))]
    pallas_call x15 -> x19, Pallas kernels: 40.3 us -> 36.7 us  [call(): return lambda *args: kernel(*args, *after)]
    ppermute x3, waiting for transfers between devices: 3.19 us -> 0.01 us  [shards(): lax.ppermute(routed[r], 'tp', shift(r, 0, 0))]
  transfers between devices with their start and end apart: 32 -> 35, of which waited for: 16 -> 18; matrix products, arithmetic and copies ran while one was open for 0% -> 0% of each run, Pallas kernels for 14% -> 20%
where the time goes in v3:
time: 183 us; the launch traced here: 179 us
  waiting for transfers between devices  68.8 us (38%)
  starting transfers between devices  56.5 us (31%)
  Pallas kernels  36.7 us (20%)
  local copies, waits for them, and re-layouts  17 us (9%)
    pallas_call x19, Pallas kernels, call(): return lambda *args: kernel(*args, *after)  36.7 us
    unnamed x40, local copies, waits for them, and re-layouts  16.9 us
    ppermute x6, waiting for transfers between devices, shards(): lax.ppermute(partial[r], 'tp', shift(-r, 0, 0))  11.6 us
    ppermute x6, starting transfers between devices, shards(): lax.ppermute(halves[i], 'tp', shift(0, 0, r))  11.2 us
    ppermute x2, waiting for transfers between devices, shards(): lax.ppermute(part, ('side', 'tp'), DIAGONAL)  10.4 us
    ppermute x6, waiting for transfers between devices, shards(): lax.ppermute(halves[i], 'tp', shift(0, 0, r))  9.14 us
    ppermute x1, waiting for transfers between devices, shards(): kv_side = lax.ppermute(kv_own, 'side', SWAP)  8.32 us
    ppermute x6, starting transfers between devices, shards(): lax.ppermute(partial[r], 'tp', shift(-r, 0, 0))  7.92 us
  transfers between devices with their start and end apart: 35, of which 18 were waited for; matrix products, arithmetic and copies ran while one was open for 0% of the time, Pallas kernels for 20%

profile of v3, /device:TPU:0, one launch (start us, length us, event | category | flops | bytes accessed | tf_op | source)
XLA Modules:
  0.0 179.4 jit_solution(12941420747159697972)
XLA Ops:
  0.0 1.7 collective-permute-start
  1.7 1.3 copy-done.2
  3.1 1.0 copy-done.9
  4.1 0.8 copy-done.14
  4.9 2.7 %pack_weights.1.refs_2_ = bf16[16,2,160,128]{3,2,1,0:T(8,128)(2,1)} custom-call(s32[7]{0:T(128)S(1)} %stack.31.refs_0_, bf16[64,10240]{1,0:T(8,128)(2,1)S(1)} %copy-done.2, f32[64,128]{1,0:T(8,128)S(1)} %bitcast.18, bf16[2,256,512]{2,1,0:T(8,128)(2,1)S(1)} %copy-done.9), custom_call_target="tpu_custom_call" | custom-call | tf_op jit(solution)/shard_map/pack_weights/pallas_call | solution.py:117
  7.6 7.9 %all-to-all-start = ((bf16[16,2,160,128]{3,2,1,0:T(8,128)(2,1)}), bf16[16,2,160,128]{3,2,1,0:T(8,128)(2,1)S(1)}, u32[]{:S(2)}, u32[]{:S(2)}) async-start(bf16[16,2,160,128]{3,2,1,0:T(8,128)(2,1)} %pack_weights.1.refs_2_), calls=%async_computation | async-start | bytes 2621440 | tf_op jit(solution)/shard_map/all_to_all | solution.py:546
  15.5 5.8 %copy-done = bf16[4,256,8192]{2,1,0:T(8,128)(2,1)S(1)} copy-done((bf16[4,256,8192]{2,1,0:T(8,128)(2,1)S(1)}, bf16[4,256,8192]{2,1,0:T(8,128)(2,1)}, u32[]{:S(2)}) %copy-start) | copy-done | bytes 16777240
  21.3 4.7 %token_norms.1 = (f32[1024,128]{1,0:T(8,128)S(1)}, bf16[1024,256]{1,0:T(8,128)(2,1)S(1)}) custom-call(s32[7]{0:T(128)S(1)} %stack.31.refs_0_, bf16[1024,8192]{1,0:T(8,128)(2,1)S(1)} %bitcast.13, bf16[16,2,160,128]{3,2,1,0:T(8,128)(2,1)} %pack_weights.1.refs_2_), custom_call_target="tpu_custom_call" | custom-call | tf_op jit(solution)/shard_map/token_norms/pallas_call | solution.py:117
  26.0 1.0 copy-done.4
  26.9 1.2 copy-done.5
  28.2 1.7 pick_rows.1
  29.8 6.2 %all-to-all-done.refs_0_ = bf16[16,2,160,128]{3,2,1,0:T(8,128)(2,1)S(1)} async-done(((bf16[16,2,160,128]{3,2,1,0:T(8,128)(2,1)}), bf16[16,2,160,128]{3,2,1,0:T(8,128)(2,1)S(1)}, u32[]{:S(2)}, u32[]{:S(2)}) %all-to-all-start) | async-done | bytes 1310752 | tf_op jit(solution)/shard_map/all_to_all | solution.py:546
  36.0 2.3 %collective-permute-start.1 = (bf16[16,128,128]{2,1,0:T(8,128)(2,1)S(1)}, bf16[16,128,128]{2,1,0:T(8,128)(2,1)S(1)}, u32[]{:S(2)}, u32[]{:S(2)}) collective-permute-start(bf16[16,128,128]{2,1,0:T(8,128)(2,1)S(1)} %get-tuple-element.34), channel_id=1, source_target_pairs={{0,36},{1,37},{2,38},{3,39},{4,32},{5,33},{6,34},{7,35},{8,44},{9,... | collective-permute-start | bytes 1572872 | tf_op jit(solution)/shard_map/ppermute | solution.py:553
  38.3 1.1 collective-permute-start.2
  39.4 1.5 route_rows.1
  40.8 10.4 %collective-permute-done.2.refs_1_ = bf16[16,32,128]{2,1,0:T(8,128)(2,1)S(1)} collective-permute-done((bf16[16,32,128]{2,1,0:T(8,128)(2,1)S(1)}, bf16[16,32,128]{2,1,0:T(8,128)(2,1)S(1)}, u32[]{:S(2)}, u32[]{:S(2)}) %collective-permute-start.2) | collective-permute-done | bytes 131104 | tf_op jit(solution)/shard_map/ppermute | solution.py:553
  51.3 0.1 collective-permute-start.4
  51.5 8.3 %collective-permute-done.4.refs_2_.refs_4_ = bf16[2,16,32,128]{3,2,1,0:T(8,128)(2,1)S(1)} collective-permute-done((bf16[2,16,32,128]{3,2,1,0:T(8,128)(2,1)S(1)}, bf16[2,16,32,128]{3,2,1,0:T(8,128)(2,1)S(1)}, u32[]{:S(2)}, u32[]{:S(2)}) %collective-permute-start.4) | collective-permute-done | bytes 262176 | tf_op jit(solution)/shard_map/ppermute | solution.py:557
  60.2 1.4 collective-permute-start.8
  61.6 2.2 %collective-permute-start.9 = (bf16[1024,256]{1,0:T(8,128)(2,1)S(1)}, bf16[1024,256]{1,0:T(8,128)(2,1)S(1)}, u32[]{:S(2)}, u32[]{:S(2)}) collective-permute-start(bf16[1024,256]{1,0:T(8,128)(2,1)S(1)} %get-tuple-element.40), channel_id=1, source_target_pairs={{0,24},{1,25},{2,26},{3,27},{4,28},{5,29},{6,30},{7,31},{8,0},{9,1... | collective-permute-start | bytes 1572872 | tf_op jit(solution)/shard_map/ppermute | solution.py:572
  63.8 5.8 %copy-done.1 = bf16[4,256,8192]{2,1,0:T(8,128)(2,1)S(1)} copy-done((bf16[4,256,8192]{2,1,0:T(8,128)(2,1)S(1)}, bf16[4,256,8192]{2,1,0:T(8,128)(2,1)}, u32[]{:S(2)}) %copy-start.1) | copy-done | bytes 16777240
  69.6 8.4 %keys_values.1.refs_0_.refs_1_ = bf16[512,128]{1,0:T(8,128)(2,1)S(1)} custom-call(s32[7]{0:T(128)S(1)} %stack.31.refs_0_, bf16[1024,8192]{1,0:T(8,128)(2,1)S(1)} %bitcast.14, bf16[2,16,32,128]{3,2,1,0:T(8,128)(2,1)S(1)} %near_kv.1.refs_2_, bf16[2,16,32,128]{3,2,1,0:T(8,128)(2,1)S(1)} %collective-permute-done.10.refs_3_, ...), custom_call_target="tpu_custom_call" | custom-call | tf_op jit(solution)/shard_map/keys_values/pallas_call | solution.py:117
  78.1 5.0 %collective-permute-done.12.refs_1_.refs_2_ = bf16[512,128]{1,0:T(8,128)(2,1)S(1)} collective-permute-done((bf16[512,128]{1,0:T(8,128)(2,1)S(1)}, bf16[512,128]{1,0:T(8,128)(2,1)S(1)}, u32[]{:S(2)}, u32[]{:S(2)}) %collective-permute-start.12) | collective-permute-done | bytes 131104 | tf_op jit(solution)/shard_map/ppermute | solution.py:566
  83.1 3.2 %collective-permute-start.13 = (bf16[2,512,128]{2,1,0:T(8,128)(2,1)S(1)}, bf16[2,512,128]{2,1,0:T(8,128)(2,1)S(1)}, u32[]{:S(2)}, u32[]{:S(2)}) collective-permute-start(bf16[2,512,128]{2,1,0:T(8,128)(2,1)S(1)} %stack_kv.1), channel_id=1, source_target_pairs={{0,2},{1,3},{2,0},{3,1},{4,6},{5,7},{6,4},{7,5},{8,10},{9,11},{10,... | collective-permute-start | bytes 786440 | tf_op jit(solution)/shard_map/ppermute | solution.py:568
  86.3 5.3 %collective-permute-done.13.refs_3_ = bf16[2,512,128]{2,1,0:T(8,128)(2,1)S(1)} collective-permute-done((bf16[2,512,128]{2,1,0:T(8,128)(2,1)S(1)}, bf16[2,512,128]{2,1,0:T(8,128)(2,1)S(1)}, u32[]{:S(2)}, u32[]{:S(2)}) %collective-permute-start.13) | collective-permute-done | bytes 262176 | tf_op jit(solution)/shard_map/ppermute | solution.py:568
  91.6 1.2 join_keys_values.1
  92.9 0.1 stack_rows.1.refs_1_.refs_10_
  93.1 0.5 collective-permute-start.5
  93.7 0.4 collective-permute-start.14
  94.1 4.7 %collective-permute-done.5.refs_3_ = bf16[2,16,128,128]{3,2,1,0:T(8,128)(2,1)S(1)} collective-permute-done((bf16[2,16,128,128]{3,2,1,0:T(8,128)(2,1)S(1)}, bf16[2,16,128,128]{3,2,1,0:T(8,128)(2,1)S(1)}, u32[]{:S(2)}, u32[]{:S(2)}) %collective-permute-start.5) | collective-permute-done | bytes 1048608 | tf_op jit(solution)/shard_map/ppermute | solution.py:561
  98.8 1.5 collective-permute-done.14.refs_5_
  100.3 8.6 %query_heads.1 = (bf16[1024,128]{1,0:T(8,128)(2,1)S(1)}, bf16[1024,128]{1,0:T(8,128)(2,1)S(1)}) custom-call(s32[7]{0:T(128)S(1)} %stack.31.refs_0_, bf16[1024,8192]{1,0:T(8,128)(2,1)S(1)} %bitcast.17, bf16[2,16,128,128]{3,2,1,0:T(8,128)(2,1)S(1)} %near_q.1.refs_12_.refs_2_, bf16[2,16,128,128]{3,2,1,0:T(8,128)(2,1)S(1)} %collective-permute-done.5.refs_3_, ...), custom_call_target="tpu_custom_call" | custom-call | tf_op jit(solution)/shard_map/query_heads/pallas_call | solution.py:117
  108.9 0.7 collective-permute-start.15
  109.6 3.2 %collective-permute-start.16 = (bf16[1024,128]{1,0:T(8,128)(2,1)S(1)}, bf16[1024,128]{1,0:T(8,128)(2,1)S(1)}, u32[]{:S(2)}, u32[]{:S(2)}) collective-permute-start(bf16[1024,128]{1,0:T(8,128)(2,1)S(1)} %get-tuple-element.43.refs_0_.refs_1_), channel_id=1, source_target_pairs={{0,2},{1,3},{2,0},{3,1},{4,6},{5,7},{6,4},{7,5},{8,10},{9,11},{10,... | collective-permute-start | bytes 786440 | tf_op jit(solution)/shard_map/ppermute | solution.py:582
  112.8 2.0 %collective-permute-start.17 = (bf16[1024,128]{1,0:T(8,128)(2,1)S(1)}, bf16[1024,128]{1,0:T(8,128)(2,1)S(1)}, u32[]{:S(2)}, u32[]{:S(2)}) collective-permute-start(bf16[1024,128]{1,0:T(8,128)(2,1)S(1)} %get-tuple-element.43.refs_0_.refs_1_), channel_id=1, source_target_pairs={{0,3},{1,0},{2,1},{3,2},{4,7},{5,4},{6,5},{7,6},{8,11},{9,8},{10,9... | collective-permute-start | bytes 786440 | tf_op jit(solution)/shard_map/ppermute | solution.py:582
  114.8 3.3 %collective-permute-start.19 = (bf16[1024,128]{1,0:T(8,128)(2,1)S(1)}, bf16[1024,128]{1,0:T(8,128)(2,1)S(1)}, u32[]{:S(2)}, u32[]{:S(2)}) collective-permute-start(bf16[1024,128]{1,0:T(8,128)(2,1)S(1)} %get-tuple-element.45.refs_1_), channel_id=1, source_target_pairs={{0,4},{1,5},{2,6},{3,7},{4,0},{5,1},{6,2},{7,3},{8,12},{9,13},{10,... | collective-permute-start | bytes 786440 | tf_op jit(solution)/shard_map/ppermute | solution.py:585
  118.1 0.7 collective-permute-done.15.refs_1_.refs_2_
  118.8 5.9 %collective-permute-done.16.refs_2_.refs_3_ = bf16[1024,128]{1,0:T(8,128)(2,1)S(1)} collective-permute-done((bf16[1024,128]{1,0:T(8,128)(2,1)S(1)}, bf16[1024,128]{1,0:T(8,128)(2,1)S(1)}, u32[]{:S(2)}, u32[]{:S(2)}) %collective-permute-start.16) | collective-permute-done | bytes 262176 | tf_op jit(solution)/shard_map/ppermute | solution.py:582
  124.9 0.6 beside.1
  125.5 1.8 collective-permute-start.25
  127.3 3.6 %collective-permute-start.24 = (bf16[4,512,128]{2,1,0:T(8,128)(2,1)S(1)}, bf16[4,512,128]{2,1,0:T(8,128)(2,1)S(1)}, u32[]{:S(2)}, u32[]{:S(2)}) collective-permute-start(bf16[4,512,128]{2,1,0:T(8,128)(2,1)S(1)} %get-tuple-element.46.refs_3_), channel_id=1, source_target_pairs={{0,4},{1,5},{2,6},{3,7},{4,0},{5,1},{6,2},{7,3},{8,12},{9,13},{10,... | collective-permute-start | bytes 1572872 | tf_op jit(solution)/shard_map/ppermute | solution.py:584
  130.9 2.4 %collective-permute-start.26 = (bf16[512,256]{1,0:T(8,128)(2,1)S(1)}, bf16[512,256]{1,0:T(8,128)(2,1)S(1)}, u32[]{:S(2)}, u32[]{:S(2)}) collective-permute-start(bf16[512,256]{1,0:T(8,128)(2,1)S(1)} %get-tuple-element.48.refs_6_), channel_id=1, source_target_pairs={{0,2},{1,3},{2,0},{3,1},{4,6},{5,7},{6,4},{7,5},{8,10},{9,11},{10,... | collective-permute-start | bytes 786440 | tf_op jit(solution)/shard_map/ppermute | solution.py:591
  133.2 1.5 collective-permute-start.27
  134.7 3.5 %collective-permute-start.18 = (bf16[4,512,128]{2,1,0:T(8,128)(2,1)S(1)}, bf16[4,512,128]{2,1,0:T(8,128)(2,1)S(1)}, u32[]{:S(2)}, u32[]{:S(2)}) collective-permute-start(bf16[4,512,128]{2,1,0:T(8,128)(2,1)S(1)} %get-tuple-element.44), channel_id=1, source_target_pairs={{0,4},{1,5},{2,6},{3,7},{4,0},{5,1},{6,2},{7,3},{8,12},{9,13},{10,... | collective-permute-start | bytes 1572872 | tf_op jit(solution)/shard_map/ppermute | solution.py:584
  138.3 3.2 %collective-permute-done.26.refs_8_ = bf16[512,256]{1,0:T(8,128)(2,1)S(1)} collective-permute-done((bf16[512,256]{1,0:T(8,128)(2,1)S(1)}, bf16[512,256]{1,0:T(8,128)(2,1)S(1)}, u32[]{:S(2)}, u32[]{:S(2)}) %collective-permute-start.26) | collective-permute-done | bytes 262176 | tf_op jit(solution)/shard_map/ppermute | solution.py:591
  141.5 1.3 collective-permute-start.20
  142.8 1.5 collective-permute-done.27.refs_9_
  144.3 2.2 %collective-permute-start.21 = (bf16[512,256]{1,0:T(8,128)(2,1)S(1)}, bf16[512,256]{1,0:T(8,128)(2,1)S(1)}, u32[]{:S(2)}, u32[]{:S(2)}) collective-permute-start(bf16[512,256]{1,0:T(8,128)(2,1)S(1)} %get-tuple-element.47.refs_6_), channel_id=1, source_target_pairs={{0,2},{1,3},{2,0},{3,1},{4,6},{5,7},{6,4},{7,5},{8,10},{9,11},{10,... | collective-permute-start | bytes 786440 | tf_op jit(solution)/shard_map/ppermute | solution.py:591
  146.5 2.0 %collective-permute-start.22 = (bf16[512,256]{1,0:T(8,128)(2,1)S(1)}, bf16[512,256]{1,0:T(8,128)(2,1)S(1)}, u32[]{:S(2)}, u32[]{:S(2)}) collective-permute-start(bf16[512,256]{1,0:T(8,128)(2,1)S(1)} %get-tuple-element.47.refs_6_), channel_id=1, source_target_pairs={{0,3},{1,0},{2,1},{3,2},{4,7},{5,4},{6,5},{7,6},{8,11},{9,8},{10,9... | collective-permute-start | bytes 786440 | tf_op jit(solution)/shard_map/ppermute | solution.py:591
  148.5 2.9 %project_out_0.1 = (bf16[512,256]{1,0:T(8,128)(2,1)S(1)}, bf16[512,256]{1,0:T(8,128)(2,1)S(1)}, bf16[512,256]{1,0:T(8,128)(2,1)S(1)}, bf16[512,256]{1,0:T(8,128)(2,1)S(1)}) custom-call(s32[7]{0:T(128)S(1)} %stack.31.refs_0_, bf16[1024,128]{1,0:T(8,128)(2,1)S(1)} %get-tuple-element.43.refs_0_.refs_1_, ...), custom_call_target="tpu_custom_call" | custom-call | tf_op jit(solution)/shard_map/project_out_0/pallas_call | solution.py:117
  151.4 1.2 collective-permute-start.31
  152.6 3.0 %collective-permute-done.20.refs_7_ = bf16[512,256]{1,0:T(8,128)(2,1)S(1)} collective-permute-done((bf16[512,256]{1,0:T(8,128)(2,1)S(1)}, bf16[512,256]{1,0:T(8,128)(2,1)S(1)}, u32[]{:S(2)}, u32[]{:S(2)}) %collective-permute-start.20) | collective-permute-done | bytes 262176 | tf_op jit(solution)/shard_map/ppermute | solution.py:591
  155.7 2.6 %collective-permute-start.32 = (bf16[512,256]{1,0:T(8,128)(2,1)S(1)}, bf16[512,256]{1,0:T(8,128)(2,1)S(1)}, u32[]{:S(2)}, u32[]{:S(2)}) collective-permute-start(bf16[512,256]{1,0:T(8,128)(2,1)S(1)} %get-tuple-element.55), channel_id=1, source_target_pairs={{0,16},{1,17},{2,18},{3,19},{4,20},{5,21},{6,22},{7,23},{8,24},{9,... | collective-permute-start | bytes 786440 | tf_op jit(solution)/shard_map/ppermute | solution.py:596
  158.3 1.4 collective-permute-done.22.refs_9_
  159.7 2.9 %project_out_1.1 = (bf16[512,256]{1,0:T(8,128)(2,1)S(1)}, bf16[512,256]{1,0:T(8,128)(2,1)S(1)}, bf16[512,256]{1,0:T(8,128)(2,1)S(1)}, bf16[512,256]{1,0:T(8,128)(2,1)S(1)}) custom-call(s32[7]{0:T(128)S(1)} %stack.31.refs_0_, bf16[1024,128]{1,0:T(8,128)(2,1)S(1)} %get-tuple-element.43.refs_0_.refs_1_, ...), custom_call_target="tpu_custom_call" | custom-call | tf_op jit(solution)/shard_map/project_out_1/pallas_call | solution.py:117
  162.6 1.9 %collective-permute-start.28 = (bf16[512,256]{1,0:T(8,128)(2,1)S(1)}, bf16[512,256]{1,0:T(8,128)(2,1)S(1)}, u32[]{:S(2)}, u32[]{:S(2)}) collective-permute-start(bf16[512,256]{1,0:T(8,128)(2,1)S(1)} %get-tuple-element.51), channel_id=1, source_target_pairs={{0,24},{1,25},{2,26},{3,27},{4,28},{5,29},{6,30},{7,31},{8,0},{9,1... | collective-permute-start | bytes 786440 | tf_op jit(solution)/shard_map/ppermute | solution.py:596
  164.5 1.4 collective-permute-start.29
  165.8 0.8 collective-permute-start.30
  166.6 0.9 collective-permute-done.33.refs_4_
  167.5 0.2 add_residual_0.1.refs_5_
  167.7 4.2 %collective-permute-done.28.refs_2_ = bf16[512,256]{1,0:T(8,128)(2,1)S(1)} collective-permute-done((bf16[512,256]{1,0:T(8,128)(2,1)S(1)}, bf16[512,256]{1,0:T(8,128)(2,1)S(1)}, u32[]{:S(2)}, u32[]{:S(2)}) %collective-permute-start.28) | collective-permute-done | bytes 262176 | tf_op jit(solution)/shard_map/ppermute | solution.py:596
  171.9 3.4 %collective-permute-done.29.refs_3_ = bf16[512,256]{1,0:T(8,128)(2,1)S(1)} collective-permute-done((bf16[512,256]{1,0:T(8,128)(2,1)S(1)}, bf16[512,256]{1,0:T(8,128)(2,1)S(1)}, u32[]{:S(2)}, u32[]{:S(2)}) %collective-permute-start.29) | collective-permute-done | bytes 262176 | tf_op jit(solution)/shard_map/ppermute | solution.py:596
  175.3 3.1 %collective-permute-done.30.refs_4_ = bf16[512,256]{1,0:T(8,128)(2,1)S(1)} collective-permute-done((bf16[512,256]{1,0:T(8,128)(2,1)S(1)}, bf16[512,256]{1,0:T(8,128)(2,1)S(1)}, u32[]{:S(2)}, u32[]{:S(2)}) %collective-permute-start.30) | collective-permute-done | bytes 262176 | tf_op jit(solution)/shard_map/ppermute | solution.py:596
  178.4 1.0 add_residual_1.1
  (68 shorter events, 1.1 us)
Async XLA Ops:
  0.0 26.0 %collective-permute-start = (bf16[2048,256]{1,0:T(8,128)(2,1)}, bf16[2048,256]{1,0:T(8,128)(2,1)S(1)}, u32[]{:S(2)}, u32[]{:S(2)}) collective-permute-start(bf16[2048,256]{1,0:T(8,128)(2,1)} %refs_1_.3), channel_id=1, source_target_pairs={{0,32},{32,0},{1,33},{33,1},{2,34},{34,2},{3,35},{35,3},{4,36},{36... | collective-permute-start | bytes 3145736 | tf_op jit(solution)/shard_map/ppermute | solution.py:544
  1.7 1.3 copy-start.2
  3.1 1.0 copy-start.9
  4.1 0.8 copy-start.14
  7.6 28.4 %all-to-all-start = ((bf16[16,2,160,128]{3,2,1,0:T(8,128)(2,1)}), bf16[16,2,160,128]{3,2,1,0:T(8,128)(2,1)S(1)}, u32[]{:S(2)}, u32[]{:S(2)}) async-start(bf16[16,2,160,128]{3,2,1,0:T(8,128)(2,1)} %pack_weights.1.refs_2_), calls=%async_computation | async-start | bytes 2621440 | tf_op jit(solution)/shard_map/all_to_all | solution.py:546
  15.5 5.8 %copy-start = (bf16[4,256,8192]{2,1,0:T(8,128)(2,1)S(1)}, bf16[4,256,8192]{2,1,0:T(8,128)(2,1)}, u32[]{:S(2)}) copy-start(bf16[4,256,8192]{2,1,0:T(8,128)(2,1)} %param.13) | copy-start | bytes 50331652
  21.3 5.7 %copy-start.3 = (bf16[2048,256]{1,0:T(8,128)(2,1)S(1)}, bf16[2048,256]{1,0:T(8,128)(2,1)}, u32[]{:S(2)}) copy-start(bf16[2048,256]{1,0:T(8,128)(2,1)} %refs_1_.3) | copy-start | bytes 3145732
  26.0 1.0 copy-start.4
  26.9 1.2 copy-start.5
  29.8 9.5 %collective-permute-start.3 = (bf16[2,1024,256]{2,1,0:T(8,128)(2,1)}, bf16[2,1024,256]{2,1,0:T(8,128)(2,1)}, u32[]{:S(2)}, u32[]{:S(2)}) collective-permute-start(bf16[2,1024,256]{2,1,0:T(8,128)(2,1)} %get-tuple-element.36), channel_id=1, source_target_pairs={{0,64},{64,0},{1,65},{65,1},{2,66},{66,2},{3,67},{67,3},{4,68},{68... | collective-permute-start | bytes 3145736 | tf_op jit(solution)/shard_map/ppermute | solution.py:551
  36.0 15.5 %collective-permute-start.1 = (bf16[16,128,128]{2,1,0:T(8,128)(2,1)S(1)}, bf16[16,128,128]{2,1,0:T(8,128)(2,1)S(1)}, u32[]{:S(2)}, u32[]{:S(2)}) collective-permute-start(bf16[16,128,128]{2,1,0:T(8,128)(2,1)S(1)} %get-tuple-element.34), channel_id=1, source_target_pairs={{0,36},{1,37},{2,38},{3,39},{4,32},{5,33},{6,34},{7,35},{8,44},{9,... | collective-permute-start | bytes 1572872 | tf_op jit(solution)/shard_map/ppermute | solution.py:553
  38.3 13.0 %collective-permute-start.2 = (bf16[16,32,128]{2,1,0:T(8,128)(2,1)S(1)}, bf16[16,32,128]{2,1,0:T(8,128)(2,1)S(1)}, u32[]{:S(2)}, u32[]{:S(2)}) collective-permute-start(bf16[16,32,128]{2,1,0:T(8,128)(2,1)S(1)} %get-tuple-element.35), channel_id=1, source_target_pairs={{0,36},{1,37},{2,38},{3,39},{4,32},{5,33},{6,34},{7,35},{8,44},{9,... | collective-permute-start | bytes 393224 | tf_op jit(solution)/shard_map/ppermute | solution.py:553
  51.3 12.5 %copy-start.15 = (bf16[10240]{0:T(1024)(128)(2,1)S(1)}, bf16[10240]{0:T(1024)(128)(2,1)}, u32[]{:S(2)}) copy-start(bf16[10240]{0:T(1024)(128)(2,1)} %param.16) | copy-start | bytes 61444
  51.3 12.5 %copy-start.6 = (f32[4,256,128]{2,1,0:T(8,128)S(1)}, f32[4,256,128]{2,1,0:T(8,128)}, u32[]{:S(2)}) copy-start(f32[4,256,128]{2,1,0:T(8,128)} %constant.79.clone.refs_10_) | copy-start | bytes 1572868
  51.3 12.5 %copy-start.7 = (f32[4,256,128]{2,1,0:T(8,128)S(1)}, f32[4,256,128]{2,1,0:T(8,128)}, u32[]{:S(2)}) copy-start(f32[4,256,128]{2,1,0:T(8,128)} %constant.80.clone.refs_11_) | copy-start | bytes 1572868
  51.3 12.5 %copy-start.10 = (bf16[4,256,128]{2,1,0:T(8,128)(2,1)S(1)}, bf16[4,256,128]{2,1,0:T(8,128)(2,1)}, u32[]{:S(2)}) copy-start(bf16[4,256,128]{2,1,0:T(8,128)(2,1)} %constant.77.clone.refs_9_) | copy-start | bytes 786436
  51.3 12.5 %copy-start.13 = (bf16[128,256]{1,0:T(8,128)(2,1)S(1)}, bf16[128,256]{1,0:T(8,128)(2,1)}, u32[]{:S(2)}) copy-start(bf16[128,256]{1,0:T(8,128)(2,1)} %constant.78.clone.refs_7_) | copy-start | bytes 196612
  51.3 8.5 %collective-permute-start.4 = (bf16[2,16,32,128]{3,2,1,0:T(8,128)(2,1)S(1)}, bf16[2,16,32,128]{3,2,1,0:T(8,128)(2,1)S(1)}, u32[]{:S(2)}, u32[]{:S(2)}) collective-permute-start(bf16[2,16,32,128]{3,2,1,0:T(8,128)(2,1)S(1)} %near_kv.1.refs_2_), channel_id=1, source_target_pairs={{0,32},{32,0},{1,33},{33,1},{2,34},{34,2},{3,35},{35,3},{4,36},{36... | collective-permute-start | bytes 786440 | tf_op jit(solution)/shard_map/ppermute | solution.py:557
  51.4 10.2 %collective-permute-start.10 = (bf16[2,16,32,128]{3,2,1,0:T(8,128)(2,1)S(1)}, bf16[2,16,32,128]{3,2,1,0:T(8,128)(2,1)S(1)}, u32[]{:S(2)}, u32[]{:S(2)}) collective-permute-start(bf16[2,16,32,128]{3,2,1,0:T(8,128)(2,1)S(1)} %near_kv.1.refs_2_), channel_id=1, source_target_pairs={{0,64},{64,0},{1,65},{65,1},{2,66},{66,2},{3,67},{67,3},{4,68},{68... | collective-permute-start | bytes 786440 | tf_op jit(solution)/shard_map/ppermute | solution.py:558
  59.9 33.7 %collective-permute-start.6 = (bf16[2,16,128,128]{3,2,1,0:T(8,128)(2,1)S(1)}, bf16[2,16,128,128]{3,2,1,0:T(8,128)(2,1)S(1)}, u32[]{:S(2)}, u32[]{:S(2)}) collective-permute-start(bf16[2,16,128,128]{3,2,1,0:T(8,128)(2,1)S(1)} %near_q.1.refs_12_.refs_2_), channel_id=1, source_target_pairs={{0,32},{32,0},{1,33},{33,1},{2,34},{34,2},{3,35},{35,3},{4,36},{36... | collective-permute-start | bytes 3145736 | tf_op jit(solution)/shard_map/ppermute | solution.py:560
  60.0 3.8 %collective-permute-start.11 = (bf16[2,16,32,128]{3,2,1,0:T(8,128)(2,1)S(1)}, bf16[2,16,32,128]{3,2,1,0:T(8,128)(2,1)S(1)}, u32[]{:S(2)}, u32[]{:S(2)}) collective-permute-start(bf16[2,16,32,128]{3,2,1,0:T(8,128)(2,1)S(1)} %collective-permute-done.4.refs_2_.refs_4_), channel_id=1, source_target_pairs={{0,64},{64,0},{1,65},{65,1},{2,66},{66,2},{3,67},{67,3},{4,68},{68... | collective-permute-start | bytes 786440 | tf_op jit(solution)/shard_map/ppermute | solution.py:562
  60.1 32.7 %collective-permute-start.7 = (bf16[1024,256]{1,0:T(8,128)(2,1)S(1)}, bf16[1024,256]{1,0:T(8,128)(2,1)S(1)}, u32[]{:S(2)}, u32[]{:S(2)}) collective-permute-start(bf16[1024,256]{1,0:T(8,128)(2,1)S(1)} %get-tuple-element.38), channel_id=1, source_target_pairs={{0,8},{1,9},{2,10},{3,11},{4,12},{5,13},{6,14},{7,15},{8,16},{9,17... | collective-permute-start | bytes 1572872 | tf_op jit(solution)/shard_map/ppermute | solution.py:572
  60.2 32.7 %collective-permute-start.8 = (bf16[1024,256]{1,0:T(8,128)(2,1)S(1)}, bf16[1024,256]{1,0:T(8,128)(2,1)S(1)}, u32[]{:S(2)}, u32[]{:S(2)}) collective-permute-start(bf16[1024,256]{1,0:T(8,128)(2,1)S(1)} %get-tuple-element.39), channel_id=1, source_target_pairs={{0,16},{1,17},{2,18},{3,19},{4,20},{5,21},{6,22},{7,23},{8,24},{9,... | collective-permute-start | bytes 1572872 | tf_op jit(solution)/shard_map/ppermute | solution.py:572
  61.6 31.3 %collective-permute-start.9 = (bf16[1024,256]{1,0:T(8,128)(2,1)S(1)}, bf16[1024,256]{1,0:T(8,128)(2,1)S(1)}, u32[]{:S(2)}, u32[]{:S(2)}) collective-permute-start(bf16[1024,256]{1,0:T(8,128)(2,1)S(1)} %get-tuple-element.40), channel_id=1, source_target_pairs={{0,24},{1,25},{2,26},{3,27},{4,28},{5,29},{6,30},{7,31},{8,0},{9,1... | collective-permute-start | bytes 1572872 | tf_op jit(solution)/shard_map/ppermute | solution.py:572
  63.8 5.8 %copy-start.1 = (bf16[4,256,8192]{2,1,0:T(8,128)(2,1)S(1)}, bf16[4,256,8192]{2,1,0:T(8,128)(2,1)}, u32[]{:S(2)}) copy-start(bf16[4,256,8192]{2,1,0:T(8,128)(2,1)} %param.13) | copy-start | bytes 50331652
  69.6 22.0 %copy-start.8 = (bf16[4,2,128,256]{3,2,1,0:T(8,128)(2,1)S(1)}, bf16[4,2,128,256]{3,2,1,0:T(8,128)(2,1)}, u32[]{:S(2)}) copy-start(bf16[4,2,128,256]{3,2,1,0:T(8,128)(2,1)} %constant.76.clone.refs_4_) | copy-start | bytes 1572868
  69.6 30.7 %slice-start = ((s8[16777216]{0:T(1024)(128)(4,1)}), s8[4194304]{0:T(1024)(128)(4,1)S(1)}, s32[]{:S(2)}) async-start(s8[16777216]{0:T(1024)(128)(4,1)} %bitcast.15), calls=%async_computation.1 | async-start | bytes 8388608
  69.6 30.7 %slice-start.1 = ((s8[16777216]{0:T(1024)(128)(4,1)}), s8[4194304]{0:T(1024)(128)(4,1)S(1)}, s32[]{:S(2)}) async-start(s8[16777216]{0:T(1024)(128)(4,1)} %bitcast.15), calls=%async_computation.2 | async-start | bytes 8388608
  69.6 30.7 %slice-start.2 = ((s8[16777216]{0:T(1024)(128)(4,1)}), s8[4194304]{0:T(1024)(128)(4,1)S(1)}, s32[]{:S(2)}) async-start(s8[16777216]{0:T(1024)(128)(4,1)} %bitcast.15), calls=%async_computation.3 | async-start | bytes 8388608
  78.0 5.1 %collective-permute-start.12 = (bf16[512,128]{1,0:T(8,128)(2,1)S(1)}, bf16[512,128]{1,0:T(8,128)(2,1)S(1)}, u32[]{:S(2)}, u32[]{:S(2)}) collective-permute-start(bf16[512,128]{1,0:T(8,128)(2,1)S(1)} %keys_values.1.refs_0_.refs_1_), channel_id=1, source_target_pairs={{0,1},{1,0},{2,3},{3,2},{4,5},{5,4},{6,7},{7,6},{8,9},{9,8},{10,11... | collective-permute-start | bytes 393224 | tf_op jit(solution)/shard_map/ppermute | solution.py:566
  83.1 8.5 %collective-permute-start.13 = (bf16[2,512,128]{2,1,0:T(8,128)(2,1)S(1)}, bf16[2,512,128]{2,1,0:T(8,128)(2,1)S(1)}, u32[]{:S(2)}, u32[]{:S(2)}) collective-permute-start(bf16[2,512,128]{2,1,0:T(8,128)(2,1)S(1)} %stack_kv.1), channel_id=1, source_target_pairs={{0,2},{1,3},{2,0},{3,1},{4,6},{5,7},{6,4},{7,5},{8,10},{9,11},{10,... | collective-permute-start | bytes 786440 | tf_op jit(solution)/shard_map/ppermute | solution.py:568
  92.9 7.4 %slice-start.3 = ((s8[16777216]{0:T(1024)(128)(4,1)}), s8[4194304]{0:T(1024)(128)(4,1)S(1)}, s32[]{:S(2)}) async-start(s8[16777216]{0:T(1024)(128)(4,1)} %bitcast.15), calls=%async_computation.4 | async-start | bytes 8388608
  93.0 7.3 %copy-start.11 = (f32[256,128]{1,0:T(8,128)S(1)}, f32[256,128]{1,0:T(8,128)}, u32[]{:S(2)}) copy-start(f32[256,128]{1,0:T(8,128)} %constant.81.clone.refs_8_) | copy-start | bytes 393220
  93.0 7.3 %copy-start.12 = (f32[256,128]{1,0:T(8,128)S(1)}, f32[256,128]{1,0:T(8,128)}, u32[]{:S(2)}) copy-start(f32[256,128]{1,0:T(8,128)} %constant.82.clone.refs_9_) | copy-start | bytes 393220
  93.1 53.4 %collective-permute-start.23 = (bf16[4,1024,256]{2,1,0:T(8,128)(2,1)S(1)}, bf16[4,1024,256]{2,1,0:T(8,128)(2,1)S(1)}, u32[]{:S(2)}, u32[]{:S(2)}) collective-permute-start(bf16[4,1024,256]{2,1,0:T(8,128)(2,1)S(1)} %stack_rows.1.refs_1_.refs_10_), channel_id=1, source_target_pairs={{0,64},{64,0},{1,65},{65,1},{2,66},{66,2},{3,67},{67,3},{4,68},{68... | collective-permute-start | bytes 6291464 | tf_op jit(solution)/shard_map/ppermute | solution.py:575
  93.1 5.6 %collective-permute-start.5 = (bf16[2,16,128,128]{3,2,1,0:T(8,128)(2,1)S(1)}, bf16[2,16,128,128]{3,2,1,0:T(8,128)(2,1)S(1)}, u32[]{:S(2)}, u32[]{:S(2)}) collective-permute-start(bf16[2,16,128,128]{3,2,1,0:T(8,128)(2,1)S(1)} %near_q.1.refs_12_.refs_2_), channel_id=1, source_target_pairs={{0,64},{64,0},{1,65},{65,1},{2,66},{66,2},{3,67},{67,3},{4,68},{68... | collective-permute-start | bytes 3145736 | tf_op jit(solution)/shard_map/ppermute | solution.py:561
  93.7 6.6 %collective-permute-start.14 = (bf16[1,2,16,128,128]{4,3,2,1,0:T(8,128)(2,1)S(1)}, bf16[1,2,16,128,128]{4,3,2,1,0:T(8,128)(2,1)S(1)}, u32[]{:S(2)}, u32[]{:S(2)}) collective-permute-start(bf16[1,2,16,128,128]{4,3,2,1,0:T(8,128)(2,1)S(1)} %late_q.1.refs_12_), channel_id=1, source_target_pairs={{0,64},{64,0},{1,65},{65,1},{2,66},{66,2},{3,67},{67,3},{4,68},{68... | collective-permute-start | bytes 3145736 | tf_op jit(solution)/shard_map/ppermute | solution.py:577
  108.9 9.9 %collective-permute-start.15 = (bf16[1024,128]{1,0:T(8,128)(2,1)S(1)}, bf16[1024,128]{1,0:T(8,128)(2,1)S(1)}, u32[]{:S(2)}, u32[]{:S(2)}) collective-permute-start(bf16[1024,128]{1,0:T(8,128)(2,1)S(1)} %get-tuple-element.43.refs_0_.refs_1_), channel_id=1, source_target_pairs={{0,1},{1,2},{2,3},{3,0},{4,5},{5,6},{6,7},{7,4},{8,9},{9,10},{10,1... | collective-permute-start | bytes 786440 | tf_op jit(solution)/shard_map/ppermute | solution.py:582
  109.6 15.1 %collective-permute-start.16 = (bf16[1024,128]{1,0:T(8,128)(2,1)S(1)}, bf16[1024,128]{1,0:T(8,128)(2,1)S(1)}, u32[]{:S(2)}, u32[]{:S(2)}) collective-permute-start(bf16[1024,128]{1,0:T(8,128)(2,1)S(1)} %get-tuple-element.43.refs_0_.refs_1_), channel_id=1, source_target_pairs={{0,2},{1,3},{2,0},{3,1},{4,6},{5,7},{6,4},{7,5},{8,10},{9,11},{10,... | collective-permute-start | bytes 786440 | tf_op jit(solution)/shard_map/ppermute | solution.py:582
  112.8 12.0 %collective-permute-start.17 = (bf16[1024,128]{1,0:T(8,128)(2,1)S(1)}, bf16[1024,128]{1,0:T(8,128)(2,1)S(1)}, u32[]{:S(2)}, u32[]{:S(2)}) collective-permute-start(bf16[1024,128]{1,0:T(8,128)(2,1)S(1)} %get-tuple-element.43.refs_0_.refs_1_), channel_id=1, source_target_pairs={{0,3},{1,0},{2,1},{3,2},{4,7},{5,4},{6,5},{7,6},{8,11},{9,8},{10,9... | collective-permute-start | bytes 786440 | tf_op jit(solution)/shard_map/ppermute | solution.py:582
  114.8 10.1 %collective-permute-start.19 = (bf16[1024,128]{1,0:T(8,128)(2,1)S(1)}, bf16[1024,128]{1,0:T(8,128)(2,1)S(1)}, u32[]{:S(2)}, u32[]{:S(2)}) collective-permute-start(bf16[1024,128]{1,0:T(8,128)(2,1)S(1)} %get-tuple-element.45.refs_1_), channel_id=1, source_target_pairs={{0,4},{1,5},{2,6},{3,7},{4,0},{5,1},{6,2},{7,3},{8,12},{9,13},{10,... | collective-permute-start | bytes 786440 | tf_op jit(solution)/shard_map/ppermute | solution.py:585
  125.5 9.2 %collective-permute-start.25 = (bf16[512,256]{1,0:T(8,128)(2,1)S(1)}, bf16[512,256]{1,0:T(8,128)(2,1)S(1)}, u32[]{:S(2)}, u32[]{:S(2)}) collective-permute-start(bf16[512,256]{1,0:T(8,128)(2,1)S(1)} %get-tuple-element.48.refs_6_), channel_id=1, source_target_pairs={{0,1},{1,2},{2,3},{3,0},{4,5},{5,6},{6,7},{7,4},{8,9},{9,10},{10,1... | collective-permute-start | bytes 786440 | tf_op jit(solution)/shard_map/ppermute | solution.py:591
  127.3 21.3 %collective-permute-start.24 = (bf16[4,512,128]{2,1,0:T(8,128)(2,1)S(1)}, bf16[4,512,128]{2,1,0:T(8,128)(2,1)S(1)}, u32[]{:S(2)}, u32[]{:S(2)}) collective-permute-start(bf16[4,512,128]{2,1,0:T(8,128)(2,1)S(1)} %get-tuple-element.46.refs_3_), channel_id=1, source_target_pairs={{0,4},{1,5},{2,6},{3,7},{4,0},{5,1},{6,2},{7,3},{8,12},{9,13},{10,... | collective-permute-start | bytes 1572872 | tf_op jit(solution)/shard_map/ppermute | solution.py:584
  130.9 10.6 %collective-permute-start.26 = (bf16[512,256]{1,0:T(8,128)(2,1)S(1)}, bf16[512,256]{1,0:T(8,128)(2,1)S(1)}, u32[]{:S(2)}, u32[]{:S(2)}) collective-permute-start(bf16[512,256]{1,0:T(8,128)(2,1)S(1)} %get-tuple-element.48.refs_6_), channel_id=1, source_target_pairs={{0,2},{1,3},{2,0},{3,1},{4,6},{5,7},{6,4},{7,5},{8,10},{9,11},{10,... | collective-permute-start | bytes 786440 | tf_op jit(solution)/shard_map/ppermute | solution.py:591
  133.2 11.1 %collective-permute-start.27 = (bf16[512,256]{1,0:T(8,128)(2,1)S(1)}, bf16[512,256]{1,0:T(8,128)(2,1)S(1)}, u32[]{:S(2)}, u32[]{:S(2)}) collective-permute-start(bf16[512,256]{1,0:T(8,128)(2,1)S(1)} %get-tuple-element.48.refs_6_), channel_id=1, source_target_pairs={{0,3},{1,0},{2,1},{3,2},{4,7},{5,4},{6,5},{7,6},{8,11},{9,8},{10,9... | collective-permute-start | bytes 786440 | tf_op jit(solution)/shard_map/ppermute | solution.py:591
  134.7 24.9 %collective-permute-start.18 = (bf16[4,512,128]{2,1,0:T(8,128)(2,1)S(1)}, bf16[4,512,128]{2,1,0:T(8,128)(2,1)S(1)}, u32[]{:S(2)}, u32[]{:S(2)}) collective-permute-start(bf16[4,512,128]{2,1,0:T(8,128)(2,1)S(1)} %get-tuple-element.44), channel_id=1, source_target_pairs={{0,4},{1,5},{2,6},{3,7},{4,0},{5,1},{6,2},{7,3},{8,12},{9,13},{10,... | collective-permute-start | bytes 1572872 | tf_op jit(solution)/shard_map/ppermute | solution.py:584
  141.5 14.2 %collective-permute-start.20 = (bf16[512,256]{1,0:T(8,128)(2,1)S(1)}, bf16[512,256]{1,0:T(8,128)(2,1)S(1)}, u32[]{:S(2)}, u32[]{:S(2)}) collective-permute-start(bf16[512,256]{1,0:T(8,128)(2,1)S(1)} %get-tuple-element.47.refs_6_), channel_id=1, source_target_pairs={{0,1},{1,2},{2,3},{3,0},{4,5},{5,6},{6,7},{7,4},{8,9},{9,10},{10,1... | collective-permute-start | bytes 786440 | tf_op jit(solution)/shard_map/ppermute | solution.py:591
  144.3 14.0 %collective-permute-start.21 = (bf16[512,256]{1,0:T(8,128)(2,1)S(1)}, bf16[512,256]{1,0:T(8,128)(2,1)S(1)}, u32[]{:S(2)}, u32[]{:S(2)}) collective-permute-start(bf16[512,256]{1,0:T(8,128)(2,1)S(1)} %get-tuple-element.47.refs_6_), channel_id=1, source_target_pairs={{0,2},{1,3},{2,0},{3,1},{4,6},{5,7},{6,4},{7,5},{8,10},{9,11},{10,... | collective-permute-start | bytes 786440 | tf_op jit(solution)/shard_map/ppermute | solution.py:591
  146.5 13.2 %collective-permute-start.22 = (bf16[512,256]{1,0:T(8,128)(2,1)S(1)}, bf16[512,256]{1,0:T(8,128)(2,1)S(1)}, u32[]{:S(2)}, u32[]{:S(2)}) collective-permute-start(bf16[512,256]{1,0:T(8,128)(2,1)S(1)} %get-tuple-element.47.refs_6_), channel_id=1, source_target_pairs={{0,3},{1,0},{2,1},{3,2},{4,7},{5,4},{6,5},{7,6},{8,11},{9,8},{10,9... | collective-permute-start | bytes 786440 | tf_op jit(solution)/shard_map/ppermute | solution.py:591
  151.4 14.4 %collective-permute-start.31 = (bf16[512,256]{1,0:T(8,128)(2,1)S(1)}, bf16[512,256]{1,0:T(8,128)(2,1)S(1)}, u32[]{:S(2)}, u32[]{:S(2)}) collective-permute-start(bf16[512,256]{1,0:T(8,128)(2,1)S(1)} %get-tuple-element.54), channel_id=1, source_target_pairs={{0,24},{1,25},{2,26},{3,27},{4,28},{5,29},{6,30},{7,31},{8,0},{9,1... | collective-permute-start | bytes 786440 | tf_op jit(solution)/shard_map/ppermute | solution.py:596
  155.7 11.0 %collective-permute-start.32 = (bf16[512,256]{1,0:T(8,128)(2,1)S(1)}, bf16[512,256]{1,0:T(8,128)(2,1)S(1)}, u32[]{:S(2)}, u32[]{:S(2)}) collective-permute-start(bf16[512,256]{1,0:T(8,128)(2,1)S(1)} %get-tuple-element.55), channel_id=1, source_target_pairs={{0,16},{1,17},{2,18},{3,19},{4,20},{5,21},{6,22},{7,23},{8,24},{9,... | collective-permute-start | bytes 786440 | tf_op jit(solution)/shard_map/ppermute | solution.py:596
  158.3 9.3 %collective-permute-start.33 = (bf16[512,256]{1,0:T(8,128)(2,1)S(1)}, bf16[512,256]{1,0:T(8,128)(2,1)S(1)}, u32[]{:S(2)}, u32[]{:S(2)}) collective-permute-start(bf16[512,256]{1,0:T(8,128)(2,1)S(1)} %get-tuple-element.56), channel_id=1, source_target_pairs={{0,8},{1,9},{2,10},{3,11},{4,12},{5,13},{6,14},{7,15},{8,16},{9,17... | collective-permute-start | bytes 786440 | tf_op jit(solution)/shard_map/ppermute | solution.py:596
  162.6 9.3 %collective-permute-start.28 = (bf16[512,256]{1,0:T(8,128)(2,1)S(1)}, bf16[512,256]{1,0:T(8,128)(2,1)S(1)}, u32[]{:S(2)}, u32[]{:S(2)}) collective-permute-start(bf16[512,256]{1,0:T(8,128)(2,1)S(1)} %get-tuple-element.51), channel_id=1, source_target_pairs={{0,24},{1,25},{2,26},{3,27},{4,28},{5,29},{6,30},{7,31},{8,0},{9,1... | collective-permute-start | bytes 786440 | tf_op jit(solution)/shard_map/ppermute | solution.py:596
  164.5 10.8 %collective-permute-start.29 = (bf16[512,256]{1,0:T(8,128)(2,1)S(1)}, bf16[512,256]{1,0:T(8,128)(2,1)S(1)}, u32[]{:S(2)}, u32[]{:S(2)}) collective-permute-start(bf16[512,256]{1,0:T(8,128)(2,1)S(1)} %get-tuple-element.52), channel_id=1, source_target_pairs={{0,16},{1,17},{2,18},{3,19},{4,20},{5,21},{6,22},{7,23},{8,24},{9,... | collective-permute-start | bytes 786440 | tf_op jit(solution)/shard_map/ppermute | solution.py:596
  165.8 12.6 %collective-permute-start.30 = (bf16[512,256]{1,0:T(8,128)(2,1)S(1)}, bf16[512,256]{1,0:T(8,128)(2,1)S(1)}, u32[]{:S(2)}, u32[]{:S(2)}) collective-permute-start(bf16[512,256]{1,0:T(8,128)(2,1)S(1)} %get-tuple-element.53), channel_id=1, source_target_pairs={{0,8},{1,9},{2,10},{3,11},{4,12},{5,13},{6,14},{7,15},{8,16},{9,17... | collective-permute-start | bytes 786440 | tf_op jit(solution)/shard_map/ppermute | solution.py:596

commit v4 on v3

--- a/solution.py
+++ b/solution.py
@@ -14,7 +14,6 @@
 BF = jnp.bfloat16
 F32 = jnp.float32
 TP, KV_HEAD, X, PAIR, Y_HI, Z, SIDE = range(7)
-VMEM_LIMIT = 20 * 1024 * 1024
 
 
 def rope_tables():
@@ -81,10 +80,6 @@
     return jnp.dot(a, b, preferred_element_type=F32)
 
 
-def params(**kw):
-    return pltpu.CompilerParams(vmem_limit_bytes=VMEM_LIMIT, **kw)
-
-
 VM = pl.BlockSpec(memory_space=pltpu.VMEM)
 SM = pl.BlockSpec(memory_space=pltpu.SMEM)
 AN = pl.BlockSpec(memory_space=pl.ANY)
@@ -98,7 +93,7 @@
     return pl.CostEstimate(flops=0, bytes_accessed=mib << 20, transcendentals=0)
 
 
-def call(body, name, in_specs, out_shape, out_specs, estimate, scratch=(), after=()):
+def call(body, name, in_specs, out_shape, out_specs, estimate, scratch=(), after=(), mib=16):
     count = len(in_specs)
 
     def run(*refs):
@@ -110,7 +105,7 @@
         out_specs=out_specs,
         out_shape=out_shape,
         scratch_shapes=list(scratch),
-        compiler_params=params(),
+        compiler_params=pltpu.CompilerParams(vmem_limit_bytes=mib << 20),
         name=name,
         cost_estimate=estimate,
     )
@@ -154,18 +149,28 @@
 
 def cut_body(src, kv, q):
     kv[...] = src[:, 1, :32, :]
-    q[...] = src[:, 1, 32:, :]
-
-
-def cut(src, after):
+    q[...] = src[:, 0, 32:, :]
+
+
+def cut_first(src, after):
     return call(
         cut_body,
-        "cut_other_half",
+        "cut_first",
         [VM],
         [shape((16, 32, 128)), shape((16, 128, 128))],
         [VM] * 2,
         cost(0),
         after=after,
+    )(src)
+
+
+def cut_q_body(src, q):
+    q[...] = src[:, 1, 32:, :]
+
+
+def cut_second(src, after):
+    return call(
+        cut_q_body, "cut_second", [VM], shape((16, 128, 128)), VM, cost(0), after=after
     )(src)
 
 
@@ -193,69 +198,88 @@
         yield ref, 1, 2 * core + 1 - here, 1 - y
 
 
-def norm_body(idx, x, out, residual):
-    def step(i, _):
-        rows = pl.ds(pl.multiple_of(i * 128, 128), 128)
+BLOCKS = [pltpu.VMEM((4, 256, D), BF), pltpu.SemaphoreType.DMA((4,))]
+
+
+def block_copy(x, buf, sem, i):
+    return pltpu.make_async_copy(x.at[pl.ds(i * 256, 256)], buf.at[i], sem.at[i])
+
+
+def start_blocks(x, buf, sem):
+    for i in range(4):
+        block_copy(x, buf, sem, i).start()
+
+
+def project_block(x, buf, sem, ws, i, width):
+    block_copy(x, buf, sem, i).wait()
+    sums = None
+    for j in range(4):
+        w = ws[j].reshape(2048, width)
+        part = dot(buf[i, :, j * 2048 : (j + 1) * 2048], w)
+        sums = part if sums is None else sums + part
+    return sums
+
+
+def norm_body(idx, x, out, residual, buf, sem):
+    columns = pl.ds(pl.multiple_of(idx[TP] * 256, 256), 256)
+    copies = [
+        pltpu.make_async_copy(x.at[pl.ds(i * 128, 128)], buf.at[i % 4], sem.at[i])
+        for i in range(8)
+    ]
+    for copy in copies[:4]:
+        copy.start()
+    for i in range(8):
+        copies[i].wait()
+        rows = slice(i * 128, (i + 1) * 128)
         square = jnp.zeros((128, 128), F32)
         for c in range(64):
-            piece = x[rows, c * 128 : (c + 1) * 128].astype(F32)
+            piece = buf[i % 4, :, c * 128 : (c + 1) * 128].astype(F32)
             square += piece * piece
         mean = jnp.sum(square, axis=1, keepdims=True) * (1.0 / D)
         out[rows, :] = jnp.broadcast_to(lax.rsqrt(mean + 1e-6), (128, 128))
-        return 0
-
-    lax.fori_loop(0, 8, step, 0)
-    residual[...] = x[:, pl.ds(pl.multiple_of(idx[TP] * 256, 256), 256)]
+        residual[rows, :] = buf[i % 4, :, columns]
+        if i < 4:
+            copies[i + 4].start()
 
 
 def norms(idx, x, after):
     return call(
         norm_body,
         "token_norms",
-        [SM, VM],
+        [SM, AN],
         [shape((1024, 128), F32), shape((1024, 256))],
         [VM] * 2,
         cost(0),
-        after=after,
+        [pltpu.VMEM((4, 128, D), BF), pltpu.SemaphoreType.DMA((8,))],
+        after,
+        50,
     )(idx, x)
 
 
-def kv_body(idx, x, own, mate, side, far, norm, unpack, bias, bsel, cos, sin, kv, ws, acc, buf, sem):
-    for i in range(4):
-        pltpu.make_async_copy(x.at[pl.ds(i * 128, 128)], buf.at[i], sem.at[i]).start()
+def kv_body(idx, x, own, mate, side, far, norm, unpack, bias, bsel, cos, sin, kv, ws, buf, sem):
+    start_blocks(x, buf, sem)
     for ref, i, block, y in row_groups(idx, own, mate, side, far):
         both = dot(ref[i].reshape(512, 128), unpack[...]).astype(BF).reshape(4, 4, 32, 256)
         for z in range(4):
             ws[block, z, y, :, :32, :] = both[z, :, :, :128]
             ws[block, z, y, :, 32:, :] = both[z, :, :, 128:]
-    tiles = [
-        pltpu.make_async_copy(x.at[pl.ds(i * 128, 128)], buf.at[i % 4], sem.at[i])
-        for i in range(8)
-    ]
-    for i in range(8):
-        tiles[i].wait()
-        sums = None
-        for j in range(4):
-            piece = buf[i % 4, :, j * 2048 : (j + 1) * 2048]
-            part = dot(piece, ws[j].reshape(2048, 128))
-            sums = part if sums is None else sums + part
-        acc[i * 128 : (i + 1) * 128, :] = sums
-        if i < 4:
-            tiles[i + 4].start()
     g = idx[KV_HEAD]
     part = idx[X]
     base = jnp.concatenate([bias[pl.ds(64 + g, 1), :], bias[pl.ds(72 + g, 1), :]], 1)
     base = dot(jnp.broadcast_to(base, (8, 256)).astype(BF), bsel[part])[0:1]
     cosine = cos[part]
     sine = sin[part]
-    acc[...] = acc[...] * norm[...] + base
     lane = lax.broadcasted_iota(jnp.int32, (SPAN, 128), 1)
-    for i in range(2):
-        a = acc[i * 256 : (i + 1) * 256]
-        b = acc[512 + i * 256 : 512 + (i + 1) * 256]
-        left = a * cosine + pltpu.roll(a, 64, 1) * sine
-        right = pltpu.roll(b, 64, 1) * cosine + b * sine
-        kv[i * 256 : (i + 1) * 256] = jnp.where(lane < 64, left, right).astype(BF)
+    for i in range(4):
+        rows = slice(i * SPAN, (i + 1) * SPAN)
+        sums = project_block(x, buf, sem, ws, i, 128) * norm[rows, :] + base
+        turned = pltpu.roll(sums, 64, 1)
+        place = slice((i % 2) * SPAN, (i % 2) * SPAN + SPAN)
+        if i < 2:
+            kv[place, :] = (sums * cosine + turned * sine).astype(BF)
+        else:
+            right = (turned * cosine + sums * sine).astype(BF)
+            kv[place, :] = jnp.where(lane < 64, kv[place, :], right)
 
 
 def keys_values(idx, x, ws, norm, tab, bias, after):
@@ -268,11 +292,10 @@
         cost(0),
         [
             pltpu.VMEM((4, 4, 2, 4, 64, 128), BF),
-            pltpu.VMEM((1024, 128), F32),
-            pltpu.VMEM((4, 128, D), BF),
-            pltpu.SemaphoreType.DMA((8,)),
+            *BLOCKS,
         ],
         after,
+        50,
     )(
         idx, x, *ws, norm, tab["unpack"], bias, tab["bias_sel"], tab["k_cos"], tab["k_sin"]
     )
@@ -299,24 +322,59 @@
     )(idx, *pieces, tab["gather"])
 
 
-def heads_body(idx, x, own, mate, side, far, norm, bias, cos, sin, keys, values, *refs):
-    atts, ws = refs[:2], refs[2]
-    for ref, i, block, y in row_groups(idx, own, mate, side, far.at[0]):
+def run_rows(ref, z):
+    rows = [ref[4 * z : 4 * z + 4, 64 * h : 64 * h + 64, :].reshape(256, 128) for h in range(2)]
+    return jnp.concatenate(rows, 1)
+
+
+def half_block(x, ref, block, y):
+    acc = None
+    for z in range(4):
+        start = pl.multiple_of(block * 2048 + z * 512 + y * 256, 256)
+        term = dot(x[:, pl.ds(start, 256)], run_rows(ref, z))
+        acc = term if acc is None else acc + term
+    return acc
+
+
+def early_body(idx, x, own, mate, side, far, got, got_mate, out, ws):
+    p, s, y = idx[PAIR], idx[SIDE], idx[Y_HI]
+    acc = half_block(x, own, 2 * p + s, y) + half_block(x, mate, 2 * (1 - p) + s, y)
+    for k, (here, there) in enumerate(((side, got), (far, got_mate))):
         for z in range(4):
-            for h in range(2):
-                rows = ref[i, 4 * z : 4 * z + 4, 64 * h : 64 * h + 64, :]
-                ws[block, z, y, :, 128 * h : 128 * h + 128] = rows.reshape(256, 128)
-    acc = None
-    for j in range(4):
-        part = dot(x[:, j * 2048 : (j + 1) * 2048], ws[j].reshape(2048, 256))
-        acc = part if acc is None else acc + part
+            ws[k, z, y] = run_rows(here, z)
+            ws[k, z, 1 - y] = run_rows(there, z)
+        core = p if k == 0 else 1 - p
+        start = pl.multiple_of((2 * core + 1 - s) * 2048, 2048)
+        acc += dot(x[:, pl.ds(start, 2048)], ws[k].reshape(2048, 256))
+    out[...] = acc
+
+
+def early_heads(idx, x, ws, after):
+    return call(
+        early_body,
+        "project_early",
+        [SM] + [VM] * 7,
+        shape((1024, 256), F32),
+        VM,
+        cost(0),
+        [pltpu.VMEM((2, 4, 2, 256, 256), BF)],
+        after,
+    )(idx, x, *ws)
+
+
+def heads_body(
+    idx, x, early, last, last_far, norm, bias, cos, sin, keys, values, first, second, acc
+):
+    p, s, y = idx[PAIR], idx[SIDE], 1 - idx[Y_HI]
+    acc[...] = early[...] + half_block(x, last, 2 * p + s, y)
+    acc[...] += half_block(x, last_far.at[0], 2 * (1 - p) + s, y)
     row = lax.broadcasted_iota(jnp.int32, (SPAN, SPAN), 0)
     col = lax.broadcasted_iota(jnp.int32, (SPAN, SPAN), 1)
     ones = jnp.ones((SPAN, HD), BF)
     for seq in range(4):
         rows = slice(seq * SPAN, (seq + 1) * SPAN)
         with_ones = jnp.concatenate([values[rows], ones], 1)
-        for h, att in enumerate(atts):
+        for h in range(2):
             query = acc[rows, h * 128 : (h + 1) * 128] * norm[rows, :]
             query += bias[pl.ds(2 * idx[TP] + h, 1), :]
             query = (query * cos[...] + pltpu.roll(query, 64, 1) * sin[...]).astype(BF)
@@ -326,28 +384,27 @@
             scores = jnp.where(row >= col, scores, -1e30)
             expo = jnp.exp(scores - jnp.max(scores, axis=1, keepdims=True)).astype(BF)
             mixed = dot(expo, with_ones)
-            att[rows] = (mixed[:, :HD] / mixed[:, HD:]).astype(BF)
+            done = (mixed[:, :HD] / mixed[:, HD:]).astype(BF)
+            (first, second)[h][rows, :] = done
 
 
 def heads(idx, x, ws, norm, tab, bias, keys, values, after):
     return call(
         heads_body,
         "query_heads",
-        [SM] + [VM] * 11,
+        [SM] + [VM] * 10,
         [shape((1024, 128))] * 2,
         [VM] * 2,
         cost(0),
-        [pltpu.VMEM((4, 4, 2, 256, 256), BF)],
-        after=after,
+        [pltpu.VMEM((1024, 256), F32)],
+        after,
     )(idx, x, *ws, norm, bias, tab["q_cos"], tab["q_sin"], keys, values)
 
 
-def beside_body(idx, att, across, *outs):
+def beside_body(idx, att, across, out):
     same = idx[Y_HI] == idx[PAIR]
-    for i, out in enumerate(outs):
-        rows = slice(512 * i, 512 * i + 512)
-        out[:, :128] = jnp.where(same, att[rows, :], across[rows, :])
-        out[:, 128:] = jnp.where(same, across[rows, :], att[rows, :])
+    out[:, :128] = jnp.where(same, att[...], across[...])
+    out[:, 128:] = jnp.where(same, across[...], att[...])
 
 
 def beside(idx, att, across, after):
@@ -355,8 +412,8 @@
         beside_body,
         "beside",
         [SM, VM, VM],
-        [shape((512, 256))] * 2,
-        [VM] * 2,
+        shape((1024, 256)),
+        VM,
         cost(0),
         after=after,
     )(idx, att, across)
@@ -375,24 +432,6 @@
         [VM] * len(arrays),
         shape(dims),
         VM,
-        cost(0),
-        after=after,
-    )(*arrays)
-
-
-def gather_body(a0, a1, a2, a3, *outs):
-    for i, out in enumerate(outs):
-        for k, ref in enumerate((a0, a1, a2, a3)):
-            out[k] = ref[512 * i : 512 * i + 512, :]
-
-
-def gather_halves(arrays, after):
-    return call(
-        gather_body,
-        "stack_head0",
-        [VM] * 4,
-        [shape((4, 512, 128))] * 2,
-        [VM] * 2,
         cost(0),
         after=after,
     )(*arrays)
@@ -418,9 +457,9 @@
     )(idx, here, across)
 
 
-def route_body(idx, keep, recv, *outs):
-    for r, out in enumerate(outs):
-        goal = (idx[Z] + r) % 4
+def route_body(idx, keep, recv, stay, leave):
+    for r, out in enumerate((stay.at[0], stay.at[1], leave.at[0], leave.at[1])):
+        goal = idx[Z] ^ r
         same = goal // 2 == idx[PAIR]
 
         @pl.when(same)
@@ -437,73 +476,96 @@
         route_body,
         "route_rows",
         [SM, VM, VM],
-        [shape((1024, 256))] * 4,
-        [VM] * 4,
+        [shape((2, 1024, 256))] * 2,
+        [VM] * 2,
         cost(0),
         after=after,
     )(idx, keep, recv)
 
 
+def second_body(stay, came, out):
+    out[0] = stay[1]
+    out[1] = came[1]
+
+
+def second_hop(stay, came, after):
+    return call(
+        second_body,
+        "second_rows",
+        [VM, VM],
+        shape((2, 1024, 256)),
+        VM,
+        cost(0),
+        after=after,
+    )(stay, came)
+
+
+def settle_body(idx, stay, came, last, out):
+    z = idx[Z]
+    out[z] = stay[0]
+    out[z ^ 2] = came[0]
+    out[z ^ 1] = last[0]
+    out[z ^ 3] = last[1]
+
+
+def settle(idx, stay, came, last, after):
+    return call(
+        settle_body,
+        "settle_rows",
+        [SM, VM, VM, VM],
+        shape((4, 1024, 256)),
+        VM,
+        cost(0),
+        after=after,
+    )(idx, stay, came, last)
+
+
 def w_rows(idx, own, other, r, part):
+    z = (idx[Z] + 4 - r) % 4
     rows = []
     for h in range(2):
         for w in (own, other):
-            rows.append(w[r, pl.ds(pl.multiple_of(part * 256 + h * 128, 128), 128), :])
+            rows.append(w[z, pl.ds(pl.multiple_of(part * 256 + h * 128, 128), 128), :])
     return jnp.concatenate(rows, 0)
 
 
-def out_body(i, idx, h0, h1, h2, h3, there, a0, a1, a2, a3, own, other, *outs):
+def out_body(r, idx, h0, h1, h2, h3, there, a0, a1, a2, a3, own, other, out):
     same = idx[Y_HI] == idx[PAIR]
-    half = slice(512 * i, 512 * i + 512)
-    lanes = []
+    acc = None
     for k, (here, both) in enumerate(zip((h0, h1, h2, h3), (a0, a1, a2, a3))):
-        near = here[half, :]
+        near = here[...]
         far = there[k]
-        lanes.append(
-            jnp.concatenate(
-                [jnp.where(same, near, far), jnp.where(same, far, near), both[...]], 1
-            )
+        lanes = jnp.concatenate(
+            [jnp.where(same, near, far), jnp.where(same, far, near), both[...]], 1
         )
-    for r, out in enumerate(outs):
-        acc = None
-        for k in range(4):
-            term = dot(lanes[k], w_rows(idx, own, other, r, (idx[X] + 4 - k) % 4))
-            acc = term if acc is None else acc + term
-        out[...] = acc.astype(BF)
-
-
-def project_out(i, idx, here, there, both, own, other, after):
-    return call(
-        functools.partial(out_body, i),
-        f"project_out_{i}",
+        term = dot(lanes, w_rows(idx, own, other, r, (idx[X] + 4 - k) % 4))
+        acc = term if acc is None else acc + term
+    out[...] = acc.astype(BF)
+
+
+def project_out(r, idx, here, there, both, own, other, after):
+    return call(
+        functools.partial(out_body, r),
+        f"project_out_{r}",
         [SM] + [VM] * 11,
-        [shape((512, 256))] * 4,
-        [VM] * 4,
+        shape((1024, 256)),
+        VM,
         cost(0),
         after=after,
     )(idx, *here, there, *both, own, other)
 
 
-def finish_body(i, residual, p0, p1, p2, p3, *refs):
-    total = residual[512 * i : 512 * i + 512, :].astype(F32)
+def finish_body(residual, p0, p1, p2, p3, out):
+    total = residual[...].astype(F32)
     for part in (p0, p1, p2, p3):
         total += part[...].astype(F32)
-    if i:
-        refs[1][:512, :] = refs[0][...]
-        refs[1][512:, :] = total.astype(BF)
-    else:
-        refs[0][...] = total.astype(BF)
-
-
-def finish(i, residual, parts, former):
-    return call(
-        functools.partial(finish_body, i),
-        f"add_residual_{i}",
-        [VM] * (5 + len(former)),
-        shape((512 + 512 * i, 256)),
-        VM,
-        cost(0),
-    )(residual, *parts, *former)
+    out[...] = total.astype(BF)
+
+
+def finish(residual, parts):
+    return call(
+        finish_body, "add_residual", [VM] * 5, shape((1024, 256)), VM, cost(0)
+    )(residual, *parts)
 
 
 SWAP = [(0, 1), (1, 0)]
@@ -548,55 +610,49 @@
     )
     norm, residual = norms(idx, x, [packed])
     keep, send = pick(idx, w_out, w_across, [norm])
-    recv = lax.ppermute(send, "pair", SWAP)
-    kv_got, q_got = [
-        lax.ppermute(part, ("side", "tp"), DIAGONAL) for part in cut(blocks, [keep])
-    ]
-    routed = route(idx, keep, recv, [])
-    kv_own = near_rows(0, 32, blocks, kv_got, [routed[0]], "near_kv")
+    kv_other, q_own = cut_first(blocks, [keep])
+    q_side = lax.ppermute(q_own, "side", SWAP)
+    kv_got = lax.ppermute(kv_other, ("side", "tp"), DIAGONAL)
+    kv_own = near_rows(0, 32, blocks, kv_got, [q_own], "near_kv")
     kv_side = lax.ppermute(kv_own, "side", SWAP)
     kv_mate = lax.ppermute(kv_own, "pair", SWAP)
-    q_own = near_rows(32, 160, blocks, q_got, [kv_side], "near_q")
-    q_side = lax.ppermute(q_own, "side", SWAP)
-    q_mate = lax.ppermute(q_own, "pair", SWAP)
+    q_got = lax.ppermute(cut_second(blocks, [kv_own]), ("side", "tp"), DIAGONAL)
+    stay, leave = route(idx, keep, lax.ppermute(send, "pair", SWAP), [kv_own])
     kv_far = lax.ppermute(kv_side, "pair", SWAP)
     kv_piece = keys_values(
-        idx, x, (kv_own, kv_mate, kv_side, kv_far), norm, tab, bias, [q_own]
-    )
+        idx, x, (kv_own, kv_mate, kv_side, kv_far), norm, tab, bias, [q_got, stay]
+    )
+    got_side = lax.ppermute(q_got, "side", SWAP)
+    q_mates = [lax.ppermute(q, "pair", SWAP) for q in (q_own, q_side, q_got)]
     first = lax.ppermute(kv_piece, "tp", flip(1))
-    pieces = stack("stack_kv", [kv_piece, first], [])
+    pieces = stack("stack_kv", [kv_piece, first], [*q_mates, got_side])
     second = lax.ppermute(pieces, "tp", flip(2))
-    keys, values = join_kv(idx, (kv_piece, first, second), tab, [])
-    w_own = stack(
-        "stack_rows",
-        [routed[0]] + [lax.ppermute(routed[r], "tp", shift(r, 0, 0)) for r in range(1, 4)],
-        [keys],
-    )
+    came = lax.ppermute(leave, "tp", flip(16))
+    hop = second_hop(stay, came, [pieces])
+    late = stack("late_q", [got_side], [hop])
+    early = early_heads(
+        idx, x, (q_own, q_mates[0], q_side, q_mates[1], q_got, q_mates[2]), [late]
+    )
+    keys, values = join_kv(idx, (kv_piece, first, second), tab, [early])
+    ws = (early, got_side, lax.ppermute(late, "pair", SWAP).reshape(1, 16, 128, 128))
+    att0, att1 = heads(idx, x, ws, norm, tab, bias, keys, values, [])
+    here = [att0] + [lax.ppermute(att0, "tp", shift(0, 0, r)) for r in range(1, 4)]
+    stacked = stack("stack_head0", here, [])
+    there = lax.ppermute(stacked, "tp", shift(0, 1, 0))
+    both = beside(idx, att1, lax.ppermute(att1, "tp", shift(0, 1, 0)), [stacked])
+    plane = [both] + [lax.ppermute(both, "tp", shift(0, 0, r)) for r in range(1, 4)]
+    w_own = settle(idx, stay, came, lax.ppermute(hop, "tp", flip(8)), [both])
     w_other = lax.ppermute(w_own, "pair", SWAP)
-    q_late = stack("late_q", [q_side], [w_own])
-    q_far = lax.ppermute(q_late, "pair", SWAP)
-    att0, att1 = heads(
-        idx, x, (q_own, q_mate, q_side, q_far), norm, tab, bias, keys, values, [q_late]
-    )
-
-    here = [att0] + [lax.ppermute(att0, "tp", shift(0, 0, r)) for r in range(1, 4)]
-    stacked = gather_halves(here, [])
-    there = [lax.ppermute(half, "tp", shift(0, 1, 0)) for half in stacked]
-    halves = beside(idx, att1, lax.ppermute(att1, "tp", shift(0, 1, 0)), [stacked[0]])
-
-    former = []
-    done = []
-    for i in range(2):
-        plane = [halves[i]] + [
-            lax.ppermute(halves[i], "tp", shift(0, 0, r)) for r in range(1, 4)
-        ]
-        partial = project_out(i, idx, here, there[i], plane, w_own, w_other, done)
-        done = [partial[0]]
-        parts = [partial[0]] + [
-            lax.ppermute(partial[r], "tp", shift(-r, 0, 0)) for r in range(1, 4)
-        ]
-        former = [finish(i, residual, parts, former)]
-    return former[0].reshape(seqs, span, 256)
+
+    parts = []
+    for r in (2, 1, 3, 0):
+        partial = project_out(r, idx, here, there, plane, w_own, w_other, parts[-1:])
+        parts.append(partial)
+    parts = [
+        lax.ppermute(part, "tp", shift(-r, 0, 0)) if r else part
+        for r, part in zip((2, 1, 3, 0), parts)
+    ]
+    return finish(residual, parts).reshape(seqs, span, 256)
 
 
 def solution(mesh):

time: 183 us -> 172 us (0.940); the launches traced: 179 us -> 171 us
  starting transfers between devices: 56.5 us -> 34.9 us
  waiting for transfers between devices: 68.8 us -> 80.5 us
  Pallas kernels: 36.7 us -> 41.8 us
  local copies, waits for them, and re-layouts: 17 us -> 13.5 us
    ppermute x22 -> x17, starting transfers between devices: 34.1 us -> 15.5 us  [the longest x3 4.07 us: shards(): lax.ppermute(part, 'tp', shift(-r, 0, 0))]
    ppermute x22 -> x17, waiting for transfers between devices: 37.4 us -> 48.6 us  [the longest x3 24.7 us: shards(): lax.ppermute(both, 'tp', shift(0, 0, r))]
    ppermute x1, waiting for transfers between devices: 5.31 us -> 0.01 us  [shards(): second = lax.ppermute(pieces, 'tp', flip(2))]
    pallas_call x19 -> x22, Pallas kernels: 36.7 us -> 41.8 us  [call(): return lambda *args: kernel(*args, *after)]
    ppermute x3, waiting for transfers between devices: 6.63 us -> 11.6 us  [shards(): lax.ppermute(att0, 'tp', shift(0, 0, r))]
    ppermute x3, starting transfers between devices: 5.88 us -> 2.09 us  [shards(): lax.ppermute(att0, 'tp', shift(0, 0, r))]
    unnamed x40, local copies, waits for them, and re-layouts: 16.9 us -> 13.5 us
    ppermute x1, waiting for transfers between devices: 8.32 us -> 6.27 us  [shards(): kv_side = lax.ppermute(kv_own, 'side', SWAP)]
  transfers between devices with their start and end apart: 35 -> 30, of which waited for: 18 -> 15; matrix products, arithmetic and copies ran while one was open for 0% -> 0% of each run, Pallas kernels for 20% -> 20%
where the time goes in v4:
time: 172 us; the launch traced here: 171 us
  waiting for transfers between devices  80.5 us (47%)
  Pallas kernels  41.8 us (24%)
  starting transfers between devices  34.9 us (20%)
  local copies, waits for them, and re-layouts  13.5 us (8%)
    pallas_call x22, Pallas kernels, call(): return lambda *args: kernel(*args, *after)  41.8 us
    ppermute x3, waiting for transfers between devices, shards(): lax.ppermute(both, 'tp', shift(0, 0, r))  24.7 us
    ppermute x3, waiting for transfers between devices, shards(): lax.ppermute(part, 'tp', shift(-r, 0, 0))  20.5 us
    unnamed x40, local copies, waits for them, and re-layouts  13.5 us
    ppermute x3, waiting for transfers between devices, shards(): lax.ppermute(att0, 'tp', shift(0, 0, r))  11.6 us
    all_to_all x1, starting transfers between devices, shards(): lax.all_to_all(packed, 'tp', split_axis=0, concat_axis=0, tiled=True, axi...  7.88 us
    all_to_all x1, waiting for transfers between devices, shards(): lax.all_to_all(packed, 'tp', split_axis=0, concat_axis=0, tiled=True, axi...  7.12 us
    ppermute x1, waiting for transfers between devices, shards(): kv_side = lax.ppermute(kv_own, 'side', SWAP)  6.27 us
  transfers between devices with their start and end apart: 30, of which 15 were waited for; matrix products, arithmetic and copies ran while one was open for 0% of the time, Pallas kernels for 20%

profile of v4, /device:TPU:0, one launch (start us, length us, event | category | flops | bytes accessed | tf_op | source)
XLA Modules:
  0.0 171.1 jit_solution(10558742877509604280)
XLA Ops:
  0.0 1.7 collective-permute-start
  1.7 1.3 copy-done.4
  3.1 1.0 copy-done.13
  4.1 0.8 copy-done.18
  4.9 2.8 %pack_weights.1.refs_2_ = bf16[16,2,160,128]{3,2,1,0:T(8,128)(2,1)} custom-call(s32[7]{0:T(128)S(1)} %stack.31.refs_0_, bf16[64,10240]{1,0:T(8,128)(2,1)S(1)} %copy-done.4, f32[64,128]{1,0:T(8,128)S(1)} %bitcast.17, bf16[2,256,512]{2,1,0:T(8,128)(2,1)S(1)} %copy-done.13), custom_call_target="tpu_custom_call" | custom-call | tf_op jit(solution)/shard_map/pack_weights/pallas_call | solution.py:112
  7.6 7.9 %all-to-all-start = ((bf16[16,2,160,128]{3,2,1,0:T(8,128)(2,1)}), bf16[16,2,160,128]{3,2,1,0:T(8,128)(2,1)S(1)}, u32[]{:S(2)}, u32[]{:S(2)}) async-start(bf16[16,2,160,128]{3,2,1,0:T(8,128)(2,1)} %pack_weights.1.refs_2_), calls=%async_computation | async-start | bytes 2621440 | tf_op jit(solution)/shard_map/all_to_all | solution.py:608
  15.5 7.2 %token_norms.1 = (f32[1024,128]{1,0:T(8,128)S(1)}, bf16[1024,256]{1,0:T(8,128)(2,1)S(1)}) custom-call(s32[7]{0:T(128)S(1)} %stack.31.refs_0_, bf16[1024,8192]{1,0:T(8,128)(2,1)} %bitcast.13, bf16[16,2,160,128]{3,2,1,0:T(8,128)(2,1)} %pack_weights.1.refs_2_), custom_call_target="tpu_custom_call" | custom-call | tf_op jit(solution)/shard_map/token_norms/pallas_call | solution.py:112
  22.8 0.8 copy-done.11
  23.6 1.4 collective-permute-done.refs_2_
  25.0 1.0 copy-done.6
  26.0 1.2 copy-done.7
  27.2 1.7 pick_rows.1
  28.9 7.1 %all-to-all-done.refs_0_ = bf16[16,2,160,128]{3,2,1,0:T(8,128)(2,1)S(1)} async-done(((bf16[16,2,160,128]{3,2,1,0:T(8,128)(2,1)}), bf16[16,2,160,128]{3,2,1,0:T(8,128)(2,1)S(1)}, u32[]{:S(2)}, u32[]{:S(2)}) %all-to-all-start) | async-done | bytes 1310752 | tf_op jit(solution)/shard_map/all_to_all | solution.py:608
  36.1 2.3 %collective-permute-start.4 = (bf16[16,32,128]{2,1,0:T(8,128)(2,1)S(1)}, bf16[16,32,128]{2,1,0:T(8,128)(2,1)S(1)}, u32[]{:S(2)}, u32[]{:S(2)}) collective-permute-start(bf16[16,32,128]{2,1,0:T(8,128)(2,1)S(1)} %get-tuple-element.21), channel_id=1, source_target_pairs={{0,36},{1,37},{2,38},{3,39},{4,32},{5,33},{6,34},{7,35},{8,44},{9,... | collective-permute-start | bytes 393224 | tf_op jit(solution)/shard_map/ppermute | solution.py:615
  38.3 0.7 collective-permute-start.2
  39.0 3.3 %collective-permute-done.4.refs_1_ = bf16[16,32,128]{2,1,0:T(8,128)(2,1)S(1)} collective-permute-done((bf16[16,32,128]{2,1,0:T(8,128)(2,1)S(1)}, bf16[16,32,128]{2,1,0:T(8,128)(2,1)S(1)}, u32[]{:S(2)}, u32[]{:S(2)}) %collective-permute-start.4) | collective-permute-done | bytes 131104 | tf_op jit(solution)/shard_map/ppermute | solution.py:615
  42.5 2.3 %collective-permute-start.5 = (bf16[16,128,128]{2,1,0:T(8,128)(2,1)S(1)}, bf16[16,128,128]{2,1,0:T(8,128)(2,1)S(1)}, u32[]{:S(2)}, u32[]{:S(2)}) collective-permute-start(bf16[16,128,128]{2,1,0:T(8,128)(2,1)S(1)} %cut_second.1), channel_id=1, source_target_pairs={{0,36},{1,37},{2,38},{3,39},{4,32},{5,33},{6,34},{7,35},{8,44},{9,... | collective-permute-start | bytes 1572872 | tf_op jit(solution)/shard_map/ppermute | solution.py:619
  44.7 0.6 collective-permute-start.11
  45.3 1.4 route_rows.1
  46.8 1.0 copy-done.2
  47.8 0.7 collective-permute-start.9
  48.5 6.3 %collective-permute-done.11.refs_4_ = bf16[2,16,32,128]{3,2,1,0:T(8,128)(2,1)S(1)} collective-permute-done((bf16[2,16,32,128]{3,2,1,0:T(8,128)(2,1)S(1)}, bf16[2,16,32,128]{3,2,1,0:T(8,128)(2,1)S(1)}, u32[]{:S(2)}, u32[]{:S(2)}) %collective-permute-start.11) | collective-permute-done | bytes 262176 | tf_op jit(solution)/shard_map/ppermute | solution.py:617
  54.8 0.5 collective-permute-start.1
  55.4 0.7 collective-permute-start.7
  56.1 0.2 collective-permute-done.12.refs_5_
  56.3 0.1 collective-permute-start.6
  56.5 8.7 %keys_values.1.refs_0_.refs_1_ = bf16[512,128]{1,0:T(8,128)(2,1)S(1)} custom-call(s32[7]{0:T(128)S(1)} %stack.31.refs_0_, bf16[1024,8192]{1,0:T(8,128)(2,1)} %bitcast.14, bf16[2,16,32,128]{3,2,1,0:T(8,128)(2,1)S(1)} %near_kv.1.refs_1_.refs_3_.refs_2_, bf16[2,16,32,128]{3,2,1,0:T(8,128)(2,1)S(1)} %collective-permute-done.10.refs_3_, ...), custom_call_target="tpu_custom_call" | custom-call | tf_op jit(solution)/shard_map/keys_values/pallas_call | solution.py:112
  65.2 0.7 collective-permute-start.13
  65.9 5.2 %collective-permute-done.13.refs_1_.refs_2_ = bf16[512,128]{1,0:T(8,128)(2,1)S(1)} collective-permute-done((bf16[512,128]{1,0:T(8,128)(2,1)S(1)}, bf16[512,128]{1,0:T(8,128)(2,1)S(1)}, u32[]{:S(2)}, u32[]{:S(2)}) %collective-permute-start.13) | collective-permute-done | bytes 131104 | tf_op jit(solution)/shard_map/ppermute | solution.py:627
  71.2 0.1 collective-permute-start.24
  71.5 4.0 %collective-permute-start.15 = (bf16[2,512,128]{2,1,0:T(8,128)(2,1)S(1)}, bf16[2,512,128]{2,1,0:T(8,128)(2,1)S(1)}, u32[]{:S(2)}, u32[]{:S(2)}) collective-permute-start(bf16[2,512,128]{2,1,0:T(8,128)(2,1)S(1)} %stack_kv.1.refs_2_), channel_id=1, source_target_pairs={{0,2},{1,3},{2,0},{3,1},{4,6},{5,7},{6,4},{7,5},{8,10},{9,11},{10,... | collective-permute-start | bytes 786440 | tf_op jit(solution)/shard_map/ppermute | solution.py:629
  75.5 5.8 %copy-done = bf16[4,256,8192]{2,1,0:T(8,128)(2,1)S(1)} copy-done((bf16[4,256,8192]{2,1,0:T(8,128)(2,1)S(1)}, bf16[4,256,8192]{2,1,0:T(8,128)(2,1)}, u32[]{:S(2)}) %copy-start) | copy-done | bytes 16777240
  81.3 4.1 %project_early.1.refs_5_.refs_2_ = f32[1024,256]{1,0:T(8,128)S(1)} custom-call(s32[7]{0:T(128)S(1)} %stack.31.refs_0_, bf16[1024,8192]{1,0:T(8,128)(2,1)S(1)} %bitcast.15, bf16[16,128,128]{2,1,0:T(8,128)(2,1)S(1)} %get-tuple-element.20.refs_2_, bf16[16,128,128]{2,1,0:T(8,128)(2,1)S(1)} %collective-permute-done.1.refs_2_.refs_3_, ...), custom_call_target="tpu_custom_call" | custom-call | tf_op jit(solution)/shard_map/project_early/pallas_call | solution.py:112
  85.4 1.2 join_keys_values.1
  86.7 0.4 copy-done.1
  87.0 0.1 copy-done.15
  87.2 4.6 %query_heads.1 = (bf16[1024,128]{1,0:T(8,128)(2,1)S(1)}, bf16[1024,128]{1,0:T(8,128)(2,1)S(1)}) custom-call(s32[7]{0:T(128)S(1)} %stack.31.refs_0_, bf16[1024,8192]{1,0:T(8,128)(2,1)S(1)} %bitcast.16, f32[1024,256]{1,0:T(8,128)S(1)} %project_early.1.refs_5_.refs_2_, bf16[16,128,128]{2,1,0:T(8,128)(2,1)S(1)} %collective-permute-done.7.refs_5_.refs_0_.refs_3_, ...), custom_call_target="tpu_custom_call" | custom-call | tf_op jit(solution)/shard_map/query_heads/pallas_call | solution.py:112
  91.9 1.7 %collective-permute-start.17 = (bf16[1024,128]{1,0:T(8,128)(2,1)S(1)}, bf16[1024,128]{1,0:T(8,128)(2,1)S(1)}, u32[]{:S(2)}, u32[]{:S(2)}) collective-permute-start(bf16[1024,128]{1,0:T(8,128)(2,1)S(1)} %get-tuple-element.27.refs_0_.refs_1_), channel_id=1, source_target_pairs={{0,2},{1,3},{2,0},{3,1},{4,6},{5,7},{6,4},{7,5},{8,10},{9,11},{10,... | collective-permute-start | bytes 786440 | tf_op jit(solution)/shard_map/ppermute | solution.py:639
  93.6 0.3 collective-permute-start.16
  93.9 1.7 %collective-permute-start.20 = (bf16[1024,128]{1,0:T(8,128)(2,1)S(1)}, bf16[1024,128]{1,0:T(8,128)(2,1)S(1)}, u32[]{:S(2)}, u32[]{:S(2)}) collective-permute-start(bf16[1024,128]{1,0:T(8,128)(2,1)S(1)} %get-tuple-element.28.refs_1_), channel_id=1, source_target_pairs={{0,4},{1,5},{2,6},{3,7},{4,0},{5,1},{6,2},{7,3},{8,12},{9,13},{10,... | collective-permute-start | bytes 786440 | tf_op jit(solution)/shard_map/ppermute | solution.py:642
  95.6 5.4 %collective-permute-done.18.refs_3_.refs_4_ = bf16[1024,128]{1,0:T(8,128)(2,1)S(1)} collective-permute-done((bf16[1024,128]{1,0:T(8,128)(2,1)S(1)}, bf16[1024,128]{1,0:T(8,128)(2,1)S(1)}, u32[]{:S(2)}, u32[]{:S(2)}) %collective-permute-start.18) | collective-permute-done | bytes 262176 | tf_op jit(solution)/shard_map/ppermute | solution.py:639
  101.1 1.6 collective-permute-done.17.refs_2_.refs_3_
  102.7 4.5 %collective-permute-done.16.refs_1_.refs_2_ = bf16[1024,128]{1,0:T(8,128)(2,1)S(1)} collective-permute-done((bf16[1024,128]{1,0:T(8,128)(2,1)S(1)}, bf16[1024,128]{1,0:T(8,128)(2,1)S(1)}, u32[]{:S(2)}, u32[]{:S(2)}) %collective-permute-start.16) | collective-permute-done | bytes 262176 | tf_op jit(solution)/shard_map/ppermute | solution.py:639
  107.3 0.7 beside.1.refs_4_.refs_6_
  108.0 0.7 settle_rows.1.refs_10_
  108.7 0.1 collective-permute-start.25
  108.8 1.8 %collective-permute-start.19 = (bf16[4,1024,128]{2,1,0:T(8,128)(2,1)S(1)}, bf16[4,1024,128]{2,1,0:T(8,128)(2,1)S(1)}, u32[]{:S(2)}, u32[]{:S(2)}) collective-permute-start(bf16[4,1024,128]{2,1,0:T(8,128)(2,1)S(1)} %stack_head0.1.refs_3_), channel_id=1, source_target_pairs={{0,4},{1,5},{2,6},{3,7},{4,0},{5,1},{6,2},{7,3},{8,12},{9,13},{10,... | collective-permute-start | bytes 3145736 | tf_op jit(solution)/shard_map/ppermute | solution.py:641
  110.6 1.1 collective-permute-start.23
  111.7 0.9 collective-permute-start.22
  112.6 0.8 collective-permute-start.21
  113.4 12.0 %collective-permute-done.23.refs_9_ = bf16[1024,256]{1,0:T(8,128)(2,1)S(1)} collective-permute-done((bf16[1024,256]{1,0:T(8,128)(2,1)S(1)}, bf16[1024,256]{1,0:T(8,128)(2,1)S(1)}, u32[]{:S(2)}, u32[]{:S(2)}) %collective-permute-start.23) | collective-permute-done | bytes 524320 | tf_op jit(solution)/shard_map/ppermute | solution.py:643
  125.4 2.7 %collective-permute-done.22.refs_8_ = bf16[1024,256]{1,0:T(8,128)(2,1)S(1)} collective-permute-done((bf16[1024,256]{1,0:T(8,128)(2,1)S(1)}, bf16[1024,256]{1,0:T(8,128)(2,1)S(1)}, u32[]{:S(2)}, u32[]{:S(2)}) %collective-permute-start.22) | collective-permute-done | bytes 524320 | tf_op jit(solution)/shard_map/ppermute | solution.py:643
  128.0 10.1 %collective-permute-done.21.refs_7_ = bf16[1024,256]{1,0:T(8,128)(2,1)S(1)} collective-permute-done((bf16[1024,256]{1,0:T(8,128)(2,1)S(1)}, bf16[1024,256]{1,0:T(8,128)(2,1)S(1)}, u32[]{:S(2)}, u32[]{:S(2)}) %collective-permute-start.21) | collective-permute-done | bytes 524320 | tf_op jit(solution)/shard_map/ppermute | solution.py:643
  138.1 1.8 %project_out_2.1.refs_12_ = bf16[1024,256]{1,0:T(8,128)(2,1)S(1)} custom-call(s32[7]{0:T(128)S(1)} %stack.31.refs_0_, bf16[1024,128]{1,0:T(8,128)(2,1)S(1)} %get-tuple-element.27.refs_0_.refs_1_, bf16[1024,128]{1,0:T(8,128)(2,1)S(1)} %collective-permute-done.16.refs_1_.refs_2_, bf16[1024,128]{1,0:T(8,128)(2,1)S(1)} %collective-permute-done.17.refs_2_.refs_3_, ...), custom_call_target="tpu_custom_call" | custom-call | tf_op jit(solution)/shard_map/project_out_2/pallas_call | solution.py:112
  139.9 1.8 %project_out_1.1.refs_12_ = bf16[1024,256]{1,0:T(8,128)(2,1)S(1)} custom-call(s32[7]{0:T(128)S(1)} %stack.31.refs_0_, bf16[1024,128]{1,0:T(8,128)(2,1)S(1)} %get-tuple-element.27.refs_0_.refs_1_, bf16[1024,128]{1,0:T(8,128)(2,1)S(1)} %collective-permute-done.16.refs_1_.refs_2_, bf16[1024,128]{1,0:T(8,128)(2,1)S(1)} %collective-permute-done.17.refs_2_.refs_3_, ...), custom_call_target="tpu_custom_call" | custom-call | tf_op jit(solution)/shard_map/project_out_1/pallas_call | solution.py:112
  141.7 1.8 %project_out_3.1.refs_12_ = bf16[1024,256]{1,0:T(8,128)(2,1)S(1)} custom-call(s32[7]{0:T(128)S(1)} %stack.31.refs_0_, bf16[1024,128]{1,0:T(8,128)(2,1)S(1)} %get-tuple-element.27.refs_0_.refs_1_, bf16[1024,128]{1,0:T(8,128)(2,1)S(1)} %collective-permute-done.16.refs_1_.refs_2_, bf16[1024,128]{1,0:T(8,128)(2,1)S(1)} %collective-permute-done.17.refs_2_.refs_3_, ...), custom_call_target="tpu_custom_call" | custom-call | tf_op jit(solution)/shard_map/project_out_3/pallas_call | solution.py:112
  143.6 1.0 collective-permute-start.28
  144.6 2.3 %collective-permute-start.27 = (bf16[1024,256]{1,0:T(8,128)(2,1)S(1)}, bf16[1024,256]{1,0:T(8,128)(2,1)S(1)}, u32[]{:S(2)}, u32[]{:S(2)}) collective-permute-start(bf16[1024,256]{1,0:T(8,128)(2,1)S(1)} %project_out_1.1.refs_12_), channel_id=1, source_target_pairs={{0,24},{1,25},{2,26},{3,27},{4,28},{5,29},{6,30},{7,31},{8,0},{9,1... | collective-permute-start | bytes 1572872 | tf_op jit(solution)/shard_map/ppermute | solution.py:652
  146.9 0.8 collective-permute-start.26
  147.6 1.8 %project_out_0.1.refs_4_ = bf16[1024,256]{1,0:T(8,128)(2,1)S(1)} custom-call(s32[7]{0:T(128)S(1)} %stack.31.refs_0_, bf16[1024,128]{1,0:T(8,128)(2,1)S(1)} %get-tuple-element.27.refs_0_.refs_1_, bf16[1024,128]{1,0:T(8,128)(2,1)S(1)} %collective-permute-done.16.refs_1_.refs_2_, bf16[1024,128]{1,0:T(8,128)(2,1)S(1)} %collective-permute-done.17.refs_2_.refs_3_, ...), custom_call_target="tpu_custom_call" | custom-call | tf_op jit(solution)/shard_map/project_out_0/pallas_call | solution.py:112
  149.4 10.1 %collective-permute-done.28.refs_3_ = bf16[1024,256]{1,0:T(8,128)(2,1)S(1)} collective-permute-done((bf16[1024,256]{1,0:T(8,128)(2,1)S(1)}, bf16[1024,256]{1,0:T(8,128)(2,1)S(1)}, u32[]{:S(2)}, u32[]{:S(2)}) %collective-permute-start.28) | collective-permute-done | bytes 524320 | tf_op jit(solution)/shard_map/ppermute | solution.py:652
  159.6 9.7 %collective-permute-done.27.refs_2_ = bf16[1024,256]{1,0:T(8,128)(2,1)S(1)} collective-permute-done((bf16[1024,256]{1,0:T(8,128)(2,1)S(1)}, bf16[1024,256]{1,0:T(8,128)(2,1)S(1)}, u32[]{:S(2)}, u32[]{:S(2)}) %collective-permute-start.27) | collective-permute-done | bytes 524320 | tf_op jit(solution)/shard_map/ppermute | solution.py:652
  169.2 0.8 collective-permute-done.26.refs_1_
  170.0 1.1 add_residual.1
  (60 shorter events, 0.8 us)
Async XLA Ops:
  0.0 25.0 %collective-permute-start = (bf16[2048,256]{1,0:T(8,128)(2,1)}, bf16[2048,256]{1,0:T(8,128)(2,1)S(1)}, u32[]{:S(2)}, u32[]{:S(2)}) collective-permute-start(bf16[2048,256]{1,0:T(8,128)(2,1)} %refs_1_.3), channel_id=1, source_target_pairs={{0,32},{32,0},{1,33},{33,1},{2,34},{34,2},{3,35},{35,3},{4,36},{36... | collective-permute-start | bytes 3145736 | tf_op jit(solution)/shard_map/ppermute | solution.py:606
  1.7 1.3 copy-start.4
  3.1 1.0 copy-start.13
  4.1 0.8 copy-start.18
  7.6 28.4 %all-to-all-start = ((bf16[16,2,160,128]{3,2,1,0:T(8,128)(2,1)}), bf16[16,2,160,128]{3,2,1,0:T(8,128)(2,1)S(1)}, u32[]{:S(2)}, u32[]{:S(2)}) async-start(bf16[16,2,160,128]{3,2,1,0:T(8,128)(2,1)} %pack_weights.1.refs_2_), calls=%async_computation | async-start | bytes 2621440 | tf_op jit(solution)/shard_map/all_to_all | solution.py:608
  15.5 10.5 %copy-start.5 = (bf16[2048,256]{1,0:T(8,128)(2,1)S(1)}, bf16[2048,256]{1,0:T(8,128)(2,1)}, u32[]{:S(2)}) copy-start(bf16[2048,256]{1,0:T(8,128)(2,1)} %refs_1_.3) | copy-start | bytes 3145732
  22.8 0.8 copy-start.11
  25.0 1.0 copy-start.6
  26.0 1.2 copy-start.7
  28.9 16.4 %collective-permute-start.8 = (bf16[2,1024,256]{2,1,0:T(8,128)(2,1)}, bf16[2,1024,256]{2,1,0:T(8,128)(2,1)}, u32[]{:S(2)}, u32[]{:S(2)}) collective-permute-start(bf16[2,1024,256]{2,1,0:T(8,128)(2,1)} %get-tuple-element.22), channel_id=1, source_target_pairs={{0,64},{64,0},{1,65},{65,1},{2,66},{66,2},{3,67},{67,3},{4,68},{68... | collective-permute-start | bytes 3145736 | tf_op jit(solution)/shard_map/ppermute | solution.py:620
  36.1 6.3 %collective-permute-start.4 = (bf16[16,32,128]{2,1,0:T(8,128)(2,1)S(1)}, bf16[16,32,128]{2,1,0:T(8,128)(2,1)S(1)}, u32[]{:S(2)}, u32[]{:S(2)}) collective-permute-start(bf16[16,32,128]{2,1,0:T(8,128)(2,1)S(1)} %get-tuple-element.21), channel_id=1, source_target_pairs={{0,36},{1,37},{2,38},{3,39},{4,32},{5,33},{6,34},{7,35},{8,44},{9,... | collective-permute-start | bytes 393224 | tf_op jit(solution)/shard_map/ppermute | solution.py:615
  38.3 17.0 %collective-permute-start.2 = (bf16[16,128,128]{2,1,0:T(8,128)(2,1)S(1)}, bf16[16,128,128]{2,1,0:T(8,128)(2,1)S(1)}, u32[]{:S(2)}, u32[]{:S(2)}) collective-permute-start(bf16[16,128,128]{2,1,0:T(8,128)(2,1)S(1)} %get-tuple-element.20.refs_2_), channel_id=1, source_target_pairs={{0,32},{32,0},{1,33},{33,1},{2,34},{34,2},{3,35},{35,3},{4,36},{36... | collective-permute-start | bytes 1572872 | tf_op jit(solution)/shard_map/ppermute | solution.py:614
  42.4 14.1 %copy-start.19 = (bf16[10240]{0:T(1024)(128)(2,1)S(1)}, bf16[10240]{0:T(1024)(128)(2,1)}, u32[]{:S(2)}) copy-start(bf16[10240]{0:T(1024)(128)(2,1)} %param.16) | copy-start | bytes 61444
  42.4 14.1 %copy-start.9 = (f32[4,256,128]{2,1,0:T(8,128)S(1)}, f32[4,256,128]{2,1,0:T(8,128)}, u32[]{:S(2)}) copy-start(f32[4,256,128]{2,1,0:T(8,128)} %constant.80.clone.refs_11_) | copy-start | bytes 1572868
  42.4 14.1 %copy-start.10 = (f32[4,256,128]{2,1,0:T(8,128)S(1)}, f32[4,256,128]{2,1,0:T(8,128)}, u32[]{:S(2)}) copy-start(f32[4,256,128]{2,1,0:T(8,128)} %constant.79.clone.refs_10_) | copy-start | bytes 1572868
  42.4 14.1 %copy-start.14 = (bf16[4,256,128]{2,1,0:T(8,128)(2,1)S(1)}, bf16[4,256,128]{2,1,0:T(8,128)(2,1)}, u32[]{:S(2)}) copy-start(bf16[4,256,128]{2,1,0:T(8,128)(2,1)} %constant.77.clone.refs_9_) | copy-start | bytes 786436
  42.4 14.1 %copy-start.17 = (bf16[128,256]{1,0:T(8,128)(2,1)S(1)}, bf16[128,256]{1,0:T(8,128)(2,1)}, u32[]{:S(2)}) copy-start(bf16[128,256]{1,0:T(8,128)(2,1)} %constant.78.clone.refs_7_) | copy-start | bytes 196612
  42.5 12.9 %collective-permute-start.5 = (bf16[16,128,128]{2,1,0:T(8,128)(2,1)S(1)}, bf16[16,128,128]{2,1,0:T(8,128)(2,1)S(1)}, u32[]{:S(2)}, u32[]{:S(2)}) collective-permute-start(bf16[16,128,128]{2,1,0:T(8,128)(2,1)S(1)} %cut_second.1), channel_id=1, source_target_pairs={{0,36},{1,37},{2,38},{3,39},{4,32},{5,33},{6,34},{7,35},{8,44},{9,... | collective-permute-start | bytes 1572872 | tf_op jit(solution)/shard_map/ppermute | solution.py:619
  44.7 10.1 %collective-permute-start.11 = (bf16[2,16,32,128]{3,2,1,0:T(8,128)(2,1)S(1)}, bf16[2,16,32,128]{3,2,1,0:T(8,128)(2,1)S(1)}, u32[]{:S(2)}, u32[]{:S(2)}) collective-permute-start(bf16[2,16,32,128]{3,2,1,0:T(8,128)(2,1)S(1)} %near_kv.1.refs_1_.refs_3_.refs_2_), channel_id=1, source_target_pairs={{0,32},{32,0},{1,33},{33,1},{2,34},{34,2},{3,35},{35,3},{4,36},{36... | collective-permute-start | bytes 786440 | tf_op jit(solution)/shard_map/ppermute | solution.py:617
  46.8 1.0 copy-start.2
  47.8 23.4 %collective-permute-start.9 = (bf16[2,1024,256]{2,1,0:T(8,128)(2,1)S(1)}, bf16[2,1024,256]{2,1,0:T(8,128)(2,1)S(1)}, u32[]{:S(2)}, u32[]{:S(2)}) collective-permute-start(bf16[2,1024,256]{2,1,0:T(8,128)(2,1)S(1)} %get-tuple-element.24), channel_id=1, source_target_pairs={{0,16},{1,17},{2,18},{3,19},{4,20},{5,21},{6,22},{7,23},{8,24},{9,... | collective-permute-start | bytes 3145736 | tf_op jit(solution)/shard_map/ppermute | solution.py:630
  48.5 6.3 %collective-permute-start.10 = (bf16[2,16,32,128]{3,2,1,0:T(8,128)(2,1)S(1)}, bf16[2,16,32,128]{3,2,1,0:T(8,128)(2,1)S(1)}, u32[]{:S(2)}, u32[]{:S(2)}) collective-permute-start(bf16[2,16,32,128]{3,2,1,0:T(8,128)(2,1)S(1)} %near_kv.1.refs_1_.refs_3_.refs_2_), channel_id=1, source_target_pairs={{0,64},{64,0},{1,65},{65,1},{2,66},{66,2},{3,67},{67,3},{4,68},{68... | collective-permute-start | bytes 786440 | tf_op jit(solution)/shard_map/ppermute | solution.py:618
  54.8 1.5 collective-permute-start.12
  54.8 10.4 %collective-permute-start.1 = (bf16[16,128,128]{2,1,0:T(8,128)(2,1)S(1)}, bf16[16,128,128]{2,1,0:T(8,128)(2,1)S(1)}, u32[]{:S(2)}, u32[]{:S(2)}) collective-permute-start(bf16[16,128,128]{2,1,0:T(8,128)(2,1)S(1)} %get-tuple-element.20.refs_2_), channel_id=1, source_target_pairs={{0,64},{64,0},{1,65},{65,1},{2,66},{66,2},{3,67},{67,3},{4,68},{68... | collective-permute-start | bytes 1572872 | tf_op jit(solution)/shard_map/ppermute | solution.py:626
  55.3 15.8 %collective-permute-start.3 = (bf16[16,128,128]{2,1,0:T(8,128)(2,1)S(1)}, bf16[16,128,128]{2,1,0:T(8,128)(2,1)S(1)}, u32[]{:S(2)}, u32[]{:S(2)}) collective-permute-start(bf16[16,128,128]{2,1,0:T(8,128)(2,1)S(1)} %collective-permute-done.2.refs_4_), channel_id=1, source_target_pairs={{0,64},{64,0},{1,65},{65,1},{2,66},{66,2},{3,67},{67,3},{4,68},{68... | collective-permute-start | bytes 1572872 | tf_op jit(solution)/shard_map/ppermute | solution.py:626
  55.4 15.7 %collective-permute-start.7 = (bf16[16,128,128]{2,1,0:T(8,128)(2,1)S(1)}, bf16[16,128,128]{2,1,0:T(8,128)(2,1)S(1)}, u32[]{:S(2)}, u32[]{:S(2)}) collective-permute-start(bf16[16,128,128]{2,1,0:T(8,128)(2,1)S(1)} %collective-permute-done.5.refs_12_.refs_6_), channel_id=1, source_target_pairs={{0,32},{32,0},{1,33},{33,1},{2,34},{34,2},{3,35},{35,3},{4,36},{36... | collective-permute-start | bytes 1572872 | tf_op jit(solution)/shard_map/ppermute | solution.py:625
  56.3 14.8 %collective-permute-start.6 = (bf16[16,128,128]{2,1,0:T(8,128)(2,1)S(1)}, bf16[16,128,128]{2,1,0:T(8,128)(2,1)S(1)}, u32[]{:S(2)}, u32[]{:S(2)}) collective-permute-start(bf16[16,128,128]{2,1,0:T(8,128)(2,1)S(1)} %collective-permute-done.5.refs_12_.refs_6_), channel_id=1, source_target_pairs={{0,64},{64,0},{1,65},{65,1},{2,66},{66,2},{3,67},{67,3},{4,68},{68... | collective-permute-start | bytes 1572872 | tf_op jit(solution)/shard_map/ppermute | solution.py:626
  65.2 5.9 %copy-start.3 = (bf16[2,1024,256]{2,1,0:T(8,128)(2,1)S(1)}, bf16[2,1024,256]{2,1,0:T(8,128)(2,1)}, u32[]{:S(2)}) copy-start(bf16[2,1024,256]{2,1,0:T(8,128)(2,1)} %copy-done.2) | copy-start | bytes 3145732
  65.2 5.9 %collective-permute-start.13 = (bf16[512,128]{1,0:T(8,128)(2,1)S(1)}, bf16[512,128]{1,0:T(8,128)(2,1)S(1)}, u32[]{:S(2)}, u32[]{:S(2)}) collective-permute-start(bf16[512,128]{1,0:T(8,128)(2,1)S(1)} %keys_values.1.refs_0_.refs_1_), channel_id=1, source_target_pairs={{0,1},{1,0},{2,3},{3,2},{4,5},{5,4},{6,7},{7,6},{8,9},{9,8},{10,11... | collective-permute-start | bytes 393224 | tf_op jit(solution)/shard_map/ppermute | solution.py:627
  71.2 36.7 %collective-permute-start.24 = (bf16[2,1024,256]{2,1,0:T(8,128)(2,1)S(1)}, bf16[2,1024,256]{2,1,0:T(8,128)(2,1)S(1)}, u32[]{:S(2)}, u32[]{:S(2)}) collective-permute-start(bf16[2,1024,256]{2,1,0:T(8,128)(2,1)S(1)} %second_rows.1.refs_1_), channel_id=1, source_target_pairs={{0,8},{1,9},{2,10},{3,11},{4,12},{5,13},{6,14},{7,15},{8,0},{9,1},... | collective-permute-start | bytes 3145736 | tf_op jit(solution)/shard_map/ppermute | solution.py:644
  71.3 14.1 %copy-start.8 = (bf16[4,2,128,256]{3,2,1,0:T(8,128)(2,1)S(1)}, bf16[4,2,128,256]{3,2,1,0:T(8,128)(2,1)}, u32[]{:S(2)}) copy-start(bf16[4,2,128,256]{3,2,1,0:T(8,128)(2,1)} %constant.76.clone.refs_4_) | copy-start | bytes 1572868
  71.4 15.3 %collective-permute-start.14 = (bf16[1,16,128,128]{3,2,1,0:T(8,128)(2,1)S(1)}, bf16[1,16,128,128]{3,2,1,0:T(8,128)(2,1)S(1)}, u32[]{:S(2)}, u32[]{:S(2)}) collective-permute-start(bf16[1,16,128,128]{3,2,1,0:T(8,128)(2,1)S(1)} %late_q.1.refs_8_), channel_id=1, source_target_pairs={{0,64},{64,0},{1,65},{65,1},{2,66},{66,2},{3,67},{67,3},{4,68},{68... | collective-permute-start | bytes 1572872 | tf_op jit(solution)/shard_map/ppermute | solution.py:637
  71.5 13.9 %collective-permute-start.15 = (bf16[2,512,128]{2,1,0:T(8,128)(2,1)S(1)}, bf16[2,512,128]{2,1,0:T(8,128)(2,1)S(1)}, u32[]{:S(2)}, u32[]{:S(2)}) collective-permute-start(bf16[2,512,128]{2,1,0:T(8,128)(2,1)S(1)} %stack_kv.1.refs_2_), channel_id=1, source_target_pairs={{0,2},{1,3},{2,0},{3,1},{4,6},{5,7},{6,4},{7,5},{8,10},{9,11},{10,... | collective-permute-start | bytes 786440 | tf_op jit(solution)/shard_map/ppermute | solution.py:629
  75.5 5.8 %copy-start = (bf16[4,256,8192]{2,1,0:T(8,128)(2,1)S(1)}, bf16[4,256,8192]{2,1,0:T(8,128)(2,1)}, u32[]{:S(2)}) copy-start(bf16[4,256,8192]{2,1,0:T(8,128)(2,1)} %param.13) | copy-start | bytes 50331652
  81.2 5.8 %copy-start.1 = (bf16[4,256,8192]{2,1,0:T(8,128)(2,1)S(1)}, bf16[4,256,8192]{2,1,0:T(8,128)(2,1)}, u32[]{:S(2)}) copy-start(bf16[4,256,8192]{2,1,0:T(8,128)(2,1)} %param.13) | copy-start | bytes 50331652
  85.4 1.8 %copy-start.15 = (f32[256,128]{1,0:T(8,128)S(1)}, f32[256,128]{1,0:T(8,128)}, u32[]{:S(2)}) copy-start(f32[256,128]{1,0:T(8,128)} %constant.82.clone.refs_8_) | copy-start | bytes 393220
  85.4 1.8 %copy-start.16 = (f32[256,128]{1,0:T(8,128)S(1)}, f32[256,128]{1,0:T(8,128)}, u32[]{:S(2)}) copy-start(f32[256,128]{1,0:T(8,128)} %constant.81.clone.refs_7_) | copy-start | bytes 393220
  91.8 9.2 %collective-permute-start.18 = (bf16[1024,128]{1,0:T(8,128)(2,1)S(1)}, bf16[1024,128]{1,0:T(8,128)(2,1)S(1)}, u32[]{:S(2)}, u32[]{:S(2)}) collective-permute-start(bf16[1024,128]{1,0:T(8,128)(2,1)S(1)} %get-tuple-element.27.refs_0_.refs_1_), channel_id=1, source_target_pairs={{0,3},{1,0},{2,1},{3,2},{4,7},{5,4},{6,5},{7,6},{8,11},{9,8},{10,9... | collective-permute-start | bytes 786440 | tf_op jit(solution)/shard_map/ppermute | solution.py:639
  91.9 10.8 %collective-permute-start.17 = (bf16[1024,128]{1,0:T(8,128)(2,1)S(1)}, bf16[1024,128]{1,0:T(8,128)(2,1)S(1)}, u32[]{:S(2)}, u32[]{:S(2)}) collective-permute-start(bf16[1024,128]{1,0:T(8,128)(2,1)S(1)} %get-tuple-element.27.refs_0_.refs_1_), channel_id=1, source_target_pairs={{0,2},{1,3},{2,0},{3,1},{4,6},{5,7},{6,4},{7,5},{8,10},{9,11},{10,... | collective-permute-start | bytes 786440 | tf_op jit(solution)/shard_map/ppermute | solution.py:639
  93.6 13.6 %collective-permute-start.16 = (bf16[1024,128]{1,0:T(8,128)(2,1)S(1)}, bf16[1024,128]{1,0:T(8,128)(2,1)S(1)}, u32[]{:S(2)}, u32[]{:S(2)}) collective-permute-start(bf16[1024,128]{1,0:T(8,128)(2,1)S(1)} %get-tuple-element.27.refs_0_.refs_1_), channel_id=1, source_target_pairs={{0,1},{1,2},{2,3},{3,0},{4,5},{5,6},{6,7},{7,4},{8,9},{9,10},{10,1... | collective-permute-start | bytes 786440 | tf_op jit(solution)/shard_map/ppermute | solution.py:639
  93.9 13.4 %collective-permute-start.20 = (bf16[1024,128]{1,0:T(8,128)(2,1)S(1)}, bf16[1024,128]{1,0:T(8,128)(2,1)S(1)}, u32[]{:S(2)}, u32[]{:S(2)}) collective-permute-start(bf16[1024,128]{1,0:T(8,128)(2,1)S(1)} %get-tuple-element.28.refs_1_), channel_id=1, source_target_pairs={{0,4},{1,5},{2,6},{3,7},{4,0},{5,1},{6,2},{7,3},{8,12},{9,13},{10,... | collective-permute-start | bytes 786440 | tf_op jit(solution)/shard_map/ppermute | solution.py:642
  108.7 29.4 %collective-permute-start.25 = (bf16[4,1024,256]{2,1,0:T(8,128)(2,1)S(1)}, bf16[4,1024,256]{2,1,0:T(8,128)(2,1)S(1)}, u32[]{:S(2)}, u32[]{:S(2)}) collective-permute-start(bf16[4,1024,256]{2,1,0:T(8,128)(2,1)S(1)} %settle_rows.1.refs_10_), channel_id=1, source_target_pairs={{0,64},{64,0},{1,65},{65,1},{2,66},{66,2},{3,67},{67,3},{4,68},{68... | collective-permute-start | bytes 6291464 | tf_op jit(solution)/shard_map/ppermute | solution.py:645
  108.8 29.3 %collective-permute-start.19 = (bf16[4,1024,128]{2,1,0:T(8,128)(2,1)S(1)}, bf16[4,1024,128]{2,1,0:T(8,128)(2,1)S(1)}, u32[]{:S(2)}, u32[]{:S(2)}) collective-permute-start(bf16[4,1024,128]{2,1,0:T(8,128)(2,1)S(1)} %stack_head0.1.refs_3_), channel_id=1, source_target_pairs={{0,4},{1,5},{2,6},{3,7},{4,0},{5,1},{6,2},{7,3},{8,12},{9,13},{10,... | collective-permute-start | bytes 3145736 | tf_op jit(solution)/shard_map/ppermute | solution.py:641
  110.6 14.8 %collective-permute-start.23 = (bf16[1024,256]{1,0:T(8,128)(2,1)S(1)}, bf16[1024,256]{1,0:T(8,128)(2,1)S(1)}, u32[]{:S(2)}, u32[]{:S(2)}) collective-permute-start(bf16[1024,256]{1,0:T(8,128)(2,1)S(1)} %beside.1.refs_4_.refs_6_), channel_id=1, source_target_pairs={{0,3},{1,0},{2,1},{3,2},{4,7},{5,4},{6,5},{7,6},{8,11},{9,8},{10,9... | collective-permute-start | bytes 1572872 | tf_op jit(solution)/shard_map/ppermute | solution.py:643
  111.7 16.4 %collective-permute-start.22 = (bf16[1024,256]{1,0:T(8,128)(2,1)S(1)}, bf16[1024,256]{1,0:T(8,128)(2,1)S(1)}, u32[]{:S(2)}, u32[]{:S(2)}) collective-permute-start(bf16[1024,256]{1,0:T(8,128)(2,1)S(1)} %beside.1.refs_4_.refs_6_), channel_id=1, source_target_pairs={{0,2},{1,3},{2,0},{3,1},{4,6},{5,7},{6,4},{7,5},{8,10},{9,11},{10,... | collective-permute-start | bytes 1572872 | tf_op jit(solution)/shard_map/ppermute | solution.py:643
  112.6 25.5 %collective-permute-start.21 = (bf16[1024,256]{1,0:T(8,128)(2,1)S(1)}, bf16[1024,256]{1,0:T(8,128)(2,1)S(1)}, u32[]{:S(2)}, u32[]{:S(2)}) collective-permute-start(bf16[1024,256]{1,0:T(8,128)(2,1)S(1)} %beside.1.refs_4_.refs_6_), channel_id=1, source_target_pairs={{0,1},{1,2},{2,3},{3,0},{4,5},{5,6},{6,7},{7,4},{8,9},{9,10},{10,1... | collective-permute-start | bytes 1572872 | tf_op jit(solution)/shard_map/ppermute | solution.py:643
  143.5 26.4 %copy-start.12 = (bf16[1024,256]{1,0:T(8,128)(2,1)S(1)}, bf16[1024,256]{1,0:T(8,128)(2,1)}, u32[]{:S(2)}) copy-start(bf16[1024,256]{1,0:T(8,128)(2,1)} %copy-done.11) | copy-start | bytes 1572868
  143.6 16.0 %collective-permute-start.28 = (bf16[1024,256]{1,0:T(8,128)(2,1)S(1)}, bf16[1024,256]{1,0:T(8,128)(2,1)S(1)}, u32[]{:S(2)}, u32[]{:S(2)}) collective-permute-start(bf16[1024,256]{1,0:T(8,128)(2,1)S(1)} %project_out_3.1.refs_12_), channel_id=1, source_target_pairs={{0,8},{1,9},{2,10},{3,11},{4,12},{5,13},{6,14},{7,15},{8,16},{9,17... | collective-permute-start | bytes 1572872 | tf_op jit(solution)/shard_map/ppermute | solution.py:652
  144.6 24.6 %collective-permute-start.27 = (bf16[1024,256]{1,0:T(8,128)(2,1)S(1)}, bf16[1024,256]{1,0:T(8,128)(2,1)S(1)}, u32[]{:S(2)}, u32[]{:S(2)}) collective-permute-start(bf16[1024,256]{1,0:T(8,128)(2,1)S(1)} %project_out_1.1.refs_12_), channel_id=1, source_target_pairs={{0,24},{1,25},{2,26},{3,27},{4,28},{5,29},{6,30},{7,31},{8,0},{9,1... | collective-permute-start | bytes 1572872 | tf_op jit(solution)/shard_map/ppermute | solution.py:652
  146.9 23.1 %collective-permute-start.26 = (bf16[1024,256]{1,0:T(8,128)(2,1)S(1)}, bf16[1024,256]{1,0:T(8,128)(2,1)S(1)}, u32[]{:S(2)}, u32[]{:S(2)}) collective-permute-start(bf16[1024,256]{1,0:T(8,128)(2,1)S(1)} %project_out_2.1.refs_12_), channel_id=1, source_target_pairs={{0,16},{1,17},{2,18},{3,19},{4,20},{5,21},{6,22},{7,23},{8,24},{9,... | collective-permute-start | bytes 1572872 | tf_op jit(solution)/shard_map/ppermute | solution.py:652

commit v5 on v4

--- a/solution.py
+++ b/solution.py
@@ -198,28 +198,6 @@
         yield ref, 1, 2 * core + 1 - here, 1 - y
 
 
-BLOCKS = [pltpu.VMEM((4, 256, D), BF), pltpu.SemaphoreType.DMA((4,))]
-
-
-def block_copy(x, buf, sem, i):
-    return pltpu.make_async_copy(x.at[pl.ds(i * 256, 256)], buf.at[i], sem.at[i])
-
-
-def start_blocks(x, buf, sem):
-    for i in range(4):
-        block_copy(x, buf, sem, i).start()
-
-
-def project_block(x, buf, sem, ws, i, width):
-    block_copy(x, buf, sem, i).wait()
-    sums = None
-    for j in range(4):
-        w = ws[j].reshape(2048, width)
-        part = dot(buf[i, :, j * 2048 : (j + 1) * 2048], w)
-        sums = part if sums is None else sums + part
-    return sums
-
-
 def norm_body(idx, x, out, residual, buf, sem):
     columns = pl.ds(pl.multiple_of(idx[TP] * 256, 256), 256)
     copies = [
@@ -256,56 +234,80 @@
     )(idx, x)
 
 
-def kv_body(idx, x, own, mate, side, far, norm, unpack, bias, bsel, cos, sin, kv, ws, buf, sem):
-    start_blocks(x, buf, sem)
-    for ref, i, block, y in row_groups(idx, own, mate, side, far):
+def kv_sums(idx, x, groups, unpack, ws):
+    acc = None
+    for k, (ref, i, block, y) in enumerate(groups):
         both = dot(ref[i].reshape(512, 128), unpack[...]).astype(BF).reshape(4, 4, 32, 256)
         for z in range(4):
-            ws[block, z, y, :, :32, :] = both[z, :, :, :128]
-            ws[block, z, y, :, 32:, :] = both[z, :, :, 128:]
+            ws[k, z, :, :32, :] = both[z, :, :, :128]
+            ws[k, z, :, 32:, :] = both[z, :, :, 128:]
+        for z in range(4):
+            start = pl.multiple_of(block * 2048 + z * 512 + y * 256, 256)
+            term = dot(x[:, pl.ds(start, 256)], ws[k, z].reshape(256, 128))
+            acc = term if acc is None else acc + term
+    return acc
+
+
+def kv_early_body(idx, x, own, mate, unpack, out, ws):
+    groups = list(row_groups(idx, own, mate, own, mate))[:4]
+    out[...] = kv_sums(idx, x, groups, unpack, ws)
+
+
+def kv_body(idx, x, early, side, far, norm, unpack, bias, bsel, cos, sin, kv, ws):
+    groups = list(row_groups(idx, side, far, side, far))[4:]
+    acc = early[...] + kv_sums(idx, x, groups, unpack, ws)
     g = idx[KV_HEAD]
     part = idx[X]
     base = jnp.concatenate([bias[pl.ds(64 + g, 1), :], bias[pl.ds(72 + g, 1), :]], 1)
     base = dot(jnp.broadcast_to(base, (8, 256)).astype(BF), bsel[part])[0:1]
     cosine = cos[part]
     sine = sin[part]
+    acc = acc * norm[...] + base
     lane = lax.broadcasted_iota(jnp.int32, (SPAN, 128), 1)
-    for i in range(4):
-        rows = slice(i * SPAN, (i + 1) * SPAN)
-        sums = project_block(x, buf, sem, ws, i, 128) * norm[rows, :] + base
-        turned = pltpu.roll(sums, 64, 1)
-        place = slice((i % 2) * SPAN, (i % 2) * SPAN + SPAN)
-        if i < 2:
-            kv[place, :] = (sums * cosine + turned * sine).astype(BF)
-        else:
-            right = (turned * cosine + sums * sine).astype(BF)
-            kv[place, :] = jnp.where(lane < 64, kv[place, :], right)
+    for i in range(2):
+        a = acc[i * 256 : (i + 1) * 256]
+        b = acc[512 + i * 256 : 512 + (i + 1) * 256]
+        left = a * cosine + pltpu.roll(a, 64, 1) * sine
+        right = pltpu.roll(b, 64, 1) * cosine + b * sine
+        kv[i * 256 : (i + 1) * 256] = jnp.where(lane < 64, left, right).astype(BF)
+
+
+KV_ROWS = pltpu.VMEM((4, 4, 4, 64, 128), BF)
+
+
+def early_keys_values(idx, x, ws, tab, after):
+    return call(
+        kv_early_body,
+        "keys_values_early",
+        [SM] + [VM] * 4,
+        shape((1024, 128), F32),
+        VM,
+        cost(0),
+        [KV_ROWS],
+        after,
+    )(idx, x, *ws, tab["unpack"])
 
 
 def keys_values(idx, x, ws, norm, tab, bias, after):
     return call(
         kv_body,
         "keys_values",
-        [SM, AN] + [VM] * 10,
+        [SM] + [VM] * 10,
         shape((512, 128)),
         VM,
         cost(0),
-        [
-            pltpu.VMEM((4, 4, 2, 4, 64, 128), BF),
-            *BLOCKS,
-        ],
+        [KV_ROWS],
         after,
-        50,
     )(
         idx, x, *ws, norm, tab["unpack"], bias, tab["bias_sel"], tab["k_cos"], tab["k_sin"]
     )
 
 
-def join_body(idx, kv, first, second, gather, keys, values):
+def join_body(idx, p0, p1, p2, p3, gather, keys, values):
     for half in range(2):
         both = jnp.zeros((512, 256), F32)
-        for k, piece in enumerate((kv, first, second.at[0], second.at[1])):
-            both += dot(piece[...], gather[idx[X] ^ k, half])
+        for k, piece in enumerate((p0, p1, p2, p3)):
+            both += dot(piece[...], gather[(idx[X] + 4 - k) % 4, half])
         keys[half * 512 : (half + 1) * 512] = both[:, :128].astype(BF)
         values[half * 512 : (half + 1) * 512] = both[:, 128:].astype(BF)
 
@@ -314,7 +316,7 @@
     return call(
         join_body,
         "join_keys_values",
-        [SM] + [VM] * 4,
+        [SM] + [VM] * 5,
         [shape((1024, 128))] * 2,
         [VM] * 2,
         cost(0),
@@ -336,13 +338,13 @@
     return acc
 
 
-def early_body(idx, x, own, mate, side, far, got, got_mate, out, ws):
+def early_body(idx, x, own, mate, both, mates, out, ws):
     p, s, y = idx[PAIR], idx[SIDE], idx[Y_HI]
     acc = half_block(x, own, 2 * p + s, y) + half_block(x, mate, 2 * (1 - p) + s, y)
-    for k, (here, there) in enumerate(((side, got), (far, got_mate))):
+    for k, rows in enumerate((both, mates)):
         for z in range(4):
-            ws[k, z, y] = run_rows(here, z)
-            ws[k, z, 1 - y] = run_rows(there, z)
+            ws[k, z, y] = run_rows(rows.at[0], z)
+            ws[k, z, 1 - y] = run_rows(rows.at[1], z)
         core = p if k == 0 else 1 - p
         start = pl.multiple_of((2 * core + 1 - s) * 2048, 2048)
         acc += dot(x[:, pl.ds(start, 2048)], ws[k].reshape(2048, 256))
@@ -353,7 +355,7 @@
     return call(
         early_body,
         "project_early",
-        [SM] + [VM] * 7,
+        [SM] + [VM] * 5,
         shape((1024, 256), F32),
         VM,
         cost(0),
@@ -483,7 +485,9 @@
     )(idx, keep, recv)
 
 
-def second_body(stay, came, out):
+def second_body(stay, came, near, out):
+    near[0] = stay[0]
+    near[1] = came[0]
     out[0] = stay[1]
     out[1] = came[1]
 
@@ -493,44 +497,24 @@
         second_body,
         "second_rows",
         [VM, VM],
-        shape((2, 1024, 256)),
-        VM,
+        [shape((2, 1024, 256))] * 2,
+        [VM] * 2,
         cost(0),
         after=after,
     )(stay, came)
 
 
-def settle_body(idx, stay, came, last, out):
-    z = idx[Z]
-    out[z] = stay[0]
-    out[z ^ 2] = came[0]
-    out[z ^ 1] = last[0]
-    out[z ^ 3] = last[1]
-
-
-def settle(idx, stay, came, last, after):
-    return call(
-        settle_body,
-        "settle_rows",
-        [SM, VM, VM, VM],
-        shape((4, 1024, 256)),
-        VM,
-        cost(0),
-        after=after,
-    )(idx, stay, came, last)
-
-
-def w_rows(idx, own, other, r, part):
-    z = (idx[Z] + 4 - r) % 4
+def w_rows(w, other, i, part):
     rows = []
     for h in range(2):
-        for w in (own, other):
-            rows.append(w[z, pl.ds(pl.multiple_of(part * 256 + h * 128, 128), 128), :])
+        for ref in (w, other):
+            rows.append(ref[i, pl.ds(pl.multiple_of(part * 256 + h * 128, 128), 128), :])
     return jnp.concatenate(rows, 0)
 
 
 def out_body(r, idx, h0, h1, h2, h3, there, a0, a1, a2, a3, own, other, out):
     same = idx[Y_HI] == idx[PAIR]
+    i = r // 2 if r % 2 == 0 else (idx[Z] + (r + 1) // 2) % 2
     acc = None
     for k, (here, both) in enumerate(zip((h0, h1, h2, h3), (a0, a1, a2, a3))):
         near = here[...]
@@ -538,7 +522,7 @@
         lanes = jnp.concatenate(
             [jnp.where(same, near, far), jnp.where(same, far, near), both[...]], 1
         )
-        term = dot(lanes, w_rows(idx, own, other, r, (idx[X] + 4 - k) % 4))
+        term = dot(lanes, w_rows(own, other, i, (idx[X] + 4 - k) % 4))
         acc = term if acc is None else acc + term
     out[...] = acc.astype(BF)
 
@@ -613,41 +597,53 @@
     kv_other, q_own = cut_first(blocks, [keep])
     q_side = lax.ppermute(q_own, "side", SWAP)
     kv_got = lax.ppermute(kv_other, ("side", "tp"), DIAGONAL)
-    kv_own = near_rows(0, 32, blocks, kv_got, [q_own], "near_kv")
+    stay, leave = route(idx, keep, lax.ppermute(send, "pair", SWAP), [q_own])
+    kv_own = near_rows(0, 32, blocks, kv_got, [stay], "near_kv")
     kv_side = lax.ppermute(kv_own, "side", SWAP)
     kv_mate = lax.ppermute(kv_own, "pair", SWAP)
-    q_got = lax.ppermute(cut_second(blocks, [kv_own]), ("side", "tp"), DIAGONAL)
-    stay, leave = route(idx, keep, lax.ppermute(send, "pair", SWAP), [kv_own])
-    kv_far = lax.ppermute(kv_side, "pair", SWAP)
+    q_other = cut_second(blocks, [kv_own])
+    q_got = lax.ppermute(q_other, ("side", "tp"), DIAGONAL)
+    kv_early = early_keys_values(idx, x, (kv_own, kv_mate), tab, [q_other])
+    kv_late = stack("late_kv", [kv_side], [kv_early])
+    kv_far = lax.ppermute(kv_late, "pair", SWAP).reshape(kv_side.shape)
+    q_mate = lax.ppermute(q_own, "pair", SWAP)
+    q_both = stack("late_queries", [q_side, q_got], [kv_late])
+    q_mates = lax.ppermute(q_both, "pair", SWAP)
     kv_piece = keys_values(
-        idx, x, (kv_own, kv_mate, kv_side, kv_far), norm, tab, bias, [q_got, stay]
+        idx, x, (kv_early, kv_side, kv_far), norm, tab, bias, [q_mate, q_mates]
     )
     got_side = lax.ppermute(q_got, "side", SWAP)
-    q_mates = [lax.ppermute(q, "pair", SWAP) for q in (q_own, q_side, q_got)]
-    first = lax.ppermute(kv_piece, "tp", flip(1))
-    pieces = stack("stack_kv", [kv_piece, first], [*q_mates, got_side])
-    second = lax.ppermute(pieces, "tp", flip(2))
+    pieces = [kv_piece] + [
+        lax.ppermute(kv_piece, "tp", shift(0, 0, r)) for r in range(1, 4)
+    ]
     came = lax.ppermute(leave, "tp", flip(16))
-    hop = second_hop(stay, came, [pieces])
-    late = stack("late_q", [got_side], [hop])
     early = early_heads(
-        idx, x, (q_own, q_mates[0], q_side, q_mates[1], q_got, q_mates[2]), [late]
-    )
-    keys, values = join_kv(idx, (kv_piece, first, second), tab, [early])
-    ws = (early, got_side, lax.ppermute(late, "pair", SWAP).reshape(1, 16, 128, 128))
+        idx,
+        x,
+        (q_own, q_mate, q_both, q_mates),
+        [kv_piece],
+    )
+    late = stack("late_q", [got_side], [early, pieces[1], pieces[3]])
+    keys, values = join_kv(idx, pieces, tab, [late])
+    late_far = lax.ppermute(late, "pair", SWAP)
+    ws = (early, got_side, late_far)
     att0, att1 = heads(idx, x, ws, norm, tab, bias, keys, values, [])
+    near, hop = second_hop(stay, came, [att0])
+    near_other = lax.ppermute(near, "pair", SWAP)
+    last = lax.ppermute(hop, "tp", flip(8))
+    last_other = lax.ppermute(last, "pair", SWAP)
     here = [att0] + [lax.ppermute(att0, "tp", shift(0, 0, r)) for r in range(1, 4)]
-    stacked = stack("stack_head0", here, [])
+    stacked = stack("stack_head0", here, [near])
     there = lax.ppermute(stacked, "tp", shift(0, 1, 0))
     both = beside(idx, att1, lax.ppermute(att1, "tp", shift(0, 1, 0)), [stacked])
     plane = [both] + [lax.ppermute(both, "tp", shift(0, 0, r)) for r in range(1, 4)]
-    w_own = settle(idx, stay, came, lax.ppermute(hop, "tp", flip(8)), [both])
-    w_other = lax.ppermute(w_own, "pair", SWAP)
 
     parts = []
     for r in (2, 1, 3, 0):
-        partial = project_out(r, idx, here, there, plane, w_own, w_other, parts[-1:])
-        parts.append(partial)
+        w, w_other = (last, last_other) if r % 2 else (near, near_other)
+        parts.append(
+            project_out(r, idx, here, there, plane, w, w_other, [both, *parts[-1:]])
+        )
     parts = [
         lax.ppermute(part, "tp", shift(-r, 0, 0)) if r else part
         for r, part in zip((2, 1, 3, 0), parts)

time: 172 us -> 169 us (0.983)
  local copies, waits for them, and re-layouts: 13.5 us -> 11.3 us
    ppermute x11 -> x12, waiting for transfers between devices: 5.47 us -> 13.4 us  [the longest x3 6.73 us: shards(): lax.ppermute(kv_piece, 'tp', shift(0, 0, r))]
    ppermute x1, waiting for transfers between devices: 6.27 us -> 0.01 us  [shards(): kv_side = lax.ppermute(kv_own, 'side', SWAP)]
    ppermute x3, waiting for transfers between devices: 20.5 us -> 15.5 us  [shards(): lax.ppermute(part, 'tp', shift(-r, 0, 0))]
    unnamed x40 -> x32, local copies, waits for them, and re-layouts: 13.5 us -> 11.2 us
    ppermute x11 -> x12, starting transfers between devices: 7.91 us -> 6.91 us  [the longest x3 2.97 us: shards(): lax.ppermute(kv_piece, 'tp', shift(0, 0, r))]
    pallas_call x22 -> x23, Pallas kernels: 41.8 us -> 41.8 us  [call(): return lambda *args: kernel(*args, *after)]
  transfers between devices with their start and end apart: 30 -> 31, of which waited for: 15 -> 18; matrix products, arithmetic and copies ran while one was open for 0% -> 0% of each run, Pallas kernels for 20% -> 24%
where the time goes in v5:
time: 169 us; the launch traced here: 167 us
  waiting for transfers between devices  79 us (47%)
  Pallas kernels  41.8 us (25%)
  starting transfers between devices  34.9 us (21%)
  local copies, waits for them, and re-layouts  11.3 us (7%)
    pallas_call x23, Pallas kernels, call(): return lambda *args: kernel(*args, *after)  41.8 us
    ppermute x3, waiting for transfers between devices, shards(): lax.ppermute(both, 'tp', shift(0, 0, r))  26.3 us
    ppermute x3, waiting for transfers between devices, shards(): lax.ppermute(part, 'tp', shift(-r, 0, 0))  15.5 us
    ppermute x3, waiting for transfers between devices, shards(): lax.ppermute(att0, 'tp', shift(0, 0, r))  11.3 us
    unnamed x32, local copies, waits for them, and re-layouts  11.2 us
    all_to_all x1, starting transfers between devices, shards(): lax.all_to_all(packed, 'tp', split_axis=0, concat_axis=0, tiled=True, axi...  7.88 us
    all_to_all x1, waiting for transfers between devices, shards(): lax.all_to_all(packed, 'tp', split_axis=0, concat_axis=0, tiled=True, axi...  7.08 us
    ppermute x3, waiting for transfers between devices, shards(): lax.ppermute(kv_piece, 'tp', shift(0, 0, r))  6.73 us
  transfers between devices with their start and end apart: 31, of which 18 were waited for; matrix products, arithmetic and copies ran while one was open for 0% of the time, Pallas kernels for 24%

profile of v5, /device:TPU:0, one launch (start us, length us, event | category | flops | bytes accessed | tf_op | source)
XLA Modules:
  0.0 167.3 jit_solution(8158519906766571223)
XLA Ops:
  0.0 1.7 collective-permute-start
  1.7 1.3 copy-done.2
  3.1 1.0 copy-done.9
  4.1 0.8 copy-done.14
  4.9 2.8 %pack_weights.1.refs_2_ = bf16[16,2,160,128]{3,2,1,0:T(8,128)(2,1)} custom-call(s32[7]{0:T(128)S(1)} %stack.31.refs_0_, bf16[64,10240]{1,0:T(8,128)(2,1)S(1)} %copy-done.2, f32[64,128]{1,0:T(8,128)S(1)} %bitcast.20, bf16[2,256,512]{2,1,0:T(8,128)(2,1)S(1)} %copy-done.9), custom_call_target="tpu_custom_call" | custom-call | tf_op jit(solution)/shard_map/pack_weights/pallas_call | solution.py:112
  7.7 7.9 %all-to-all-start = ((bf16[16,2,160,128]{3,2,1,0:T(8,128)(2,1)}), bf16[16,2,160,128]{3,2,1,0:T(8,128)(2,1)S(1)}, u32[]{:S(2)}, u32[]{:S(2)}) async-start(bf16[16,2,160,128]{3,2,1,0:T(8,128)(2,1)} %pack_weights.1.refs_2_), calls=%async_computation | async-start | bytes 2621440 | tf_op jit(solution)/shard_map/all_to_all | solution.py:592
  15.6 7.2 %token_norms.1 = (f32[1024,128]{1,0:T(8,128)S(1)}, bf16[1024,256]{1,0:T(8,128)(2,1)S(1)}) custom-call(s32[7]{0:T(128)S(1)} %stack.31.refs_0_, bf16[1024,8192]{1,0:T(8,128)(2,1)} %bitcast.14, bf16[16,2,160,128]{3,2,1,0:T(8,128)(2,1)} %pack_weights.1.refs_2_), custom_call_target="tpu_custom_call" | custom-call | tf_op jit(solution)/shard_map/token_norms/pallas_call | solution.py:112
  22.8 2.2 %collective-permute-done.refs_2_ = bf16[2048,256]{1,0:T(8,128)(2,1)S(1)} collective-permute-done((bf16[2048,256]{1,0:T(8,128)(2,1)}, bf16[2048,256]{1,0:T(8,128)(2,1)S(1)}, u32[]{:S(2)}, u32[]{:S(2)}) %collective-permute-start) | collective-permute-done | bytes 1048608 | tf_op jit(solution)/shard_map/ppermute | solution.py:590
  25.0 1.0 copy-done.4
  26.0 1.2 copy-done.5
  27.3 1.7 %pick_rows.1 = (bf16[2,1024,256]{2,1,0:T(8,128)(2,1)S(1)}, bf16[2,1024,256]{2,1,0:T(8,128)(2,1)}) custom-call(s32[7]{0:T(128)S(1)} %stack.31.refs_0_, bf16[2048,256]{1,0:T(8,128)(2,1)S(1)} %copy-done.3, bf16[2048,256]{1,0:T(8,128)(2,1)S(1)} %copy-done.5, f32[1024,128]{1,0:T(8,128)S(1)} %get-tuple-element.20.refs_3_.refs_5_), custom_call_target="tpu_custom_call" | custom-call | tf_op jit(solution)/shard_map/pick_rows/pallas_call | solution.py:112
  28.9 7.1 %all-to-all-done.refs_0_ = bf16[16,2,160,128]{3,2,1,0:T(8,128)(2,1)S(1)} async-done(((bf16[16,2,160,128]{3,2,1,0:T(8,128)(2,1)}), bf16[16,2,160,128]{3,2,1,0:T(8,128)(2,1)S(1)}, u32[]{:S(2)}, u32[]{:S(2)}) %all-to-all-start) | async-done | bytes 1310752 | tf_op jit(solution)/shard_map/all_to_all | solution.py:592
  36.1 2.3 %collective-permute-start.3 = (bf16[16,32,128]{2,1,0:T(8,128)(2,1)S(1)}, bf16[16,32,128]{2,1,0:T(8,128)(2,1)S(1)}, u32[]{:S(2)}, u32[]{:S(2)}) collective-permute-start(bf16[16,32,128]{2,1,0:T(8,128)(2,1)S(1)} %get-tuple-element.23), channel_id=1, source_target_pairs={{0,36},{1,37},{2,38},{3,39},{4,32},{5,33},{6,34},{7,35},{8,44},{9,... | collective-permute-start | bytes 393224 | tf_op jit(solution)/shard_map/ppermute | solution.py:599
  38.3 0.7 collective-permute-start.2
  39.0 1.4 route_rows.1
  40.5 1.9 %collective-permute-done.3.refs_1_ = bf16[16,32,128]{2,1,0:T(8,128)(2,1)S(1)} collective-permute-done((bf16[16,32,128]{2,1,0:T(8,128)(2,1)S(1)}, bf16[16,32,128]{2,1,0:T(8,128)(2,1)S(1)}, u32[]{:S(2)}, u32[]{:S(2)}) %collective-permute-start.3) | collective-permute-done | bytes 131104 | tf_op jit(solution)/shard_map/ppermute | solution.py:599
  42.4 2.3 %collective-permute-start.5 = (bf16[16,128,128]{2,1,0:T(8,128)(2,1)S(1)}, bf16[16,128,128]{2,1,0:T(8,128)(2,1)S(1)}, u32[]{:S(2)}, u32[]{:S(2)}) collective-permute-start(bf16[16,128,128]{2,1,0:T(8,128)(2,1)S(1)} %cut_second.1.refs_5_), channel_id=1, source_target_pairs={{0,36},{1,37},{2,38},{3,39},{4,32},{5,33},{6,34},{7,35},{8,44},{9,... | collective-permute-start | bytes 1572872 | tf_op jit(solution)/shard_map/ppermute | solution.py:605
  44.7 0.6 collective-permute-start.6
  45.2 1.0 collective-permute-done.7.refs_3_
  46.2 5.8 %copy-done = bf16[4,256,8192]{2,1,0:T(8,128)(2,1)S(1)} copy-done((bf16[4,256,8192]{2,1,0:T(8,128)(2,1)S(1)}, bf16[4,256,8192]{2,1,0:T(8,128)(2,1)}, u32[]{:S(2)}) %copy-start) | copy-done | bytes 16777240
  52.0 5.3 %keys_values_early.1.refs_1_.refs_2_ = f32[1024,128]{1,0:T(8,128)S(1)} custom-call(s32[7]{0:T(128)S(1)} %stack.31.refs_0_, bf16[1024,8192]{1,0:T(8,128)(2,1)S(1)} %bitcast.15, bf16[2,16,32,128]{3,2,1,0:T(8,128)(2,1)S(1)} %near_kv.1.refs_1_.refs_2_, bf16[2,16,32,128]{3,2,1,0:T(8,128)(2,1)S(1)} %collective-permute-done.7.refs_3_, ...), custom_call_target="tpu_custom_call" | custom-call | tf_op jit(solution)/shard_map/keys_values_early/pallas_call | solution.py:112
  57.5 0.2 collective-permute-start.8
  57.7 0.4 collective-permute-start.1
  58.1 0.6 collective-permute-start.10
  58.6 0.9 collective-permute-start.18
  59.6 1.4 collective-permute-done.1.refs_11_.refs_3_
  61.0 0.4 collective-permute-done.9
  61.4 3.9 %keys_values.1.refs_6_.refs_1_ = bf16[512,128]{1,0:T(8,128)(2,1)S(1)} custom-call(s32[7]{0:T(128)S(1)} %stack.31.refs_0_, bf16[1024,8192]{1,0:T(8,128)(2,1)S(1)} %bitcast.16, f32[1024,128]{1,0:T(8,128)S(1)} %keys_values_early.1.refs_1_.refs_2_, bf16[2,16,32,128]{3,2,1,0:T(8,128)(2,1)S(1)} %collective-permute-done.6.refs_0_.refs_3_, ...), custom_call_target="tpu_custom_call" | custom-call | tf_op jit(solution)/shard_map/keys_values/pallas_call | solution.py:112
  65.3 0.3 collective-permute-start.12
  65.7 1.8 %collective-permute-start.11 = (bf16[512,128]{1,0:T(8,128)(2,1)S(1)}, bf16[512,128]{1,0:T(8,128)(2,1)S(1)}, u32[]{:S(2)}, u32[]{:S(2)}) collective-permute-start(bf16[512,128]{1,0:T(8,128)(2,1)S(1)} %keys_values.1.refs_6_.refs_1_), channel_id=1, source_target_pairs={{0,1},{1,2},{2,3},{3,0},{4,5},{5,6},{6,7},{7,4},{8,9},{9,10},{10,1... | collective-permute-start | bytes 393224 | tf_op jit(solution)/shard_map/ppermute | solution.py:617
  67.4 4.1 %project_early.1.refs_1_.refs_2_ = f32[1024,256]{1,0:T(8,128)S(1)} custom-call(s32[7]{0:T(128)S(1)} %stack.31.refs_0_, bf16[1024,8192]{1,0:T(8,128)(2,1)S(1)} %bitcast.17, bf16[16,128,128]{2,1,0:T(8,128)(2,1)S(1)} %get-tuple-element.22.refs_3_.refs_2_, bf16[16,128,128]{2,1,0:T(8,128)(2,1)S(1)} %collective-permute-done.1.refs_11_.refs_3_, ...), custom_call_target="tpu_custom_call" | custom-call | tf_op jit(solution)/shard_map/project_early/pallas_call | solution.py:112
  71.6 0.5 collective-permute-done.10.refs_0_.refs_3_
  72.0 0.2 collective-permute-done.11.refs_2_
  72.4 0.9 collective-permute-start.14
  73.3 6.5 %collective-permute-done.14.refs_3_ = bf16[512,128]{1,0:T(8,128)(2,1)S(1)} collective-permute-done((bf16[512,128]{1,0:T(8,128)(2,1)S(1)}, bf16[512,128]{1,0:T(8,128)(2,1)S(1)}, u32[]{:S(2)}, u32[]{:S(2)}) %collective-permute-start.14) | collective-permute-done | bytes 131104 | tf_op jit(solution)/shard_map/ppermute | solution.py:617
  79.8 1.2 join_keys_values.1
  81.1 4.6 %query_heads.1 = (bf16[1024,128]{1,0:T(8,128)(2,1)S(1)}, bf16[1024,128]{1,0:T(8,128)(2,1)S(1)}) custom-call(s32[7]{0:T(128)S(1)} %stack.31.refs_0_, bf16[1024,8192]{1,0:T(8,128)(2,1)S(1)} %bitcast.18, f32[1024,256]{1,0:T(8,128)S(1)} %project_early.1.refs_1_.refs_2_, bf16[16,128,128]{2,1,0:T(8,128)(2,1)S(1)} %collective-permute-done.10.refs_0_.refs_3_, ...), custom_call_target="tpu_custom_call" | custom-call | tf_op jit(solution)/shard_map/query_heads/pallas_call | solution.py:112
  85.7 0.1 second_rows.1
  85.9 1.0 collective-permute-start.26
  86.9 1.0 collective-permute-start.17
  87.8 0.7 collective-permute-start.16
  88.5 0.3 collective-permute-start.15
  88.9 2.1 %collective-permute-start.20 = (bf16[1024,128]{1,0:T(8,128)(2,1)S(1)}, bf16[1024,128]{1,0:T(8,128)(2,1)S(1)}, u32[]{:S(2)}, u32[]{:S(2)}) collective-permute-start(bf16[1024,128]{1,0:T(8,128)(2,1)S(1)} %get-tuple-element.31.refs_1_), channel_id=1, source_target_pairs={{0,4},{1,5},{2,6},{3,7},{4,0},{5,1},{6,2},{7,3},{8,12},{9,13},{10,... | collective-permute-start | bytes 786440 | tf_op jit(solution)/shard_map/ppermute | solution.py:638
  91.0 5.1 %collective-permute-done.17.refs_3_.refs_4_ = bf16[1024,128]{1,0:T(8,128)(2,1)S(1)} collective-permute-done((bf16[1024,128]{1,0:T(8,128)(2,1)S(1)}, bf16[1024,128]{1,0:T(8,128)(2,1)S(1)}, u32[]{:S(2)}, u32[]{:S(2)}) %collective-permute-start.17) | collective-permute-done | bytes 262176 | tf_op jit(solution)/shard_map/ppermute | solution.py:635
  96.1 2.5 %collective-permute-done.16.refs_2_.refs_3_ = bf16[1024,128]{1,0:T(8,128)(2,1)S(1)} collective-permute-done((bf16[1024,128]{1,0:T(8,128)(2,1)S(1)}, bf16[1024,128]{1,0:T(8,128)(2,1)S(1)}, u32[]{:S(2)}, u32[]{:S(2)}) %collective-permute-start.16) | collective-permute-done | bytes 262176 | tf_op jit(solution)/shard_map/ppermute | solution.py:635
  98.6 3.6 %collective-permute-done.15.refs_1_.refs_2_ = bf16[1024,128]{1,0:T(8,128)(2,1)S(1)} collective-permute-done((bf16[1024,128]{1,0:T(8,128)(2,1)S(1)}, bf16[1024,128]{1,0:T(8,128)(2,1)S(1)}, u32[]{:S(2)}, u32[]{:S(2)}) %collective-permute-start.15) | collective-permute-done | bytes 262176 | tf_op jit(solution)/shard_map/ppermute | solution.py:635
  102.3 0.7 beside.1.refs_6_.refs_12_
  103.0 0.7 collective-permute-start.23
  103.7 2.1 %collective-permute-start.19 = (bf16[4,1024,128]{2,1,0:T(8,128)(2,1)S(1)}, bf16[4,1024,128]{2,1,0:T(8,128)(2,1)S(1)}, u32[]{:S(2)}, u32[]{:S(2)}) collective-permute-start(bf16[4,1024,128]{2,1,0:T(8,128)(2,1)S(1)} %stack_head0.1.refs_3_), channel_id=1, source_target_pairs={{0,4},{1,5},{2,6},{3,7},{4,0},{5,1},{6,2},{7,3},{8,12},{9,13},{10,... | collective-permute-start | bytes 3145736 | tf_op jit(solution)/shard_map/ppermute | solution.py:637
  105.8 4.9 %collective-permute-done.26.refs_10_ = bf16[2,1024,256]{2,1,0:T(8,128)(2,1)S(1)} collective-permute-done((bf16[2,1024,256]{2,1,0:T(8,128)(2,1)S(1)}, bf16[2,1024,256]{2,1,0:T(8,128)(2,1)S(1)}, u32[]{:S(2)}, u32[]{:S(2)}) %collective-permute-start.26) | collective-permute-done | bytes 1048608 | tf_op jit(solution)/shard_map/ppermute | solution.py:633
  110.6 0.8 collective-permute-start.22
  111.4 6.4 %collective-permute-done.23.refs_9_ = bf16[1024,256]{1,0:T(8,128)(2,1)S(1)} collective-permute-done((bf16[1024,256]{1,0:T(8,128)(2,1)S(1)}, bf16[1024,256]{1,0:T(8,128)(2,1)S(1)}, u32[]{:S(2)}, u32[]{:S(2)}) %collective-permute-start.23) | collective-permute-done | bytes 524320 | tf_op jit(solution)/shard_map/ppermute | solution.py:639
  117.8 9.1 %collective-permute-done.22.refs_8_ = bf16[1024,256]{1,0:T(8,128)(2,1)S(1)} collective-permute-done((bf16[1024,256]{1,0:T(8,128)(2,1)S(1)}, bf16[1024,256]{1,0:T(8,128)(2,1)S(1)}, u32[]{:S(2)}, u32[]{:S(2)}) %collective-permute-start.22) | collective-permute-done | bytes 524320 | tf_op jit(solution)/shard_map/ppermute | solution.py:639
  126.9 10.8 %collective-permute-done.21.refs_7_ = bf16[1024,256]{1,0:T(8,128)(2,1)S(1)} collective-permute-done((bf16[1024,256]{1,0:T(8,128)(2,1)S(1)}, bf16[1024,256]{1,0:T(8,128)(2,1)S(1)}, u32[]{:S(2)}, u32[]{:S(2)}) %collective-permute-start.21) | collective-permute-done | bytes 524320 | tf_op jit(solution)/shard_map/ppermute | solution.py:639
  137.7 1.8 %project_out_2.1.refs_13_ = bf16[1024,256]{1,0:T(8,128)(2,1)S(1)} custom-call(s32[7]{0:T(128)S(1)} %stack.31.refs_0_, bf16[1024,128]{1,0:T(8,128)(2,1)S(1)} %get-tuple-element.28.refs_2_.refs_0_.refs_1_, bf16[1024,128]{1,0:T(8,128)(2,1)S(1)} %collective-permute-done.15.refs_1_.refs_2_, bf16[1024,128]{1,0:T(8,128)(2,1)S(1)} %collective-permute-done.16.refs_2_.refs_3_, ...), custom_call_target="tpu_custom_call" | custom-call | tf_op jit(solution)/shard_map/project_out_2/pallas_call | solution.py:112
  139.5 2.4 %collective-permute-start.25 = (bf16[1024,256]{1,0:T(8,128)(2,1)S(1)}, bf16[1024,256]{1,0:T(8,128)(2,1)S(1)}, u32[]{:S(2)}, u32[]{:S(2)}) collective-permute-start(bf16[1024,256]{1,0:T(8,128)(2,1)S(1)} %project_out_2.1.refs_13_), channel_id=1, source_target_pairs={{0,16},{1,17},{2,18},{3,19},{4,20},{5,21},{6,22},{7,23},{8,24},{9,... | collective-permute-start | bytes 1572872 | tf_op jit(solution)/shard_map/ppermute | solution.py:648
  142.0 1.8 %project_out_1.1.refs_13_ = bf16[1024,256]{1,0:T(8,128)(2,1)S(1)} custom-call(s32[7]{0:T(128)S(1)} %stack.31.refs_0_, bf16[1024,128]{1,0:T(8,128)(2,1)S(1)} %get-tuple-element.28.refs_2_.refs_0_.refs_1_, bf16[1024,128]{1,0:T(8,128)(2,1)S(1)} %collective-permute-done.15.refs_1_.refs_2_, bf16[1024,128]{1,0:T(8,128)(2,1)S(1)} %collective-permute-done.16.refs_2_.refs_3_, ...), custom_call_target="tpu_custom_call" | custom-call | tf_op jit(solution)/shard_map/project_out_1/pallas_call | solution.py:112
  143.8 1.8 %project_out_3.1.refs_13_ = bf16[1024,256]{1,0:T(8,128)(2,1)S(1)} custom-call(s32[7]{0:T(128)S(1)} %stack.31.refs_0_, bf16[1024,128]{1,0:T(8,128)(2,1)S(1)} %get-tuple-element.28.refs_2_.refs_0_.refs_1_, bf16[1024,128]{1,0:T(8,128)(2,1)S(1)} %collective-permute-done.15.refs_1_.refs_2_, bf16[1024,128]{1,0:T(8,128)(2,1)S(1)} %collective-permute-done.16.refs_2_.refs_3_, ...), custom_call_target="tpu_custom_call" | custom-call | tf_op jit(solution)/shard_map/project_out_3/pallas_call | solution.py:112
  145.6 0.5 collective-permute-start.29
  146.1 2.8 %collective-permute-start.28 = (bf16[1024,256]{1,0:T(8,128)(2,1)S(1)}, bf16[1024,256]{1,0:T(8,128)(2,1)S(1)}, u32[]{:S(2)}, u32[]{:S(2)}) collective-permute-start(bf16[1024,256]{1,0:T(8,128)(2,1)S(1)} %project_out_1.1.refs_13_), channel_id=1, source_target_pairs={{0,24},{1,25},{2,26},{3,27},{4,28},{5,29},{6,30},{7,31},{8,0},{9,1... | collective-permute-start | bytes 1572872 | tf_op jit(solution)/shard_map/ppermute | solution.py:648
  148.9 1.8 %project_out_0.1.refs_4_ = bf16[1024,256]{1,0:T(8,128)(2,1)S(1)} custom-call(s32[7]{0:T(128)S(1)} %stack.31.refs_0_, bf16[1024,128]{1,0:T(8,128)(2,1)S(1)} %get-tuple-element.28.refs_2_.refs_0_.refs_1_, bf16[1024,128]{1,0:T(8,128)(2,1)S(1)} %collective-permute-done.15.refs_1_.refs_2_, bf16[1024,128]{1,0:T(8,128)(2,1)S(1)} %collective-permute-done.16.refs_2_.refs_3_, ...), custom_call_target="tpu_custom_call" | custom-call | tf_op jit(solution)/shard_map/project_out_0/pallas_call | solution.py:112
  150.7 5.2 %collective-permute-done.25.refs_1_ = bf16[1024,256]{1,0:T(8,128)(2,1)S(1)} collective-permute-done((bf16[1024,256]{1,0:T(8,128)(2,1)S(1)}, bf16[1024,256]{1,0:T(8,128)(2,1)S(1)}, u32[]{:S(2)}, u32[]{:S(2)}) %collective-permute-start.25) | collective-permute-done | bytes 524320 | tf_op jit(solution)/shard_map/ppermute | solution.py:648
  155.9 10.3 %collective-permute-done.29.refs_3_ = bf16[1024,256]{1,0:T(8,128)(2,1)S(1)} collective-permute-done((bf16[1024,256]{1,0:T(8,128)(2,1)S(1)}, bf16[1024,256]{1,0:T(8,128)(2,1)S(1)}, u32[]{:S(2)}, u32[]{:S(2)}) %collective-permute-start.29) | collective-permute-done | bytes 524320 | tf_op jit(solution)/shard_map/ppermute | solution.py:648
  166.2 1.1 add_residual.1
  (55 shorter events, 0.6 us)
Async XLA Ops:
  0.0 25.0 %collective-permute-start = (bf16[2048,256]{1,0:T(8,128)(2,1)}, bf16[2048,256]{1,0:T(8,128)(2,1)S(1)}, u32[]{:S(2)}, u32[]{:S(2)}) collective-permute-start(bf16[2048,256]{1,0:T(8,128)(2,1)} %refs_1_.3), channel_id=1, source_target_pairs={{0,32},{32,0},{1,33},{33,1},{2,34},{34,2},{3,35},{35,3},{4,36},{36... | collective-permute-start | bytes 3145736 | tf_op jit(solution)/shard_map/ppermute | solution.py:590
  1.7 1.3 copy-start.2
  3.1 1.0 copy-start.9
  4.1 0.8 copy-start.14
  7.7 28.4 %all-to-all-start = ((bf16[16,2,160,128]{3,2,1,0:T(8,128)(2,1)}), bf16[16,2,160,128]{3,2,1,0:T(8,128)(2,1)S(1)}, u32[]{:S(2)}, u32[]{:S(2)}) async-start(bf16[16,2,160,128]{3,2,1,0:T(8,128)(2,1)} %pack_weights.1.refs_2_), calls=%async_computation | async-start | bytes 2621440 | tf_op jit(solution)/shard_map/all_to_all | solution.py:592
  15.5 10.5 %copy-start.3 = (bf16[2048,256]{1,0:T(8,128)(2,1)S(1)}, bf16[2048,256]{1,0:T(8,128)(2,1)}, u32[]{:S(2)}) copy-start(bf16[2048,256]{1,0:T(8,128)(2,1)} %refs_1_.3) | copy-start | bytes 3145732
  25.0 1.0 copy-start.4
  26.0 1.2 copy-start.5
  28.9 10.1 %collective-permute-start.4 = (bf16[2,1024,256]{2,1,0:T(8,128)(2,1)}, bf16[2,1024,256]{2,1,0:T(8,128)(2,1)}, u32[]{:S(2)}, u32[]{:S(2)}) collective-permute-start(bf16[2,1024,256]{2,1,0:T(8,128)(2,1)} %get-tuple-element.24), channel_id=1, source_target_pairs={{0,64},{64,0},{1,65},{65,1},{2,66},{66,2},{3,67},{67,3},{4,68},{68... | collective-permute-start | bytes 3145736 | tf_op jit(solution)/shard_map/ppermute | solution.py:600
  36.1 6.3 %collective-permute-start.3 = (bf16[16,32,128]{2,1,0:T(8,128)(2,1)S(1)}, bf16[16,32,128]{2,1,0:T(8,128)(2,1)S(1)}, u32[]{:S(2)}, u32[]{:S(2)}) collective-permute-start(bf16[16,32,128]{2,1,0:T(8,128)(2,1)S(1)} %get-tuple-element.23), channel_id=1, source_target_pairs={{0,36},{1,37},{2,38},{3,39},{4,32},{5,33},{6,34},{7,35},{8,44},{9,... | collective-permute-start | bytes 393224 | tf_op jit(solution)/shard_map/ppermute | solution.py:599
  38.3 19.1 %collective-permute-start.2 = (bf16[16,128,128]{2,1,0:T(8,128)(2,1)S(1)}, bf16[16,128,128]{2,1,0:T(8,128)(2,1)S(1)}, u32[]{:S(2)}, u32[]{:S(2)}) collective-permute-start(bf16[16,128,128]{2,1,0:T(8,128)(2,1)S(1)} %get-tuple-element.22.refs_3_.refs_2_), channel_id=1, source_target_pairs={{0,32},{32,0},{1,33},{33,1},{2,34},{34,2},{3,35},{35,3},{4,36},{36... | collective-permute-start | bytes 1572872 | tf_op jit(solution)/shard_map/ppermute | solution.py:598
  42.4 3.9 %copy-start.11 = (bf16[128,256]{1,0:T(8,128)(2,1)S(1)}, bf16[128,256]{1,0:T(8,128)(2,1)}, u32[]{:S(2)}) copy-start(bf16[128,256]{1,0:T(8,128)(2,1)} %constant.78.clone.refs_4_.refs_6_) | copy-start | bytes 196612
  42.4 15.0 %collective-permute-start.5 = (bf16[16,128,128]{2,1,0:T(8,128)(2,1)S(1)}, bf16[16,128,128]{2,1,0:T(8,128)(2,1)S(1)}, u32[]{:S(2)}, u32[]{:S(2)}) collective-permute-start(bf16[16,128,128]{2,1,0:T(8,128)(2,1)S(1)} %cut_second.1.refs_5_), channel_id=1, source_target_pairs={{0,36},{1,37},{2,38},{3,39},{4,32},{5,33},{6,34},{7,35},{8,44},{9,... | collective-permute-start | bytes 1572872 | tf_op jit(solution)/shard_map/ppermute | solution.py:605
  44.7 1.5 collective-permute-start.7
  44.7 12.6 %collective-permute-start.6 = (bf16[2,16,32,128]{3,2,1,0:T(8,128)(2,1)S(1)}, bf16[2,16,32,128]{3,2,1,0:T(8,128)(2,1)S(1)}, u32[]{:S(2)}, u32[]{:S(2)}) collective-permute-start(bf16[2,16,32,128]{3,2,1,0:T(8,128)(2,1)S(1)} %near_kv.1.refs_1_.refs_2_), channel_id=1, source_target_pairs={{0,32},{32,0},{1,33},{33,1},{2,34},{34,2},{3,35},{35,3},{4,36},{36... | collective-permute-start | bytes 786440 | tf_op jit(solution)/shard_map/ppermute | solution.py:602
  46.2 5.8 %copy-start = (bf16[4,256,8192]{2,1,0:T(8,128)(2,1)S(1)}, bf16[4,256,8192]{2,1,0:T(8,128)(2,1)}, u32[]{:S(2)}) copy-start(bf16[4,256,8192]{2,1,0:T(8,128)(2,1)} %param.13) | copy-start | bytes 50331652
  52.0 9.4 %copy-start.1 = (bf16[4,256,8192]{2,1,0:T(8,128)(2,1)S(1)}, bf16[4,256,8192]{2,1,0:T(8,128)(2,1)}, u32[]{:S(2)}) copy-start(bf16[4,256,8192]{2,1,0:T(8,128)(2,1)} %param.13) | copy-start | bytes 50331652
  57.3 2.2 %copy-start.15 = (bf16[10240]{0:T(1024)(128)(2,1)S(1)}, bf16[10240]{0:T(1024)(128)(2,1)}, u32[]{:S(2)}) copy-start(bf16[10240]{0:T(1024)(128)(2,1)} %param.16) | copy-start | bytes 61444
  57.3 4.0 %copy-start.6 = (f32[4,256,128]{2,1,0:T(8,128)S(1)}, f32[4,256,128]{2,1,0:T(8,128)}, u32[]{:S(2)}) copy-start(f32[4,256,128]{2,1,0:T(8,128)} %constant.80.clone.refs_10_) | copy-start | bytes 1572868
  57.4 4.0 %copy-start.7 = (f32[4,256,128]{2,1,0:T(8,128)S(1)}, f32[4,256,128]{2,1,0:T(8,128)}, u32[]{:S(2)}) copy-start(f32[4,256,128]{2,1,0:T(8,128)} %constant.79.clone.refs_9_) | copy-start | bytes 1572868
  57.4 4.0 %copy-start.10 = (bf16[4,256,128]{2,1,0:T(8,128)(2,1)S(1)}, bf16[4,256,128]{2,1,0:T(8,128)(2,1)}, u32[]{:S(2)}) copy-start(bf16[4,256,128]{2,1,0:T(8,128)(2,1)} %constant.77.clone.refs_8_) | copy-start | bytes 786436
  57.5 3.9 %collective-permute-start.8 = (bf16[2,16,128,128]{3,2,1,0:T(8,128)(2,1)S(1)}, bf16[2,16,128,128]{3,2,1,0:T(8,128)(2,1)S(1)}, u32[]{:S(2)}, u32[]{:S(2)}) collective-permute-start(bf16[2,16,128,128]{3,2,1,0:T(8,128)(2,1)S(1)} %late_queries.1.refs_4_), channel_id=1, source_target_pairs={{0,64},{64,0},{1,65},{65,1},{2,66},{66,2},{3,67},{67,3},{4,68},{68... | collective-permute-start | bytes 3145736 | tf_op jit(solution)/shard_map/ppermute | solution.py:611
  57.7 3.3 %collective-permute-start.1 = (bf16[16,128,128]{2,1,0:T(8,128)(2,1)S(1)}, bf16[16,128,128]{2,1,0:T(8,128)(2,1)S(1)}, u32[]{:S(2)}, u32[]{:S(2)}) collective-permute-start(bf16[16,128,128]{2,1,0:T(8,128)(2,1)S(1)} %get-tuple-element.22.refs_3_.refs_2_), channel_id=1, source_target_pairs={{0,64},{64,0},{1,65},{65,1},{2,66},{66,2},{3,67},{67,3},{4,68},{68... | collective-permute-start | bytes 1572872 | tf_op jit(solution)/shard_map/ppermute | solution.py:609
  58.1 14.0 %collective-permute-start.10 = (bf16[16,128,128]{2,1,0:T(8,128)(2,1)S(1)}, bf16[16,128,128]{2,1,0:T(8,128)(2,1)S(1)}, u32[]{:S(2)}, u32[]{:S(2)}) collective-permute-start(bf16[16,128,128]{2,1,0:T(8,128)(2,1)S(1)} %collective-permute-done.5.refs_1_), channel_id=1, source_target_pairs={{0,32},{32,0},{1,33},{33,1},{2,34},{34,2},{3,35},{35,3},{4,36},{36... | collective-permute-start | bytes 1572872 | tf_op jit(solution)/shard_map/ppermute | solution.py:615
  58.6 27.1 %collective-permute-start.18 = (bf16[2,1024,256]{2,1,0:T(8,128)(2,1)S(1)}, bf16[2,1024,256]{2,1,0:T(8,128)(2,1)S(1)}, u32[]{:S(2)}, u32[]{:S(2)}) collective-permute-start(bf16[2,1024,256]{2,1,0:T(8,128)(2,1)S(1)} %get-tuple-element.29), channel_id=1, source_target_pairs={{0,16},{1,17},{2,18},{3,19},{4,20},{5,21},{6,22},{7,23},{8,24},{9,... | collective-permute-start | bytes 3145736 | tf_op jit(solution)/shard_map/ppermute | solution.py:619
  59.6 1.8 %collective-permute-start.9 = (bf16[1,2,16,32,128]{4,3,2,1,0:T(8,128)(2,1)S(1)}, bf16[1,2,16,32,128]{4,3,2,1,0:T(8,128)(2,1)S(1)}, u32[]{:S(2)}, u32[]{:S(2)}) collective-permute-start(bf16[1,2,16,32,128]{4,3,2,1,0:T(8,128)(2,1)S(1)} %late_kv.1.refs_2_), channel_id=1, source_target_pairs={{0,64},{64,0},{1,65},{65,1},{2,66},{66,2},{3,67},{67,3},{4,68},{68... | collective-permute-start | bytes 786440 | tf_op jit(solution)/shard_map/ppermute | solution.py:608
  65.3 6.7 %collective-permute-start.12 = (bf16[512,128]{1,0:T(8,128)(2,1)S(1)}, bf16[512,128]{1,0:T(8,128)(2,1)S(1)}, u32[]{:S(2)}, u32[]{:S(2)}) collective-permute-start(bf16[512,128]{1,0:T(8,128)(2,1)S(1)} %keys_values.1.refs_6_.refs_1_), channel_id=1, source_target_pairs={{0,3},{1,0},{2,1},{3,2},{4,7},{5,4},{6,5},{7,6},{8,11},{9,8},{10,9... | collective-permute-start | bytes 393224 | tf_op jit(solution)/shard_map/ppermute | solution.py:617
  65.7 6.6 %collective-permute-start.11 = (bf16[512,128]{1,0:T(8,128)(2,1)S(1)}, bf16[512,128]{1,0:T(8,128)(2,1)S(1)}, u32[]{:S(2)}, u32[]{:S(2)}) collective-permute-start(bf16[512,128]{1,0:T(8,128)(2,1)S(1)} %keys_values.1.refs_6_.refs_1_), channel_id=1, source_target_pairs={{0,1},{1,2},{2,3},{3,0},{4,5},{5,6},{6,7},{7,4},{8,9},{9,10},{10,1... | collective-permute-start | bytes 393224 | tf_op jit(solution)/shard_map/ppermute | solution.py:617
  71.6 8.2 %copy-start.8 = (bf16[4,2,128,256]{3,2,1,0:T(8,128)(2,1)S(1)}, bf16[4,2,128,256]{3,2,1,0:T(8,128)(2,1)}, u32[]{:S(2)}) copy-start(bf16[4,2,128,256]{3,2,1,0:T(8,128)(2,1)} %constant.76.clone.refs_5_) | copy-start | bytes 1572868
  72.3 8.8 %copy-start.12 = (f32[256,128]{1,0:T(8,128)S(1)}, f32[256,128]{1,0:T(8,128)}, u32[]{:S(2)}) copy-start(f32[256,128]{1,0:T(8,128)} %constant.82.clone.refs_8_) | copy-start | bytes 393220
  72.3 8.8 %copy-start.13 = (f32[256,128]{1,0:T(8,128)S(1)}, f32[256,128]{1,0:T(8,128)}, u32[]{:S(2)}) copy-start(f32[256,128]{1,0:T(8,128)} %constant.81.clone.refs_7_) | copy-start | bytes 393220
  72.3 8.8 %collective-permute-start.13 = (bf16[1,16,128,128]{3,2,1,0:T(8,128)(2,1)S(1)}, bf16[1,16,128,128]{3,2,1,0:T(8,128)(2,1)S(1)}, u32[]{:S(2)}, u32[]{:S(2)}) collective-permute-start(bf16[1,16,128,128]{3,2,1,0:T(8,128)(2,1)S(1)} %late_q.1.refs_6_), channel_id=1, source_target_pairs={{0,64},{64,0},{1,65},{65,1},{2,66},{66,2},{3,67},{67,3},{4,68},{68... | collective-permute-start | bytes 1572872 | tf_op jit(solution)/shard_map/ppermute | solution.py:628
  72.4 7.4 %collective-permute-start.14 = (bf16[512,128]{1,0:T(8,128)(2,1)S(1)}, bf16[512,128]{1,0:T(8,128)(2,1)S(1)}, u32[]{:S(2)}, u32[]{:S(2)}) collective-permute-start(bf16[512,128]{1,0:T(8,128)(2,1)S(1)} %keys_values.1.refs_6_.refs_1_), channel_id=1, source_target_pairs={{0,2},{1,3},{2,0},{3,1},{4,6},{5,7},{6,4},{7,5},{8,10},{9,11},{10,... | collective-permute-start | bytes 393224 | tf_op jit(solution)/shard_map/ppermute | solution.py:617
  85.9 24.8 %collective-permute-start.26 = (bf16[2,1024,256]{2,1,0:T(8,128)(2,1)S(1)}, bf16[2,1024,256]{2,1,0:T(8,128)(2,1)S(1)}, u32[]{:S(2)}, u32[]{:S(2)}) collective-permute-start(bf16[2,1024,256]{2,1,0:T(8,128)(2,1)S(1)} %get-tuple-element.32), channel_id=1, source_target_pairs={{0,8},{1,9},{2,10},{3,11},{4,12},{5,13},{6,14},{7,15},{8,0},{9,1},... | collective-permute-start | bytes 3145736 | tf_op jit(solution)/shard_map/ppermute | solution.py:633
  86.9 9.2 %collective-permute-start.17 = (bf16[1024,128]{1,0:T(8,128)(2,1)S(1)}, bf16[1024,128]{1,0:T(8,128)(2,1)S(1)}, u32[]{:S(2)}, u32[]{:S(2)}) collective-permute-start(bf16[1024,128]{1,0:T(8,128)(2,1)S(1)} %get-tuple-element.28.refs_2_.refs_0_.refs_1_), channel_id=1, source_target_pairs={{0,3},{1,0},{2,1},{3,2},{4,7},{5,4},{6,5},{7,6},{8,11},{9,8},{10,9... | collective-permute-start | bytes 786440 | tf_op jit(solution)/shard_map/ppermute | solution.py:635
  87.8 10.8 %collective-permute-start.16 = (bf16[1024,128]{1,0:T(8,128)(2,1)S(1)}, bf16[1024,128]{1,0:T(8,128)(2,1)S(1)}, u32[]{:S(2)}, u32[]{:S(2)}) collective-permute-start(bf16[1024,128]{1,0:T(8,128)(2,1)S(1)} %get-tuple-element.28.refs_2_.refs_0_.refs_1_), channel_id=1, source_target_pairs={{0,2},{1,3},{2,0},{3,1},{4,6},{5,7},{6,4},{7,5},{8,10},{9,11},{10,... | collective-permute-start | bytes 786440 | tf_op jit(solution)/shard_map/ppermute | solution.py:635
  88.5 13.7 %collective-permute-start.15 = (bf16[1024,128]{1,0:T(8,128)(2,1)S(1)}, bf16[1024,128]{1,0:T(8,128)(2,1)S(1)}, u32[]{:S(2)}, u32[]{:S(2)}) collective-permute-start(bf16[1024,128]{1,0:T(8,128)(2,1)S(1)} %get-tuple-element.28.refs_2_.refs_0_.refs_1_), channel_id=1, source_target_pairs={{0,1},{1,2},{2,3},{3,0},{4,5},{5,6},{6,7},{7,4},{8,9},{9,10},{10,1... | collective-permute-start | bytes 786440 | tf_op jit(solution)/shard_map/ppermute | solution.py:635
  88.9 13.4 %collective-permute-start.20 = (bf16[1024,128]{1,0:T(8,128)(2,1)S(1)}, bf16[1024,128]{1,0:T(8,128)(2,1)S(1)}, u32[]{:S(2)}, u32[]{:S(2)}) collective-permute-start(bf16[1024,128]{1,0:T(8,128)(2,1)S(1)} %get-tuple-element.31.refs_1_), channel_id=1, source_target_pairs={{0,4},{1,5},{2,6},{3,7},{4,0},{5,1},{6,2},{7,3},{8,12},{9,13},{10,... | collective-permute-start | bytes 786440 | tf_op jit(solution)/shard_map/ppermute | solution.py:638
  103.0 14.9 %collective-permute-start.23 = (bf16[1024,256]{1,0:T(8,128)(2,1)S(1)}, bf16[1024,256]{1,0:T(8,128)(2,1)S(1)}, u32[]{:S(2)}, u32[]{:S(2)}) collective-permute-start(bf16[1024,256]{1,0:T(8,128)(2,1)S(1)} %beside.1.refs_6_.refs_12_), channel_id=1, source_target_pairs={{0,3},{1,0},{2,1},{3,2},{4,7},{5,4},{6,5},{7,6},{8,11},{9,8},{10,9... | collective-permute-start | bytes 1572872 | tf_op jit(solution)/shard_map/ppermute | solution.py:639
  103.7 34.1 %collective-permute-start.24 = (bf16[2,1024,256]{2,1,0:T(8,128)(2,1)S(1)}, bf16[2,1024,256]{2,1,0:T(8,128)(2,1)S(1)}, u32[]{:S(2)}, u32[]{:S(2)}) collective-permute-start(bf16[2,1024,256]{2,1,0:T(8,128)(2,1)S(1)} %get-tuple-element.30.refs_4_.refs_10_), channel_id=1, source_target_pairs={{0,64},{64,0},{1,65},{65,1},{2,66},{66,2},{3,67},{67,3},{4,68},{68... | collective-permute-start | bytes 3145736 | tf_op jit(solution)/shard_map/ppermute | solution.py:632
  103.7 34.1 %collective-permute-start.19 = (bf16[4,1024,128]{2,1,0:T(8,128)(2,1)S(1)}, bf16[4,1024,128]{2,1,0:T(8,128)(2,1)S(1)}, u32[]{:S(2)}, u32[]{:S(2)}) collective-permute-start(bf16[4,1024,128]{2,1,0:T(8,128)(2,1)S(1)} %stack_head0.1.refs_3_), channel_id=1, source_target_pairs={{0,4},{1,5},{2,6},{3,7},{4,0},{5,1},{6,2},{7,3},{8,12},{9,13},{10,... | collective-permute-start | bytes 3145736 | tf_op jit(solution)/shard_map/ppermute | solution.py:637
  110.6 31.3 %collective-permute-start.27 = (bf16[2,1024,256]{2,1,0:T(8,128)(2,1)S(1)}, bf16[2,1024,256]{2,1,0:T(8,128)(2,1)S(1)}, u32[]{:S(2)}, u32[]{:S(2)}) collective-permute-start(bf16[2,1024,256]{2,1,0:T(8,128)(2,1)S(1)} %collective-permute-done.26.refs_10_), channel_id=1, source_target_pairs={{0,64},{64,0},{1,65},{65,1},{2,66},{66,2},{3,67},{67,3},{4,68},{68... | collective-permute-start | bytes 3145736 | tf_op jit(solution)/shard_map/ppermute | solution.py:634
  110.6 16.3 %collective-permute-start.22 = (bf16[1024,256]{1,0:T(8,128)(2,1)S(1)}, bf16[1024,256]{1,0:T(8,128)(2,1)S(1)}, u32[]{:S(2)}, u32[]{:S(2)}) collective-permute-start(bf16[1024,256]{1,0:T(8,128)(2,1)S(1)} %beside.1.refs_6_.refs_12_), channel_id=1, source_target_pairs={{0,2},{1,3},{2,0},{3,1},{4,6},{5,7},{6,4},{7,5},{8,10},{9,11},{10,... | collective-permute-start | bytes 1572872 | tf_op jit(solution)/shard_map/ppermute | solution.py:639
  117.8 19.9 %collective-permute-start.21 = (bf16[1024,256]{1,0:T(8,128)(2,1)S(1)}, bf16[1024,256]{1,0:T(8,128)(2,1)S(1)}, u32[]{:S(2)}, u32[]{:S(2)}) collective-permute-start(bf16[1024,256]{1,0:T(8,128)(2,1)S(1)} %beside.1.refs_6_.refs_12_), channel_id=1, source_target_pairs={{0,1},{1,2},{2,3},{3,0},{4,5},{5,6},{6,7},{7,4},{8,9},{9,10},{10,1... | collective-permute-start | bytes 1572872 | tf_op jit(solution)/shard_map/ppermute | solution.py:639
  139.5 16.4 %collective-permute-start.25 = (bf16[1024,256]{1,0:T(8,128)(2,1)S(1)}, bf16[1024,256]{1,0:T(8,128)(2,1)S(1)}, u32[]{:S(2)}, u32[]{:S(2)}) collective-permute-start(bf16[1024,256]{1,0:T(8,128)(2,1)S(1)} %project_out_2.1.refs_13_), channel_id=1, source_target_pairs={{0,16},{1,17},{2,18},{3,19},{4,20},{5,21},{6,22},{7,23},{8,24},{9,... | collective-permute-start | bytes 1572872 | tf_op jit(solution)/shard_map/ppermute | solution.py:648
  145.6 20.6 %collective-permute-start.29 = (bf16[1024,256]{1,0:T(8,128)(2,1)S(1)}, bf16[1024,256]{1,0:T(8,128)(2,1)S(1)}, u32[]{:S(2)}, u32[]{:S(2)}) collective-permute-start(bf16[1024,256]{1,0:T(8,128)(2,1)S(1)} %project_out_3.1.refs_13_), channel_id=1, source_target_pairs={{0,8},{1,9},{2,10},{3,11},{4,12},{5,13},{6,14},{7,15},{8,16},{9,17... | collective-permute-start | bytes 1572872 | tf_op jit(solution)/shard_map/ppermute | solution.py:648
  146.1 20.1 %collective-permute-start.28 = (bf16[1024,256]{1,0:T(8,128)(2,1)S(1)}, bf16[1024,256]{1,0:T(8,128)(2,1)S(1)}, u32[]{:S(2)}, u32[]{:S(2)}) collective-permute-start(bf16[1024,256]{1,0:T(8,128)(2,1)S(1)} %project_out_1.1.refs_13_), channel_id=1, source_target_pairs={{0,24},{1,25},{2,26},{3,27},{4,28},{5,29},{6,30},{7,31},{8,0},{9,1... | collective-permute-start | bytes 1572872 | tf_op jit(solution)/shard_map/ppermute | solution.py:648

commit v6 on v5

--- a/solution.py
+++ b/solution.py
@@ -635,7 +635,7 @@
     here = [att0] + [lax.ppermute(att0, "tp", shift(0, 0, r)) for r in range(1, 4)]
     stacked = stack("stack_head0", here, [near])
     there = lax.ppermute(stacked, "tp", shift(0, 1, 0))
-    both = beside(idx, att1, lax.ppermute(att1, "tp", shift(0, 1, 0)), [stacked])
+    both = beside(idx, att1, lax.ppermute(att1, "tp", shift(0, 1, 0)), [stacked, near_other])
     plane = [both] + [lax.ppermute(both, "tp", shift(0, 0, r)) for r in range(1, 4)]
 
     parts = []

time: 169 us -> 193 us (1.14)
  waiting for transfers between devices: 79 us -> 103 us
    ppermute x1, waiting for transfers between devices: 0.01 us -> 23.2 us  [shards(): lax.ppermute(att1, 'tp', shift(0, 1, 0))]
    ppermute x3, waiting for transfers between devices: 11.3 us -> 14.5 us  [shards(): lax.ppermute(att0, 'tp', shift(0, 0, r))]
    ppermute x3, waiting for transfers between devices: 26.3 us -> 23.7 us  [shards(): lax.ppermute(both, 'tp', shift(0, 0, r))]
  transfers between devices with their start and end apart: 31 -> 31, of which waited for: 18 -> 19; matrix products, arithmetic and copies ran while one was open for 0% -> 0% of each run, Pallas kernels for 24% -> 21%
where the time goes in v6:
time: 193 us; the launch traced here: 192 us
  waiting for transfers between devices  103 us (53%)
  Pallas kernels  41.8 us (22%)
  starting transfers between devices  35.8 us (19%)
  local copies, waits for them, and re-layouts  11.3 us (6%)
    pallas_call x23, Pallas kernels, call(): return lambda *args: kernel(*args, *after)  41.8 us
    ppermute x3, waiting for transfers between devices, shards(): lax.ppermute(both, 'tp', shift(0, 0, r))  23.7 us
    ppermute x1, waiting for transfers between devices, shards(): lax.ppermute(att1, 'tp', shift(0, 1, 0))  23.2 us
    ppermute x3, waiting for transfers between devices, shards(): lax.ppermute(part, 'tp', shift(-r, 0, 0))  15.3 us
    ppermute x3, waiting for transfers between devices, shards(): lax.ppermute(att0, 'tp', shift(0, 0, r))  14.5 us
    unnamed x32, local copies, waits for them, and re-layouts  11.2 us
    all_to_all x1, starting transfers between devices, shards(): lax.all_to_all(packed, 'tp', split_axis=0, concat_axis=0, tiled=True, axi...  7.88 us
    all_to_all x1, waiting for transfers between devices, shards(): lax.all_to_all(packed, 'tp', split_axis=0, concat_axis=0, tiled=True, axi...  7.08 us
  transfers between devices with their start and end apart: 31, of which 19 were waited for; matrix products, arithmetic and copies ran while one was open for 0% of the time, Pallas kernels for 21%

profile of v6, /device:TPU:0, one launch (start us, length us, event | category | flops | bytes accessed | tf_op | source)
XLA Modules:
  0.0 191.9 jit_solution(10596245395787429776)
XLA Ops:
  0.0 1.7 collective-permute-start
  1.7 1.3 copy-done.2
  3.1 1.0 copy-done.9
  4.1 0.8 copy-done.14
  4.9 2.8 %pack_weights.1.refs_2_ = bf16[16,2,160,128]{3,2,1,0:T(8,128)(2,1)} custom-call(s32[7]{0:T(128)S(1)} %stack.31.refs_0_, bf16[64,10240]{1,0:T(8,128)(2,1)S(1)} %copy-done.2, f32[64,128]{1,0:T(8,128)S(1)} %bitcast.20, bf16[2,256,512]{2,1,0:T(8,128)(2,1)S(1)} %copy-done.9), custom_call_target="tpu_custom_call" | custom-call | tf_op jit(solution)/shard_map/pack_weights/pallas_call | solution.py:112
  7.7 7.9 %all-to-all-start = ((bf16[16,2,160,128]{3,2,1,0:T(8,128)(2,1)}), bf16[16,2,160,128]{3,2,1,0:T(8,128)(2,1)S(1)}, u32[]{:S(2)}, u32[]{:S(2)}) async-start(bf16[16,2,160,128]{3,2,1,0:T(8,128)(2,1)} %pack_weights.1.refs_2_), calls=%async_computation | async-start | bytes 2621440 | tf_op jit(solution)/shard_map/all_to_all | solution.py:592
  15.6 7.2 %token_norms.1 = (f32[1024,128]{1,0:T(8,128)S(1)}, bf16[1024,256]{1,0:T(8,128)(2,1)S(1)}) custom-call(s32[7]{0:T(128)S(1)} %stack.31.refs_0_, bf16[1024,8192]{1,0:T(8,128)(2,1)} %bitcast.14, bf16[16,2,160,128]{3,2,1,0:T(8,128)(2,1)} %pack_weights.1.refs_2_), custom_call_target="tpu_custom_call" | custom-call | tf_op jit(solution)/shard_map/token_norms/pallas_call | solution.py:112
  22.8 2.2 %collective-permute-done.refs_2_ = bf16[2048,256]{1,0:T(8,128)(2,1)S(1)} collective-permute-done((bf16[2048,256]{1,0:T(8,128)(2,1)}, bf16[2048,256]{1,0:T(8,128)(2,1)S(1)}, u32[]{:S(2)}, u32[]{:S(2)}) %collective-permute-start) | collective-permute-done | bytes 1048608 | tf_op jit(solution)/shard_map/ppermute | solution.py:590
  25.0 1.0 copy-done.4
  26.0 1.2 copy-done.5
  27.3 1.7 pick_rows.1
  28.9 7.1 %all-to-all-done.refs_0_ = bf16[16,2,160,128]{3,2,1,0:T(8,128)(2,1)S(1)} async-done(((bf16[16,2,160,128]{3,2,1,0:T(8,128)(2,1)}), bf16[16,2,160,128]{3,2,1,0:T(8,128)(2,1)S(1)}, u32[]{:S(2)}, u32[]{:S(2)}) %all-to-all-start) | async-done | bytes 1310752 | tf_op jit(solution)/shard_map/all_to_all | solution.py:592
  36.1 2.3 %collective-permute-start.3 = (bf16[16,32,128]{2,1,0:T(8,128)(2,1)S(1)}, bf16[16,32,128]{2,1,0:T(8,128)(2,1)S(1)}, u32[]{:S(2)}, u32[]{:S(2)}) collective-permute-start(bf16[16,32,128]{2,1,0:T(8,128)(2,1)S(1)} %get-tuple-element.23), channel_id=1, source_target_pairs={{0,36},{1,37},{2,38},{3,39},{4,32},{5,33},{6,34},{7,35},{8,44},{9,... | collective-permute-start | bytes 393224 | tf_op jit(solution)/shard_map/ppermute | solution.py:599
  38.3 0.7 collective-permute-start.2
  39.0 1.4 route_rows.1
  40.5 1.9 collective-permute-done.3.refs_1_
  42.4 2.3 %collective-permute-start.5 = (bf16[16,128,128]{2,1,0:T(8,128)(2,1)S(1)}, bf16[16,128,128]{2,1,0:T(8,128)(2,1)S(1)}, u32[]{:S(2)}, u32[]{:S(2)}) collective-permute-start(bf16[16,128,128]{2,1,0:T(8,128)(2,1)S(1)} %cut_second.1.refs_5_), channel_id=1, source_target_pairs={{0,36},{1,37},{2,38},{3,39},{4,32},{5,33},{6,34},{7,35},{8,44},{9,... | collective-permute-start | bytes 1572872 | tf_op jit(solution)/shard_map/ppermute | solution.py:605
  44.7 0.6 collective-permute-start.6
  45.2 1.0 collective-permute-done.7.refs_3_
  46.2 5.8 %copy-done = bf16[4,256,8192]{2,1,0:T(8,128)(2,1)S(1)} copy-done((bf16[4,256,8192]{2,1,0:T(8,128)(2,1)S(1)}, bf16[4,256,8192]{2,1,0:T(8,128)(2,1)}, u32[]{:S(2)}) %copy-start) | copy-done | bytes 16777240
  52.0 5.3 %keys_values_early.1.refs_1_.refs_2_ = f32[1024,128]{1,0:T(8,128)S(1)} custom-call(s32[7]{0:T(128)S(1)} %stack.31.refs_0_, bf16[1024,8192]{1,0:T(8,128)(2,1)S(1)} %bitcast.15, bf16[2,16,32,128]{3,2,1,0:T(8,128)(2,1)S(1)} %near_kv.1.refs_1_.refs_2_, bf16[2,16,32,128]{3,2,1,0:T(8,128)(2,1)S(1)} %collective-permute-done.7.refs_3_, ...), custom_call_target="tpu_custom_call" | custom-call | tf_op jit(solution)/shard_map/keys_values_early/pallas_call | solution.py:112
  57.5 0.2 collective-permute-start.8
  57.7 0.4 collective-permute-start.1
  58.1 0.6 collective-permute-start.10
  58.6 0.9 collective-permute-start.18
  59.6 1.4 collective-permute-done.1.refs_11_.refs_3_
  61.0 0.4 collective-permute-done.9
  61.4 3.9 %keys_values.1.refs_6_.refs_1_ = bf16[512,128]{1,0:T(8,128)(2,1)S(1)} custom-call(s32[7]{0:T(128)S(1)} %stack.31.refs_0_, bf16[1024,8192]{1,0:T(8,128)(2,1)S(1)} %bitcast.16, f32[1024,128]{1,0:T(8,128)S(1)} %keys_values_early.1.refs_1_.refs_2_, bf16[2,16,32,128]{3,2,1,0:T(8,128)(2,1)S(1)} %collective-permute-done.6.refs_0_.refs_3_, ...), custom_call_target="tpu_custom_call" | custom-call | tf_op jit(solution)/shard_map/keys_values/pallas_call | solution.py:112
  65.3 0.3 collective-permute-start.12
  65.7 1.8 collective-permute-start.11
  67.4 4.1 %project_early.1.refs_1_.refs_2_ = f32[1024,256]{1,0:T(8,128)S(1)} custom-call(s32[7]{0:T(128)S(1)} %stack.31.refs_0_, bf16[1024,8192]{1,0:T(8,128)(2,1)S(1)} %bitcast.17, bf16[16,128,128]{2,1,0:T(8,128)(2,1)S(1)} %get-tuple-element.22.refs_3_.refs_2_, bf16[16,128,128]{2,1,0:T(8,128)(2,1)S(1)} %collective-permute-done.1.refs_11_.refs_3_, ...), custom_call_target="tpu_custom_call" | custom-call | tf_op jit(solution)/shard_map/project_early/pallas_call | solution.py:112
  71.6 0.5 collective-permute-done.10.refs_0_.refs_3_
  72.0 0.2 collective-permute-done.11.refs_2_
  72.4 0.9 collective-permute-start.14
  73.3 6.5 %collective-permute-done.14.refs_3_ = bf16[512,128]{1,0:T(8,128)(2,1)S(1)} collective-permute-done((bf16[512,128]{1,0:T(8,128)(2,1)S(1)}, bf16[512,128]{1,0:T(8,128)(2,1)S(1)}, u32[]{:S(2)}, u32[]{:S(2)}) %collective-permute-start.14) | collective-permute-done | bytes 131104 | tf_op jit(solution)/shard_map/ppermute | solution.py:617
  79.8 1.2 join_keys_values.1
  81.1 4.6 %query_heads.1 = (bf16[1024,128]{1,0:T(8,128)(2,1)S(1)}, bf16[1024,128]{1,0:T(8,128)(2,1)S(1)}) custom-call(s32[7]{0:T(128)S(1)} %stack.31.refs_0_, bf16[1024,8192]{1,0:T(8,128)(2,1)S(1)} %bitcast.18, f32[1024,256]{1,0:T(8,128)S(1)} %project_early.1.refs_1_.refs_2_, bf16[16,128,128]{2,1,0:T(8,128)(2,1)S(1)} %collective-permute-done.10.refs_0_.refs_3_, ...), custom_call_target="tpu_custom_call" | custom-call | tf_op jit(solution)/shard_map/query_heads/pallas_call | solution.py:112
  85.9 1.0 collective-permute-start.26
  86.9 1.0 collective-permute-start.17
  87.8 0.8 collective-permute-start.16
  88.6 0.3 collective-permute-start.15
  88.9 7.1 %collective-permute-done.17.refs_3_.refs_4_ = bf16[1024,128]{1,0:T(8,128)(2,1)S(1)} collective-permute-done((bf16[1024,128]{1,0:T(8,128)(2,1)S(1)}, bf16[1024,128]{1,0:T(8,128)(2,1)S(1)}, u32[]{:S(2)}, u32[]{:S(2)}) %collective-permute-start.17) | collective-permute-done | bytes 262176 | tf_op jit(solution)/shard_map/ppermute | solution.py:635
  96.0 2.5 %collective-permute-done.16.refs_2_.refs_3_ = bf16[1024,128]{1,0:T(8,128)(2,1)S(1)} collective-permute-done((bf16[1024,128]{1,0:T(8,128)(2,1)S(1)}, bf16[1024,128]{1,0:T(8,128)(2,1)S(1)}, u32[]{:S(2)}, u32[]{:S(2)}) %collective-permute-start.16) | collective-permute-done | bytes 262176 | tf_op jit(solution)/shard_map/ppermute | solution.py:635
  98.5 4.9 %collective-permute-done.15.refs_1_.refs_2_ = bf16[1024,128]{1,0:T(8,128)(2,1)S(1)} collective-permute-done((bf16[1024,128]{1,0:T(8,128)(2,1)S(1)}, bf16[1024,128]{1,0:T(8,128)(2,1)S(1)}, u32[]{:S(2)}, u32[]{:S(2)}) %collective-permute-start.15) | collective-permute-done | bytes 262176 | tf_op jit(solution)/shard_map/ppermute | solution.py:635
  103.4 2.2 %collective-permute-start.19 = (bf16[4,1024,128]{2,1,0:T(8,128)(2,1)S(1)}, bf16[4,1024,128]{2,1,0:T(8,128)(2,1)S(1)}, u32[]{:S(2)}, u32[]{:S(2)}) collective-permute-start(bf16[4,1024,128]{2,1,0:T(8,128)(2,1)S(1)} %stack_head0.1.refs_3_), channel_id=1, source_target_pairs={{0,4},{1,5},{2,6},{3,7},{4,0},{5,1},{6,2},{7,3},{8,12},{9,13},{10,... | collective-permute-start | bytes 3145736 | tf_op jit(solution)/shard_map/ppermute | solution.py:637
  105.6 5.0 %collective-permute-done.26.refs_10_ = bf16[2,1024,256]{2,1,0:T(8,128)(2,1)S(1)} collective-permute-done((bf16[2,1024,256]{2,1,0:T(8,128)(2,1)S(1)}, bf16[2,1024,256]{2,1,0:T(8,128)(2,1)S(1)}, u32[]{:S(2)}, u32[]{:S(2)}) %collective-permute-start.26) | collective-permute-done | bytes 1048608 | tf_op jit(solution)/shard_map/ppermute | solution.py:633
  110.6 1.9 %collective-permute-start.20 = (bf16[1024,128]{1,0:T(8,128)(2,1)S(1)}, bf16[1024,128]{1,0:T(8,128)(2,1)S(1)}, u32[]{:S(2)}, u32[]{:S(2)}) collective-permute-start(bf16[1024,128]{1,0:T(8,128)(2,1)S(1)} %get-tuple-element.31.refs_1_), channel_id=1, source_target_pairs={{0,4},{1,5},{2,6},{3,7},{4,0},{5,1},{6,2},{7,3},{8,12},{9,13},{10,... | collective-permute-start | bytes 786440 | tf_op jit(solution)/shard_map/ppermute | solution.py:638
  112.6 23.2 %collective-permute-done.20.refs_2_ = bf16[1024,128]{1,0:T(8,128)(2,1)S(1)} collective-permute-done((bf16[1024,128]{1,0:T(8,128)(2,1)S(1)}, bf16[1024,128]{1,0:T(8,128)(2,1)S(1)}, u32[]{:S(2)}, u32[]{:S(2)}) %collective-permute-start.20) | collective-permute-done | bytes 262176 | tf_op jit(solution)/shard_map/ppermute | solution.py:638
  135.7 0.7 beside.1.refs_6_.refs_12_
  136.4 0.3 collective-permute-start.24
  136.7 0.6 collective-permute-start.23
  137.3 1.3 collective-permute-start.22
  138.7 12.7 %collective-permute-done.24.refs_9_ = bf16[1024,256]{1,0:T(8,128)(2,1)S(1)} collective-permute-done((bf16[1024,256]{1,0:T(8,128)(2,1)S(1)}, bf16[1024,256]{1,0:T(8,128)(2,1)S(1)}, u32[]{:S(2)}, u32[]{:S(2)}) %collective-permute-start.24) | collective-permute-done | bytes 524320 | tf_op jit(solution)/shard_map/ppermute | solution.py:639
  151.3 1.8 collective-permute-done.23.refs_8_
  153.1 9.2 %collective-permute-done.22.refs_7_ = bf16[1024,256]{1,0:T(8,128)(2,1)S(1)} collective-permute-done((bf16[1024,256]{1,0:T(8,128)(2,1)S(1)}, bf16[1024,256]{1,0:T(8,128)(2,1)S(1)}, u32[]{:S(2)}, u32[]{:S(2)}) %collective-permute-start.22) | collective-permute-done | bytes 524320 | tf_op jit(solution)/shard_map/ppermute | solution.py:639
  162.3 1.8 project_out_2.1.refs_13_
  164.1 2.6 %collective-permute-start.25 = (bf16[1024,256]{1,0:T(8,128)(2,1)S(1)}, bf16[1024,256]{1,0:T(8,128)(2,1)S(1)}, u32[]{:S(2)}, u32[]{:S(2)}) collective-permute-start(bf16[1024,256]{1,0:T(8,128)(2,1)S(1)} %project_out_2.1.refs_13_), channel_id=1, source_target_pairs={{0,16},{1,17},{2,18},{3,19},{4,20},{5,21},{6,22},{7,23},{8,24},{9,... | collective-permute-start | bytes 1572872 | tf_op jit(solution)/shard_map/ppermute | solution.py:648
  166.8 1.8 project_out_1.1.refs_13_
  168.6 1.8 project_out_3.1.refs_13_
  170.5 3.2 %collective-permute-start.28 = (bf16[1024,256]{1,0:T(8,128)(2,1)S(1)}, bf16[1024,256]{1,0:T(8,128)(2,1)S(1)}, u32[]{:S(2)}, u32[]{:S(2)}) collective-permute-start(bf16[1024,256]{1,0:T(8,128)(2,1)S(1)} %project_out_1.1.refs_13_), channel_id=1, source_target_pairs={{0,24},{1,25},{2,26},{3,27},{4,28},{5,29},{6,30},{7,31},{8,0},{9,1... | collective-permute-start | bytes 1572872 | tf_op jit(solution)/shard_map/ppermute | solution.py:648
  173.7 1.8 project_out_0.1.refs_4_
  175.5 5.0 %collective-permute-done.25.refs_1_ = bf16[1024,256]{1,0:T(8,128)(2,1)S(1)} collective-permute-done((bf16[1024,256]{1,0:T(8,128)(2,1)S(1)}, bf16[1024,256]{1,0:T(8,128)(2,1)S(1)}, u32[]{:S(2)}, u32[]{:S(2)}) %collective-permute-start.25) | collective-permute-done | bytes 524320 | tf_op jit(solution)/shard_map/ppermute | solution.py:648
  180.5 10.3 %collective-permute-done.29.refs_3_ = bf16[1024,256]{1,0:T(8,128)(2,1)S(1)} collective-permute-done((bf16[1024,256]{1,0:T(8,128)(2,1)S(1)}, bf16[1024,256]{1,0:T(8,128)(2,1)S(1)}, u32[]{:S(2)}, u32[]{:S(2)}) %collective-permute-start.29) | collective-permute-done | bytes 524320 | tf_op jit(solution)/shard_map/ppermute | solution.py:648
  190.8 1.1 add_residual.1
  (55 shorter events, 0.8 us)
Async XLA Ops:
  0.0 25.0 %collective-permute-start = (bf16[2048,256]{1,0:T(8,128)(2,1)}, bf16[2048,256]{1,0:T(8,128)(2,1)S(1)}, u32[]{:S(2)}, u32[]{:S(2)}) collective-permute-start(bf16[2048,256]{1,0:T(8,128)(2,1)} %refs_1_.3), channel_id=1, source_target_pairs={{0,32},{32,0},{1,33},{33,1},{2,34},{34,2},{3,35},{35,3},{4,36},{36... | collective-permute-start | bytes 3145736 | tf_op jit(solution)/shard_map/ppermute | solution.py:590
  1.7 1.3 copy-start.2
  3.1 1.0 copy-start.9
  4.1 0.8 copy-start.14
  7.7 28.4 %all-to-all-start = ((bf16[16,2,160,128]{3,2,1,0:T(8,128)(2,1)}), bf16[16,2,160,128]{3,2,1,0:T(8,128)(2,1)S(1)}, u32[]{:S(2)}, u32[]{:S(2)}) async-start(bf16[16,2,160,128]{3,2,1,0:T(8,128)(2,1)} %pack_weights.1.refs_2_), calls=%async_computation | async-start | bytes 2621440 | tf_op jit(solution)/shard_map/all_to_all | solution.py:592
  15.5 10.5 %copy-start.3 = (bf16[2048,256]{1,0:T(8,128)(2,1)S(1)}, bf16[2048,256]{1,0:T(8,128)(2,1)}, u32[]{:S(2)}) copy-start(bf16[2048,256]{1,0:T(8,128)(2,1)} %refs_1_.3) | copy-start | bytes 3145732
  25.0 1.0 copy-start.4
  26.0 1.2 copy-start.5
  28.9 10.1 %collective-permute-start.4 = (bf16[2,1024,256]{2,1,0:T(8,128)(2,1)}, bf16[2,1024,256]{2,1,0:T(8,128)(2,1)}, u32[]{:S(2)}, u32[]{:S(2)}) collective-permute-start(bf16[2,1024,256]{2,1,0:T(8,128)(2,1)} %get-tuple-element.24), channel_id=1, source_target_pairs={{0,64},{64,0},{1,65},{65,1},{2,66},{66,2},{3,67},{67,3},{4,68},{68... | collective-permute-start | bytes 3145736 | tf_op jit(solution)/shard_map/ppermute | solution.py:600
  36.1 6.3 %collective-permute-start.3 = (bf16[16,32,128]{2,1,0:T(8,128)(2,1)S(1)}, bf16[16,32,128]{2,1,0:T(8,128)(2,1)S(1)}, u32[]{:S(2)}, u32[]{:S(2)}) collective-permute-start(bf16[16,32,128]{2,1,0:T(8,128)(2,1)S(1)} %get-tuple-element.23), channel_id=1, source_target_pairs={{0,36},{1,37},{2,38},{3,39},{4,32},{5,33},{6,34},{7,35},{8,44},{9,... | collective-permute-start | bytes 393224 | tf_op jit(solution)/shard_map/ppermute | solution.py:599
  38.3 19.1 %collective-permute-start.2 = (bf16[16,128,128]{2,1,0:T(8,128)(2,1)S(1)}, bf16[16,128,128]{2,1,0:T(8,128)(2,1)S(1)}, u32[]{:S(2)}, u32[]{:S(2)}) collective-permute-start(bf16[16,128,128]{2,1,0:T(8,128)(2,1)S(1)} %get-tuple-element.22.refs_3_.refs_2_), channel_id=1, source_target_pairs={{0,32},{32,0},{1,33},{33,1},{2,34},{34,2},{3,35},{35,3},{4,36},{36... | collective-permute-start | bytes 1572872 | tf_op jit(solution)/shard_map/ppermute | solution.py:598
  42.4 3.9 %copy-start.11 = (bf16[128,256]{1,0:T(8,128)(2,1)S(1)}, bf16[128,256]{1,0:T(8,128)(2,1)}, u32[]{:S(2)}) copy-start(bf16[128,256]{1,0:T(8,128)(2,1)} %constant.78.clone.refs_4_.refs_6_) | copy-start | bytes 196612
  42.4 15.0 %collective-permute-start.5 = (bf16[16,128,128]{2,1,0:T(8,128)(2,1)S(1)}, bf16[16,128,128]{2,1,0:T(8,128)(2,1)S(1)}, u32[]{:S(2)}, u32[]{:S(2)}) collective-permute-start(bf16[16,128,128]{2,1,0:T(8,128)(2,1)S(1)} %cut_second.1.refs_5_), channel_id=1, source_target_pairs={{0,36},{1,37},{2,38},{3,39},{4,32},{5,33},{6,34},{7,35},{8,44},{9,... | collective-permute-start | bytes 1572872 | tf_op jit(solution)/shard_map/ppermute | solution.py:605
  44.7 1.5 collective-permute-start.7
  44.7 12.6 %collective-permute-start.6 = (bf16[2,16,32,128]{3,2,1,0:T(8,128)(2,1)S(1)}, bf16[2,16,32,128]{3,2,1,0:T(8,128)(2,1)S(1)}, u32[]{:S(2)}, u32[]{:S(2)}) collective-permute-start(bf16[2,16,32,128]{3,2,1,0:T(8,128)(2,1)S(1)} %near_kv.1.refs_1_.refs_2_), channel_id=1, source_target_pairs={{0,32},{32,0},{1,33},{33,1},{2,34},{34,2},{3,35},{35,3},{4,36},{36... | collective-permute-start | bytes 786440 | tf_op jit(solution)/shard_map/ppermute | solution.py:602
  46.2 5.8 %copy-start = (bf16[4,256,8192]{2,1,0:T(8,128)(2,1)S(1)}, bf16[4,256,8192]{2,1,0:T(8,128)(2,1)}, u32[]{:S(2)}) copy-start(bf16[4,256,8192]{2,1,0:T(8,128)(2,1)} %param.13) | copy-start | bytes 50331652
  52.0 9.4 %copy-start.1 = (bf16[4,256,8192]{2,1,0:T(8,128)(2,1)S(1)}, bf16[4,256,8192]{2,1,0:T(8,128)(2,1)}, u32[]{:S(2)}) copy-start(bf16[4,256,8192]{2,1,0:T(8,128)(2,1)} %param.13) | copy-start | bytes 50331652
  57.3 2.2 %copy-start.15 = (bf16[10240]{0:T(1024)(128)(2,1)S(1)}, bf16[10240]{0:T(1024)(128)(2,1)}, u32[]{:S(2)}) copy-start(bf16[10240]{0:T(1024)(128)(2,1)} %param.16) | copy-start | bytes 61444
  57.3 4.0 %copy-start.6 = (f32[4,256,128]{2,1,0:T(8,128)S(1)}, f32[4,256,128]{2,1,0:T(8,128)}, u32[]{:S(2)}) copy-start(f32[4,256,128]{2,1,0:T(8,128)} %constant.80.clone.refs_10_) | copy-start | bytes 1572868
  57.4 4.0 %copy-start.7 = (f32[4,256,128]{2,1,0:T(8,128)S(1)}, f32[4,256,128]{2,1,0:T(8,128)}, u32[]{:S(2)}) copy-start(f32[4,256,128]{2,1,0:T(8,128)} %constant.79.clone.refs_9_) | copy-start | bytes 1572868
  57.4 4.0 %copy-start.10 = (bf16[4,256,128]{2,1,0:T(8,128)(2,1)S(1)}, bf16[4,256,128]{2,1,0:T(8,128)(2,1)}, u32[]{:S(2)}) copy-start(bf16[4,256,128]{2,1,0:T(8,128)(2,1)} %constant.77.clone.refs_8_) | copy-start | bytes 786436
  57.5 3.9 %collective-permute-start.8 = (bf16[2,16,128,128]{3,2,1,0:T(8,128)(2,1)S(1)}, bf16[2,16,128,128]{3,2,1,0:T(8,128)(2,1)S(1)}, u32[]{:S(2)}, u32[]{:S(2)}) collective-permute-start(bf16[2,16,128,128]{3,2,1,0:T(8,128)(2,1)S(1)} %late_queries.1.refs_4_), channel_id=1, source_target_pairs={{0,64},{64,0},{1,65},{65,1},{2,66},{66,2},{3,67},{67,3},{4,68},{68... | collective-permute-start | bytes 3145736 | tf_op jit(solution)/shard_map/ppermute | solution.py:611
  57.7 3.3 %collective-permute-start.1 = (bf16[16,128,128]{2,1,0:T(8,128)(2,1)S(1)}, bf16[16,128,128]{2,1,0:T(8,128)(2,1)S(1)}, u32[]{:S(2)}, u32[]{:S(2)}) collective-permute-start(bf16[16,128,128]{2,1,0:T(8,128)(2,1)S(1)} %get-tuple-element.22.refs_3_.refs_2_), channel_id=1, source_target_pairs={{0,64},{64,0},{1,65},{65,1},{2,66},{66,2},{3,67},{67,3},{4,68},{68... | collective-permute-start | bytes 1572872 | tf_op jit(solution)/shard_map/ppermute | solution.py:609
  58.1 14.0 %collective-permute-start.10 = (bf16[16,128,128]{2,1,0:T(8,128)(2,1)S(1)}, bf16[16,128,128]{2,1,0:T(8,128)(2,1)S(1)}, u32[]{:S(2)}, u32[]{:S(2)}) collective-permute-start(bf16[16,128,128]{2,1,0:T(8,128)(2,1)S(1)} %collective-permute-done.5.refs_1_), channel_id=1, source_target_pairs={{0,32},{32,0},{1,33},{33,1},{2,34},{34,2},{3,35},{35,3},{4,36},{36... | collective-permute-start | bytes 1572872 | tf_op jit(solution)/shard_map/ppermute | solution.py:615
  58.6 27.1 %collective-permute-start.18 = (bf16[2,1024,256]{2,1,0:T(8,128)(2,1)S(1)}, bf16[2,1024,256]{2,1,0:T(8,128)(2,1)S(1)}, u32[]{:S(2)}, u32[]{:S(2)}) collective-permute-start(bf16[2,1024,256]{2,1,0:T(8,128)(2,1)S(1)} %get-tuple-element.29), channel_id=1, source_target_pairs={{0,16},{1,17},{2,18},{3,19},{4,20},{5,21},{6,22},{7,23},{8,24},{9,... | collective-permute-start | bytes 3145736 | tf_op jit(solution)/shard_map/ppermute | solution.py:619
  59.6 1.8 collective-permute-start.9
  65.3 6.7 %collective-permute-start.12 = (bf16[512,128]{1,0:T(8,128)(2,1)S(1)}, bf16[512,128]{1,0:T(8,128)(2,1)S(1)}, u32[]{:S(2)}, u32[]{:S(2)}) collective-permute-start(bf16[512,128]{1,0:T(8,128)(2,1)S(1)} %keys_values.1.refs_6_.refs_1_), channel_id=1, source_target_pairs={{0,3},{1,0},{2,1},{3,2},{4,7},{5,4},{6,5},{7,6},{8,11},{9,8},{10,9... | collective-permute-start | bytes 393224 | tf_op jit(solution)/shard_map/ppermute | solution.py:617
  65.7 6.6 %collective-permute-start.11 = (bf16[512,128]{1,0:T(8,128)(2,1)S(1)}, bf16[512,128]{1,0:T(8,128)(2,1)S(1)}, u32[]{:S(2)}, u32[]{:S(2)}) collective-permute-start(bf16[512,128]{1,0:T(8,128)(2,1)S(1)} %keys_values.1.refs_6_.refs_1_), channel_id=1, source_target_pairs={{0,1},{1,2},{2,3},{3,0},{4,5},{5,6},{6,7},{7,4},{8,9},{9,10},{10,1... | collective-permute-start | bytes 393224 | tf_op jit(solution)/shard_map/ppermute | solution.py:617
  71.6 8.2 %copy-start.8 = (bf16[4,2,128,256]{3,2,1,0:T(8,128)(2,1)S(1)}, bf16[4,2,128,256]{3,2,1,0:T(8,128)(2,1)}, u32[]{:S(2)}) copy-start(bf16[4,2,128,256]{3,2,1,0:T(8,128)(2,1)} %constant.76.clone.refs_5_) | copy-start | bytes 1572868
  72.3 8.8 %copy-start.12 = (f32[256,128]{1,0:T(8,128)S(1)}, f32[256,128]{1,0:T(8,128)}, u32[]{:S(2)}) copy-start(f32[256,128]{1,0:T(8,128)} %constant.82.clone.refs_8_) | copy-start | bytes 393220
  72.3 8.8 %copy-start.13 = (f32[256,128]{1,0:T(8,128)S(1)}, f32[256,128]{1,0:T(8,128)}, u32[]{:S(2)}) copy-start(f32[256,128]{1,0:T(8,128)} %constant.81.clone.refs_7_) | copy-start | bytes 393220
  72.3 8.8 %collective-permute-start.13 = (bf16[1,16,128,128]{3,2,1,0:T(8,128)(2,1)S(1)}, bf16[1,16,128,128]{3,2,1,0:T(8,128)(2,1)S(1)}, u32[]{:S(2)}, u32[]{:S(2)}) collective-permute-start(bf16[1,16,128,128]{3,2,1,0:T(8,128)(2,1)S(1)} %late_q.1.refs_6_), channel_id=1, source_target_pairs={{0,64},{64,0},{1,65},{65,1},{2,66},{66,2},{3,67},{67,3},{4,68},{68... | collective-permute-start | bytes 1572872 | tf_op jit(solution)/shard_map/ppermute | solution.py:628
  72.4 7.4 %collective-permute-start.14 = (bf16[512,128]{1,0:T(8,128)(2,1)S(1)}, bf16[512,128]{1,0:T(8,128)(2,1)S(1)}, u32[]{:S(2)}, u32[]{:S(2)}) collective-permute-start(bf16[512,128]{1,0:T(8,128)(2,1)S(1)} %keys_values.1.refs_6_.refs_1_), channel_id=1, source_target_pairs={{0,2},{1,3},{2,0},{3,1},{4,6},{5,7},{6,4},{7,5},{8,10},{9,11},{10,... | collective-permute-start | bytes 393224 | tf_op jit(solution)/shard_map/ppermute | solution.py:617
  85.9 24.8 %collective-permute-start.26 = (bf16[2,1024,256]{2,1,0:T(8,128)(2,1)S(1)}, bf16[2,1024,256]{2,1,0:T(8,128)(2,1)S(1)}, u32[]{:S(2)}, u32[]{:S(2)}) collective-permute-start(bf16[2,1024,256]{2,1,0:T(8,128)(2,1)S(1)} %get-tuple-element.32), channel_id=1, source_target_pairs={{0,8},{1,9},{2,10},{3,11},{4,12},{5,13},{6,14},{7,15},{8,0},{9,1},... | collective-permute-start | bytes 3145736 | tf_op jit(solution)/shard_map/ppermute | solution.py:633
  86.9 48.9 %collective-permute-start.21 = (bf16[2,1024,256]{2,1,0:T(8,128)(2,1)S(1)}, bf16[2,1024,256]{2,1,0:T(8,128)(2,1)S(1)}, u32[]{:S(2)}, u32[]{:S(2)}) collective-permute-start(bf16[2,1024,256]{2,1,0:T(8,128)(2,1)S(1)} %get-tuple-element.30.refs_4_.refs_10_), channel_id=1, source_target_pairs={{0,64},{64,0},{1,65},{65,1},{2,66},{66,2},{3,67},{67,3},{4,68},{68... | collective-permute-start | bytes 3145736 | tf_op jit(solution)/shard_map/ppermute | solution.py:632
  86.9 9.1 %collective-permute-start.17 = (bf16[1024,128]{1,0:T(8,128)(2,1)S(1)}, bf16[1024,128]{1,0:T(8,128)(2,1)S(1)}, u32[]{:S(2)}, u32[]{:S(2)}) collective-permute-start(bf16[1024,128]{1,0:T(8,128)(2,1)S(1)} %get-tuple-element.28.refs_2_.refs_0_.refs_1_), channel_id=1, source_target_pairs={{0,3},{1,0},{2,1},{3,2},{4,7},{5,4},{6,5},{7,6},{8,11},{9,8},{10,9... | collective-permute-start | bytes 786440 | tf_op jit(solution)/shard_map/ppermute | solution.py:635
  87.8 10.7 %collective-permute-start.16 = (bf16[1024,128]{1,0:T(8,128)(2,1)S(1)}, bf16[1024,128]{1,0:T(8,128)(2,1)S(1)}, u32[]{:S(2)}, u32[]{:S(2)}) collective-permute-start(bf16[1024,128]{1,0:T(8,128)(2,1)S(1)} %get-tuple-element.28.refs_2_.refs_0_.refs_1_), channel_id=1, source_target_pairs={{0,2},{1,3},{2,0},{3,1},{4,6},{5,7},{6,4},{7,5},{8,10},{9,11},{10,... | collective-permute-start | bytes 786440 | tf_op jit(solution)/shard_map/ppermute | solution.py:635
  88.6 14.7 %collective-permute-start.15 = (bf16[1024,128]{1,0:T(8,128)(2,1)S(1)}, bf16[1024,128]{1,0:T(8,128)(2,1)S(1)}, u32[]{:S(2)}, u32[]{:S(2)}) collective-permute-start(bf16[1024,128]{1,0:T(8,128)(2,1)S(1)} %get-tuple-element.28.refs_2_.refs_0_.refs_1_), channel_id=1, source_target_pairs={{0,1},{1,2},{2,3},{3,0},{4,5},{5,6},{6,7},{7,4},{8,9},{9,10},{10,1... | collective-permute-start | bytes 786440 | tf_op jit(solution)/shard_map/ppermute | solution.py:635
  103.4 35.2 %collective-permute-start.19 = (bf16[4,1024,128]{2,1,0:T(8,128)(2,1)S(1)}, bf16[4,1024,128]{2,1,0:T(8,128)(2,1)S(1)}, u32[]{:S(2)}, u32[]{:S(2)}) collective-permute-start(bf16[4,1024,128]{2,1,0:T(8,128)(2,1)S(1)} %stack_head0.1.refs_3_), channel_id=1, source_target_pairs={{0,4},{1,5},{2,6},{3,7},{4,0},{5,1},{6,2},{7,3},{8,12},{9,13},{10,... | collective-permute-start | bytes 3145736 | tf_op jit(solution)/shard_map/ppermute | solution.py:637
  110.6 56.1 %collective-permute-start.27 = (bf16[2,1024,256]{2,1,0:T(8,128)(2,1)S(1)}, bf16[2,1024,256]{2,1,0:T(8,128)(2,1)S(1)}, u32[]{:S(2)}, u32[]{:S(2)}) collective-permute-start(bf16[2,1024,256]{2,1,0:T(8,128)(2,1)S(1)} %collective-permute-done.26.refs_10_), channel_id=1, source_target_pairs={{0,64},{64,0},{1,65},{65,1},{2,66},{66,2},{3,67},{67,3},{4,68},{68... | collective-permute-start | bytes 3145736 | tf_op jit(solution)/shard_map/ppermute | solution.py:634
  110.6 25.1 %collective-permute-start.20 = (bf16[1024,128]{1,0:T(8,128)(2,1)S(1)}, bf16[1024,128]{1,0:T(8,128)(2,1)S(1)}, u32[]{:S(2)}, u32[]{:S(2)}) collective-permute-start(bf16[1024,128]{1,0:T(8,128)(2,1)S(1)} %get-tuple-element.31.refs_1_), channel_id=1, source_target_pairs={{0,4},{1,5},{2,6},{3,7},{4,0},{5,1},{6,2},{7,3},{8,12},{9,13},{10,... | collective-permute-start | bytes 786440 | tf_op jit(solution)/shard_map/ppermute | solution.py:638
  136.4 14.9 %collective-permute-start.24 = (bf16[1024,256]{1,0:T(8,128)(2,1)S(1)}, bf16[1024,256]{1,0:T(8,128)(2,1)S(1)}, u32[]{:S(2)}, u32[]{:S(2)}) collective-permute-start(bf16[1024,256]{1,0:T(8,128)(2,1)S(1)} %beside.1.refs_6_.refs_12_), channel_id=1, source_target_pairs={{0,3},{1,0},{2,1},{3,2},{4,7},{5,4},{6,5},{7,6},{8,11},{9,8},{10,9... | collective-permute-start | bytes 1572872 | tf_op jit(solution)/shard_map/ppermute | solution.py:639
  136.7 16.4 %collective-permute-start.23 = (bf16[1024,256]{1,0:T(8,128)(2,1)S(1)}, bf16[1024,256]{1,0:T(8,128)(2,1)S(1)}, u32[]{:S(2)}, u32[]{:S(2)}) collective-permute-start(bf16[1024,256]{1,0:T(8,128)(2,1)S(1)} %beside.1.refs_6_.refs_12_), channel_id=1, source_target_pairs={{0,2},{1,3},{2,0},{3,1},{4,6},{5,7},{6,4},{7,5},{8,10},{9,11},{10,... | collective-permute-start | bytes 1572872 | tf_op jit(solution)/shard_map/ppermute | solution.py:639
  137.3 25.0 %collective-permute-start.22 = (bf16[1024,256]{1,0:T(8,128)(2,1)S(1)}, bf16[1024,256]{1,0:T(8,128)(2,1)S(1)}, u32[]{:S(2)}, u32[]{:S(2)}) collective-permute-start(bf16[1024,256]{1,0:T(8,128)(2,1)S(1)} %beside.1.refs_6_.refs_12_), channel_id=1, source_target_pairs={{0,1},{1,2},{2,3},{3,0},{4,5},{5,6},{6,7},{7,4},{8,9},{9,10},{10,1... | collective-permute-start | bytes 1572872 | tf_op jit(solution)/shard_map/ppermute | solution.py:639
  164.1 16.4 %collective-permute-start.25 = (bf16[1024,256]{1,0:T(8,128)(2,1)S(1)}, bf16[1024,256]{1,0:T(8,128)(2,1)S(1)}, u32[]{:S(2)}, u32[]{:S(2)}) collective-permute-start(bf16[1024,256]{1,0:T(8,128)(2,1)S(1)} %project_out_2.1.refs_13_), channel_id=1, source_target_pairs={{0,16},{1,17},{2,18},{3,19},{4,20},{5,21},{6,22},{7,23},{8,24},{9,... | collective-permute-start | bytes 1572872 | tf_op jit(solution)/shard_map/ppermute | solution.py:648
  170.4 20.4 %collective-permute-start.29 = (bf16[1024,256]{1,0:T(8,128)(2,1)S(1)}, bf16[1024,256]{1,0:T(8,128)(2,1)S(1)}, u32[]{:S(2)}, u32[]{:S(2)}) collective-permute-start(bf16[1024,256]{1,0:T(8,128)(2,1)S(1)} %project_out_3.1.refs_13_), channel_id=1, source_target_pairs={{0,8},{1,9},{2,10},{3,11},{4,12},{5,13},{6,14},{7,15},{8,16},{9,17... | collective-permute-start | bytes 1572872 | tf_op jit(solution)/shard_map/ppermute | solution.py:648
  170.5 20.3 %collective-permute-start.28 = (bf16[1024,256]{1,0:T(8,128)(2,1)S(1)}, bf16[1024,256]{1,0:T(8,128)(2,1)S(1)}, u32[]{:S(2)}, u32[]{:S(2)}) collective-permute-start(bf16[1024,256]{1,0:T(8,128)(2,1)S(1)} %project_out_1.1.refs_13_), channel_id=1, source_target_pairs={{0,24},{1,25},{2,26},{3,27},{4,28},{5,29},{6,30},{7,31},{8,0},{9,1... | collective-permute-start | bytes 1572872 | tf_op jit(solution)/shard_map/ppermute | solution.py:648
